TPU v7x, 128 devices: a whole 4x4x4 slice. The times are simulated.
128 devices in a mesh: row: 16 (over x, y), col: 8 (over z, core).
Axes of the slice: x: 4, y: 4, z: 4, core: 2. Of those that a mesh axis runs over, the one named last changes fastest.
Arguments:
- layer_input: bfloat16 [2048, 8192], P('col', 'row'), may hold values from -6 to 6
- gate_pre: bfloat16 [2048, 14336], P('row', 'col'), may hold values from -8 to 8
- up_pre: bfloat16 [2048, 14336], P('row', 'col'), may hold values from -6 to 6
- grad_out: bfloat16 [2048, 8192], P('col', 'row'), may hold values from -2 to 2
- w_gate: bfloat16 [8192, 14336], P('row', 'col'), may hold values from -0.0625 to 0.0625
- w_up: bfloat16 [8192, 14336], P('row', 'col'), may hold values from -0.0625 to 0.0625
- w_down: bfloat16 [14336, 8192], P('col', 'row'), may hold values from -0.046875 to 0.046875
Outputs:
- grad_input: bfloat16 [2048, 8192], P('col', 'row')
- grad_gate: float32 [8192, 14336], P('row', 'col')
- grad_up: float32 [8192, 14336], P('row', 'col')
- grad_down: float32 [14336, 8192], P('col', 'row')
All inputs are finite; a program needn't handle non-finite values.
Results may differ from a plain program's by a relative error of at most 0.027.
Values may be sent and summed in bfloat16 or wider, within the bound.
No kernel may reach another device: no remote copies, remote signals or barrier semaphores. Data moves between devices by JAX's collectives and lax.ppermute only.
A program may use at most 128 MiB of HBM per device.

v0:
```python
import jax
import jax.numpy as jnp
from jax import lax
from jax.sharding import PartitionSpec as P


def swiglu_parts(grad_hidden, gate_pre, up_pre):
    gate_val = gate_pre.astype(jnp.float32)
    up_val = up_pre.astype(jnp.float32)
    sigmoid_val = jax.nn.sigmoid(gate_val)
    silu_val = gate_val * sigmoid_val
    hidden = (silu_val * up_val).astype(jnp.bfloat16)
    up_grad = (grad_hidden * silu_val).astype(jnp.bfloat16)
    gate_grad = (
        grad_hidden * up_val * sigmoid_val * (1.0 + gate_val * (1.0 - sigmoid_val))
    ).astype(jnp.bfloat16)
    return (hidden, gate_grad, up_grad)


def on_device(layer_input, gate_pre, up_pre, grad_out, w_gate, w_up, w_down):
    last_dims = (((1,), (1,)), ((), ()))
    first_dims = (((0,), (0,)), ((), ()))
    input_all, out_all = (
        lax.all_gather(layer_input, "col", axis=0, tiled=True),
        lax.all_gather(grad_out, "col", axis=0, tiled=True),
    )
    grad_hidden = lax.psum_scatter(
        lax.dot_general(out_all, w_down, last_dims, preferred_element_type=jnp.float32).astype(
            jnp.bfloat16
        ),
        "row",
        scatter_dimension=0,
        tiled=True,
    ).astype(jnp.float32)
    hidden_own, gate_own, up_own = swiglu_parts(grad_hidden, gate_pre, up_pre)
    hidden, gate_grad, up_grad = (
        lax.all_gather(hidden_own, "row", axis=0, tiled=True),
        lax.all_gather(gate_own, "row", axis=0, tiled=True),
        lax.all_gather(up_own, "row", axis=0, tiled=True),
    )
    grad_down = lax.dot_general(hidden, out_all, first_dims, preferred_element_type=jnp.float32)
    grad_gate = lax.dot_general(
        input_all, gate_grad, first_dims, preferred_element_type=jnp.float32
    )
    grad_up = lax.dot_general(input_all, up_grad, first_dims, preferred_element_type=jnp.float32)
    total = lax.dot_general(gate_grad, w_gate, last_dims, preferred_element_type=jnp.float32)
    grad_input = lax.psum_scatter(
        (
            total + lax.dot_general(up_grad, w_up, last_dims, preferred_element_type=jnp.float32)
        ).astype(jnp.bfloat16),
        "col",
        scatter_dimension=0,
        tiled=True,
    )
    return (grad_input, grad_gate, grad_up, grad_down)


def solution(mesh):
    in_specs = (
        P("col", "row"),
        P("row", "col"),
        P("row", "col"),
        P("col", "row"),
        P("row", "col"),
        P("row", "col"),
        P("col", "row"),
    )
    out_specs = (P("col", "row"), P("row", "col"), P("row", "col"), P("col", "row"))
    return jax.shard_map(
        on_device, mesh=mesh, in_specs=in_specs, out_specs=out_specs, check_vma=False
    )
```

profile of v0, /device:TPU:1, one launch (start us, length us, event | category | flops | bytes accessed | tf_op | source)
XLA Modules:
  0.0 403.0 jit_solution(12319125267816661540)
XLA Ops:
  7.2 0.7 all-gather.6.cloned.1.call-update
  7.9 0.0 reduce-scatter.3.cloned.1.call-start
  8.0 30.8 %all-gather.6.cloned.1.call-done = bf16[2048,512]{1,0:T(8,128)(2,1)} async-done(((bf16[256,512]{1,0:T(8,128)(2,1)}), bf16[2048,512]{1,0:T(8,128)(2,1)}) %all-gather.6.cloned.1.call-update) | async-done | bytes 2097168 | tf_op jit(solution)/shard_map/all_gather | solution.py:25
  38.8 8.3 %convolution_convert_fusion = bf16[2048,1792]{1,0:T(8,128)(2,1)} fusion(bf16[2048,512]{1,0:T(8,128)(2,1)} %all-gather.6.cloned.1.call-done, bf16[1792,512]{1,0:T(8,128)(2,1)S(1)} %copy-done), kind=kOutput, calls=%fused_computation | convolution fusion | flops 3761766400 | bytes 11272192 | tf_op jit(solution)/shard_map/dot_general | solution.py:28
  47.1 0.0 all-gather.8.cloned.1.call-start
  47.1 81.7 %reduce-scatter.3.cloned.1.call-done = bf16[128,1792]{1,0:T(8,128)(2,1)} async-done(((bf16[2048,1792]{1,0:T(8,128)(2,1)}), bf16[128,1792]{1,0:T(8,128)(2,1)}) %reduce-scatter.3.cloned.1.call-update) | async-done | bytes 458768 | tf_op jit(solution)/shard_map/reduce_scatter | solution.py:27
  128.8 2.6 fusion.4
  131.4 0.0 all-gather.10.cloned.1.call-start
  131.5 0.5 all-gather.10.cloned.1.call-update
  132.0 0.5 all-gather.12.cloned.1.call-update
  132.6 0.5 all-gather.14.cloned.1.call-update
  133.2 0.0 reduce-scatter.5.cloned.1.call-start
  133.2 65.2 %all-gather.8.cloned.1.call-done = bf16[2048,1792]{1,0:T(8,128)(2,1)} async-done(((bf16[128,1792]{1,0:T(8,128)(2,1)}), bf16[2048,1792]{1,0:T(8,128)(2,1)}) %all-gather.8.cloned.1.call-update) | async-done | bytes 7340048 | tf_op jit(solution)/shard_map/all_gather | solution.py:38
  198.4 9.6 %fusion.9 = f32[2048,512]{1,0:T(8,128)} fusion(bf16[2048,1792]{1,0:T(8,128)(2,1)} %all-gather.8.cloned.1.call-done, bf16[512,1792]{1,0:T(8,128)(2,1)} %param.11), kind=kOutput, calls=%fused_computation.19 | convolution fusion | flops 3758096384 | bytes 13369344 | tf_op jit(solution)/shard_map/dot_general | solution.py:46
  208.1 59.0 %all-gather.10.cloned.1.call-done = bf16[2048,1792]{1,0:T(8,128)(2,1)} async-done(((bf16[128,1792]{1,0:T(8,128)(2,1)}), bf16[2048,1792]{1,0:T(8,128)(2,1)}) %all-gather.10.cloned.1.call-update) | async-done | bytes 7340048 | tf_op jit(solution)/shard_map/all_gather | solution.py:39
  267.1 9.0 %add_convert_fusion = bf16[2048,512]{1,0:T(8,128)(2,1)} fusion(f32[2048,512]{1,0:T(8,128)} %fusion.9, bf16[2048,1792]{1,0:T(8,128)(2,1)} %all-gather.10.cloned.1.call-done, bf16[512,1792]{1,0:T(8,128)(2,1)S(1)} %copy-done.4), kind=kOutput, calls=%fused_computation.1 | convolution fusion | flops 3760193536 | bytes 15466496 | tf_op jit(solution)/shard_map/dot_general | solution.py:49
  276.0 18.2 %all-gather.12.cloned.1.call-done = bf16[2048,512]{1,0:T(8,128)(2,1)} async-done(((bf16[256,512]{1,0:T(8,128)(2,1)}), bf16[2048,512]{1,0:T(8,128)(2,1)}) %all-gather.12.cloned.1.call-update) | async-done | bytes 2097168 | tf_op jit(solution)/shard_map/all_gather | solution.py:24
  294.3 9.5 %convolution_bitcast_fusion.1 = f32[512,1792]{0,1:T(8,128)} fusion(bf16[2048,1792]{1,0:T(8,128)(2,1)} %all-gather.8.cloned.1.call-done, bf16[2048,512]{1,0:T(8,128)(2,1)} %all-gather.12.cloned.1.call-done), kind=kOutput, calls=%fused_computation.3 | convolution fusion | flops 3758096384 | bytes 13107200 | tf_op jit(solution)/shard_map/dot_general | solution.py:42
  303.8 5.2 %copy.11 = f32[512,1792]{1,0:T(8,128)} copy(f32[512,1792]{0,1:T(8,128)} %convolution_bitcast_fusion.1) | data formatting | bytes 7340032
  308.9 9.5 %convolution_bitcast_fusion = f32[512,1792]{0,1:T(8,128)} fusion(bf16[2048,1792]{1,0:T(8,128)(2,1)} %all-gather.10.cloned.1.call-done, bf16[2048,512]{1,0:T(8,128)(2,1)} %all-gather.12.cloned.1.call-done), kind=kOutput, calls=%fused_computation.2 | convolution fusion | flops 3758096384 | bytes 13107200 | tf_op jit(solution)/shard_map/dot_general | solution.py:45
  318.5 5.1 %copy.12 = f32[512,1792]{1,0:T(8,128)} copy(f32[512,1792]{0,1:T(8,128)} %convolution_bitcast_fusion) | data formatting | bytes 7340032
  323.6 39.0 %all-gather.14.cloned.1.call-done = bf16[2048,1792]{1,0:T(8,128)(2,1)} async-done(((bf16[128,1792]{1,0:T(8,128)(2,1)}), bf16[2048,1792]{1,0:T(8,128)(2,1)}) %all-gather.14.cloned.1.call-update) | async-done | bytes 7340048 | tf_op jit(solution)/shard_map/all_gather | solution.py:37
  362.6 9.7 %fusion.10 = f32[1792,512]{1,0:T(8,128)} fusion(bf16[2048,1792]{1,0:T(8,128)(2,1)} %all-gather.14.cloned.1.call-done, bf16[2048,512]{1,0:T(8,128)(2,1)} %all-gather.6.cloned.1.call-done), kind=kOutput, calls=%fused_computation.20 | convolution fusion | flops 3758096384 | bytes 13107200 | tf_op jit(solution)/shard_map/dot_general | solution.py:41
  372.2 23.9 %reduce-scatter.5.cloned.1.call-done = bf16[256,512]{1,0:T(8,128)(2,1)} async-done(((bf16[2048,512]{1,0:T(8,128)(2,1)}), bf16[256,512]{1,0:T(8,128)(2,1)}) %reduce-scatter.5.cloned.1.call-update) | async-done | bytes 262160 | tf_op jit(solution)/shard_map/reduce_scatter | solution.py:47
  (16 shorter events, 0.2 us)
Async XLA Ops:
  7.2 31.6 %copy-start = (bf16[1792,512]{1,0:T(8,128)(2,1)S(1)}, bf16[1792,512]{1,0:T(8,128)(2,1)}, u32[]{:S(2)}) copy-start(bf16[1792,512]{1,0:T(8,128)(2,1)} %param.13) | copy-start | bytes 5505028
  7.2 31.6 %all-gather.6.cloned.1.call-start = ((), (), s32[]{:S(2)}) async-start(), calls=%async_computation.2 | async-start | bytes 2359296 | tf_op jit(solution)/shard_map/all_gather | solution.py:25
  7.9 120.9 %reduce-scatter.3.cloned.1.call-start = ((), (), s32[]{:S(2)}) async-start(), calls=%async_computation.3 | async-start | bytes 7798784 | tf_op jit(solution)/shard_map/reduce_scatter | solution.py:27
  47.1 81.8 %copy-start.2 = (bf16[128,1792]{1,0:T(8,128)(2,1)S(1)}, bf16[128,1792]{1,0:T(8,128)(2,1)}, u32[]{:S(2)}) copy-start(bf16[128,1792]{1,0:T(8,128)(2,1)} %param.9) | copy-start | bytes 1376260
  47.1 81.8 %copy-start.3 = (bf16[128,1792]{1,0:T(8,128)(2,1)S(1)}, bf16[128,1792]{1,0:T(8,128)(2,1)}, u32[]{:S(2)}) copy-start(bf16[128,1792]{1,0:T(8,128)(2,1)} %param.8) | copy-start | bytes 1376260
  47.1 151.4 %all-gather.8.cloned.1.call-start = ((), (), s32[]{:S(2)}) async-start(), calls=%async_computation.4 | async-start | bytes 7798784 | tf_op jit(solution)/shard_map/all_gather | solution.py:38
  131.4 135.6 %all-gather.10.cloned.1.call-start = ((), (), s32[]{:S(2)}) async-start(), calls=%async_computation.5 | async-start | bytes 7798784 | tf_op jit(solution)/shard_map/all_gather | solution.py:39
  132.0 162.3 %all-gather.12.cloned.1.call-start = ((), (), s32[]{:S(2)}) async-start(), calls=%async_computation.7 | async-start | bytes 2359296 | tf_op jit(solution)/shard_map/all_gather | solution.py:24
  132.6 230.0 %all-gather.14.cloned.1.call-start = ((), (), s32[]{:S(2)}) async-start(), calls=%async_computation.8 | async-start | bytes 7798784 | tf_op jit(solution)/shard_map/all_gather | solution.py:37
  133.2 133.9 %copy-start.4 = (bf16[512,1792]{1,0:T(8,128)(2,1)S(1)}, bf16[512,1792]{1,0:T(8,128)(2,1)}, u32[]{:S(2)}) copy-start(bf16[512,1792]{1,0:T(8,128)(2,1)} %param.12) | copy-start | bytes 5505028
  133.2 262.9 %reduce-scatter.5.cloned.1.call-start = ((), (), s32[]{:S(2)}) async-start(), calls=%async_computation.6 | async-start | bytes 2359296 | tf_op jit(solution)/shard_map/reduce_scatter | solution.py:47
  362.6 33.6 %copy-start.1 = (bf16[1792,512]{1,0:T(8,128)(2,1)S(1)}, bf16[1792,512]{1,0:T(8,128)(2,1)}, u32[]{:S(2)}) copy-start(bf16[1792,512]{1,0:T(8,128)(2,1)} %param.13) | copy-start | bytes 5505028
Sparse Core Ops, SparseCore 0:
  9.7 28.9 all-gather.5
  47.2 81.5 reduce-scatter.2
  131.8 66.5 all-gather.7
  201.3 65.7 all-gather.9
  268.7 25.4 all-gather.11
  296.5 65.9 all-gather.13
  365.7 30.4 reduce-scatter.4
where the time goes:
time: 406 us; the launch traced here: 403 us
  waiting for transfers between devices  320 us (79%)
  matrix products  55.6 us (14%)
  between operations  14.1 us (3%)
  local copies, waits for them, and re-layouts  10.3 us (3%)
    reduce_scatter x1, waiting for transfers between devices, on_device(): lax.psum_scatter(lax.dot_general(out_all, w_down, last_dims, preferred_el...  81.7 us
    all_gather x1, waiting for transfers between devices, on_device(): lax.all_gather(gate_own, 'row', axis=0, tiled=True)  65.2 us
    all_gather x1, waiting for transfers between devices, on_device(): lax.all_gather(up_own, 'row', axis=0, tiled=True)  59 us
    all_gather x1, waiting for transfers between devices, on_device(): lax.all_gather(hidden_own, 'row', axis=0, tiled=True)  39 us
    all_gather x1, waiting for transfers between devices, on_device(): lax.all_gather(grad_out, 'col', axis=0, tiled=True)  30.8 us
    reduce_scatter x1, waiting for transfers between devices, on_device(): lax.psum_scatter((total + lax.dot_general(up_grad, w_up, last_dims, prefe...  23.9 us
    all_gather x1, waiting for transfers between devices, on_device(): lax.all_gather(layer_input, 'col', axis=0, tiled=True)  18.2 us
    unnamed x12, local copies, waits for them, and re-layouts  10.3 us
  transfers between devices with their start and end apart: 7, of which 7 were waited for; matrix products, arithmetic and copies ran while one was open for 14% of the time, Pallas kernels for 0%

commit v1 on v0

v1 whole, which is shorter than its diff:
```python
import jax
import jax.numpy as jnp
from jax import lax
from jax.experimental import pallas as pl
from jax.experimental.pallas import tpu as pltpu
from jax.sharding import Mesh, PartitionSpec as P

F32 = jnp.float32
BF16 = jnp.bfloat16
RING = 4
LAST = (((1,), (1,)), ((), ()))
FIRST = (((0,), (0,)), ((), ()))
MIB = 2**20


def mix(value, phase, step):
    pairs = []
    for x in range(RING):
        for y in range(RING):
            for core in range(2):
                if (core == 0) == (phase == 1):
                    to = ((x + step) % RING, y)
                else:
                    to = (x, (y + step) % RING)
                pairs.append(((x * RING + y) * 2 + core, (to[0] * RING + to[1]) * 2 + core))
    return lax.ppermute(value, ("x", "y", "c"), pairs)


def along_z(value, step):
    return lax.ppermute(value, "z", [(z, (z + step) % RING) for z in range(RING)])


def swap(value):
    return lax.ppermute(value, "c", [(0, 1), (1, 0)])


def pick(value, at, axis=0):
    return lax.dynamic_index_in_dim(value, at, axis, keepdims=False)


def tie(value, *after):
    return lax.optimization_barrier((value, *after))[0]


def params(mebibytes):
    return pltpu.CompilerParams(vmem_limit_bytes=mebibytes * MIB)


def cost(flops, moved):
    return pl.CostEstimate(flops=flops, bytes_accessed=moved, transcendentals=0)


def travel_order(place, value):
    tokens, model = value.shape
    half = tokens // 32
    value = value.reshape(RING, RING, 2, half, model)

    def kernel(place_ref, value_ref, *results):
        x, y, core = place_ref[0], place_ref[1], place_ref[3]
        for result, owner in zip(results, (core, 1 - core)):
            for second in range(RING):
                for first in range(RING):
                    at_x = lax.rem(x + jnp.where(owner == 0, first, second), RING)
                    at_y = lax.rem(y + jnp.where(owner == 0, second, first), RING)
                    rows = slice(first * half, (first + 1) * half)
                    result[second, rows] = value_ref[at_x, at_y, owner]

    return pl.pallas_call(
        kernel,
        grid=(1,),
        in_specs=[
            pl.BlockSpec(memory_space=pltpu.SMEM),
            pl.BlockSpec(value.shape, lambda j: (0,) * 5),
        ],
        out_specs=[pl.BlockSpec((RING, RING * half, model), lambda j: (0,) * 3)] * 2,
        out_shape=[jax.ShapeDtypeStruct((RING, RING * half, model), BF16)] * 2,
        compiler_params=params(12),
        cost_estimate=cost(0, 2 * tokens * model * 2),
        name="travel_order",
    )(place, value)


def down_products(tokens, parts):
    _, rows, model = tokens.shape
    width = parts[0][1].shape[0]
    tile = width // 2
    operands, in_specs = [], []
    for k, weight, extras in parts:
        operands += [tokens, weight, *extras]
        in_specs.append(pl.BlockSpec((1, rows, model), lambda j, k=k: (k, 0, 0)))
        in_specs.append(pl.BlockSpec((tile, model), lambda j: (j, 0)))
        in_specs += [pl.BlockSpec((rows, tile), lambda j: (0, j)) for _ in extras]

    def kernel(*refs):
        at = 0
        for out, (_, _, extras) in zip(refs[len(operands) :], parts):
            total = lax.dot_general(
                refs[at][0], refs[at + 1][...], LAST, preferred_element_type=F32
            )
            for i in range(len(extras)):
                total = total + refs[at + 2 + i][...].astype(F32)
            at += 2 + len(extras)
            out[...] = total.astype(BF16)

    return pl.pallas_call(
        kernel,
        grid=(2,),
        in_specs=in_specs,
        out_specs=[pl.BlockSpec((rows, tile), lambda j: (0, j))] * len(parts),
        out_shape=[jax.ShapeDtypeStruct((rows, width), BF16)] * len(parts),
        compiler_params=params(12),
        cost_estimate=cost(
            2 * rows * model * width * len(parts), (model + rows) * width * 2 * len(parts)
        ),
        name="down_products",
    )(*operands)


def scatter_sum(tokens, weight, weight_other, before, beside):
    own2, other2 = down_products(tokens, [(2, weight, ()), (2, weight_other, ())])
    other1, own3 = down_products(tokens, [(1, weight_other, ()), (3, weight, ())])
    own2, other2, other1, own3, *_ = lax.optimization_barrier((own2, other2, other1, own3, *before))
    own_fwd, other_back = mix(own2, 2, 1), mix(other2, 2, -1)
    other_fwd, own_back = mix(other1, 2, 1), mix(own3, 2, -1)
    own1, other3 = down_products(
        tokens, [(1, weight, (own_fwd,)), (3, weight_other, (other_back,))]
    )
    own_fwd, other_back = mix(own1, 2, 1), mix(other3, 2, -1)
    sums = jnp.stack(
        down_products(
            tokens, [(0, weight, (own_fwd, own_back)), (0, weight_other, (other_fwd, other_back))]
        )
    )
    sums = sums.reshape(2, RING, -1, sums.shape[-1])
    done = beside(sums)
    total = tie(sums[:, 0], *done).astype(F32)
    for distance, step in ((1, 1), (3, -1), (2, 2)):
        total = total + mix(sums[:, distance], 1, step).astype(F32)
    return total, done


def first_gather(block):
    _, n, half, width = block.shape
    pieces = [block, mix(block, 1, -1), mix(block, 1, 2), mix(block, 1, 1)]
    return tuple(
        jnp.stack([piece[i] for piece in pieces], 1).reshape(n, RING * half, width)
        for i in range(2)
    )


def weight_grads(left_mine, left_theirs, mine, theirs, flip=False):
    n, rows, width = mine[0].shape
    model = left_mine.shape[2]
    pieces = [*mine, *theirs]
    tile = 256

    def kernel(mine_ref, theirs_ref, *refs):
        left = refs[-1]

        @pl.when(pl.program_id(0) == 0)
        def _():
            for k in range(RING):
                left[:, k * rows : (k + 1) * rows] = mine_ref[k].T
                left[:, (RING + k) * rows : (RING + k + 1) * rows] = theirs_ref[k].T

        for i in range(n):
            right = jnp.concatenate([ref[i] for ref in refs[: len(pieces)]], 0)
            result = jnp.dot(left[...], right, preferred_element_type=F32)
            refs[len(pieces) + i][...] = result.T if flip else result

    if flip:
        shape, out_spec = (width, model), pl.BlockSpec((tile, model), lambda j: (j, 0))
    else:
        shape, out_spec = (model, width), pl.BlockSpec((model, tile), lambda j: (0, j))

    return pl.pallas_call(
        kernel,
        grid=(width // tile,),
        in_specs=[pl.BlockSpec(left_mine.shape, lambda j: (0, 0, 0))] * 2
        + [pl.BlockSpec((n, rows, tile), lambda j: (0, 0, j)) for _ in pieces],
        out_specs=[out_spec] * n,
        out_shape=[jax.ShapeDtypeStruct(shape, F32)] * n,
        scratch_shapes=[pltpu.VMEM((model, rows * len(pieces)), BF16)],
        compiler_params=params(18 if n > 1 else 14),
        cost_estimate=cost(
            2 * n * model * width * rows * len(pieces),
            n * model * width * 4 + n * rows * width * 2 * len(pieces),
        ),
        name="weight_grads",
    )(left_mine, left_theirs, *pieces)


def input_products(own, other, weights, ready=(), place=None):
    count = len(own)
    _, rows, width = own[0].shape
    model = weights[0].shape[0]
    last = place is not None
    tile = width // 2 if last else 256
    steps = width // tile
    half = rows // RING

    def kernel(*refs):
        place_ref, refs = (refs[0], refs[1:]) if last else (None, refs)
        own_refs, other_refs = refs[:count], refs[count : 2 * count]
        weight_refs = refs[2 * count : 2 * count + 4]
        ready_refs = refs[2 * count + 4 : 2 * count + 4 + len(ready)]
        total, outs = refs[-1], refs[2 * count + 4 + len(ready) : -1]
        if last:
            outs, held = outs[:-1], outs[-1]
        step = pl.program_id(0)
        for p in range(count):
            value = None
            for piece, pair in ((own_refs[p], weight_refs[:2]), (other_refs[p], weight_refs[2:])):
                for i in range(2):
                    term = lax.dot_general(
                        piece[i], pair[i][...], LAST, preferred_element_type=F32
                    )
                    value = term if value is None else value + term

            @pl.when(step == 0)
            def _():
                total[p] = value

            @pl.when((step > 0) & (step < steps - 1))
            def _():
                total[p] += value

            @pl.when(step == steps - 1)
            def _():
                value_all = (total[p] + value).astype(BF16)
                if not last:
                    outs[p][...] = value_all
                    return
                x, y, z, core = (place_ref[i] for i in range(4))
                for k, ref in zip((0, 1, 3), ready_refs):
                    held[k] = ref[...].reshape(RING, half, model)
                held[2] = value_all.reshape(RING, half, model)
                for distance in range(RING):
                    at_x = lax.rem(z + distance - x + RING, RING)
                    for j in range(2):
                        for low in range(2):
                            at_y = lax.rem(2 * lax.rem(core + j, 2) + low - y + RING, RING)
                            second = jnp.where(core == 0, at_y, at_x)
                            first = jnp.where(core == 0, at_x, at_y)
                            outs[distance][j, low] = held[second, first]

    scratch = [pltpu.VMEM((count, rows, model), F32)]
    whole = pl.BlockSpec((rows, model), lambda j: (0, 0))
    if last:
        scratch = [pltpu.VMEM((RING, RING, half, model), BF16)] + scratch
        out_specs = [pl.BlockSpec((2, 2, half, model), lambda j: (0, 0, 0, 0))] * RING
        out_shape = [jax.ShapeDtypeStruct((2, 2, half, model), BF16)] * RING
    else:
        out_specs = [whole] * count
        out_shape = [jax.ShapeDtypeStruct((rows, model), BF16)] * count
    return pl.pallas_call(
        kernel,
        grid=(steps,),
        in_specs=([pl.BlockSpec(memory_space=pltpu.SMEM)] if last else [])
        + [pl.BlockSpec((2, rows, tile), lambda j: (0, 0, j))] * (2 * count)
        + [pl.BlockSpec((model, tile), lambda j: (0, j))] * 4
        + [whole] * len(ready),
        out_specs=out_specs,
        out_shape=out_shape,
        scratch_shapes=scratch,
        compiler_params=params(16),
        cost_estimate=cost(
            8 * count * rows * model * width, 8 * model * width + 8 * count * rows * width
        ),
        name="input_products",
    )(*([place] if last else []), *own, *other, *weights, *ready)


def on_device(layer_input, gate_pre, up_pre, grad_out, w_gate, w_up, w_down):
    x, y, z, core = (lax.axis_index(name) for name in ("x", "y", "z", "c"))
    place = jnp.stack([x, y, z, core]).astype(jnp.int32)
    rows, width = gate_pre.shape
    half, model = rows // 2, w_down.shape[1]

    both = jnp.concatenate([grad_out, layer_input], 1)
    both = lax.all_gather(both, ("z", "c"), axis=0, tiled=True)

    def half_of_tokens(value, shape):
        halves = value.reshape(shape)
        return jnp.stack([pick(halves, core, 1), swap(pick(halves, 1 - core, 1))])

    gate_val, up_val = gate_pre.astype(F32), up_pre.astype(F32)
    hidden = (gate_val * jax.nn.sigmoid(gate_val) * up_val).astype(BF16)
    hid_own, hid_other = first_gather(half_of_tokens(hidden, (1, 2, half, width)))
    hid_own_after, hid_other_before = mix(hid_own, 2, -1), mix(hid_other, 2, 1)
    hid_own_before, hid_other_after = mix(hid_own, 2, 1), mix(hid_other, 2, -1)

    tokens, tokens_theirs = travel_order(place, both[:, :model])
    w_down_other, w_gate_other, w_up_other = swap(w_down), swap(w_gate), swap(w_up)

    def hidden_across(sums):
        return (
            mix(tie(hid_other_before, sums), 2, 1),
            mix(tie(hid_own_after, sums), 2, -1),
        )

    grad_hidden, (hid_other_across, hid_own_across) = scatter_sum(
        tokens,
        w_down,
        w_down_other,
        (hid_own_after, hid_other_before, hid_own_before, hid_other_after)
        + (w_gate_other, w_up_other),
        hidden_across,
    )

    gate_val = half_of_tokens(gate_pre, (1, 2, half, width))[:, 0].astype(F32)
    up_val = half_of_tokens(up_pre, (1, 2, half, width))[:, 0].astype(F32)
    sigmoid_val = jax.nn.sigmoid(gate_val)
    gate_grad = grad_hidden * up_val * sigmoid_val * (1.0 + gate_val * (1.0 - sigmoid_val))
    up_grad = grad_hidden * (gate_val * sigmoid_val)
    own, other = first_gather(jnp.stack([gate_grad, up_grad], 1).astype(BF16))

    own_after, other_before = mix(own, 2, -1), mix(other, 2, 1)
    own_before, other_after = mix(own, 2, 1), mix(other, 2, -1)

    (grad_down,) = weight_grads(
        tokens,
        tokens_theirs,
        [hid_own, hid_own_after, hid_own_across, hid_own_before],
        [swap(p) for p in (hid_other, hid_other_after, hid_other_across, hid_other_before)],
        flip=True,
    )
    input_mine, input_theirs = travel_order(place, tie(both, own)[:, model:])
    own_after, other_before, own_before, other_after, grad_down, *_ = lax.optimization_barrier(
        (own_after, other_before, own_before, other_after, grad_down, input_mine)
    )
    other_across, own_across = mix(other_before, 2, 1), mix(own_after, 2, -1)

    weights = (w_gate, w_up, w_gate_other, w_up_other)
    ready = input_products(
        [own, own_after, own_before],
        [other, other_after, other_before],
        weights,
    )
    theirs = [swap(p) for p in (other, other_after, other_before)]
    own_across, other_across, *ready = lax.optimization_barrier(
        (own_across, other_across, *ready, *theirs)
    )[:5]
    parts = input_products([own_across], [other_across], weights, ready, place)
    grad_gate, grad_up = weight_grads(
        input_mine,
        input_theirs,
        [own, own_after, own_across, own_before],
        [theirs[0], theirs[1], swap(other_across), theirs[2]],
    )
    received = [along_z(parts[k], step) for k, step in ((1, 1), (3, -1), (2, 2))]
    total = tie(parts[0], grad_gate, grad_up).astype(F32)
    for part in received:
        total = total + part.astype(F32)
    total = total.astype(BF16)
    keep, got = total[0], swap(total[1])
    grad_input = jnp.where(
        core == 0, jnp.stack([keep, got], 1), jnp.stack([got, keep], 1)
    ).reshape(4 * half, model)

    return grad_input, grad_gate, grad_up, grad_down


def solution(mesh):
    chips = Mesh(mesh.devices.reshape(RING, RING, RING, 2), ("x", "y", "z", "c"))
    row, col = ("x", "y"), ("z", "c")
    in_specs = (
        P(col, row),
        P(row, col),
        P(row, col),
        P(col, row),
        P(row, col),
        P(row, col),
        P(col, row),
    )
    out_specs = (P(col, row), P(row, col), P(row, col), P(col, row))
    return jax.shard_map(
        on_device, mesh=chips, in_specs=in_specs, out_specs=out_specs, check_vma=False
    )
```

time: 406 us -> 258 us (0.64)
  waiting for transfers between devices: 320 us -> 122 us
  starting transfers between devices: 0.27 us -> 62.7 us
  matrix products: 55.6 us -> 0 us
  Pallas kernels: 0 us -> 47.1 us
  local copies, waits for them, and re-layouts: 10.3 us -> 6.15 us
    all_gather x5 -> x1, waiting for transfers between devices: 212 us -> 0.01 us  [on_device(): both = lax.all_gather(both, ('z', 'c'), axis=0, tiled=True)]
    ppermute x0 -> x45, waiting for transfers between devices: none -> 122 us  [the longest x27 118 us: mix(): return lax.ppermute(value, ('x', 'y', 'c'), pairs)]
    reduce_scatter x2 -> x0, waiting for transfers between devices: 106 us -> none  [the longest x1 81.7 us: on_device(): lax.psum_scatter(lax.dot_general(out_all, w_down, last_dims, preferred_el...]
    ppermute x0 -> x45, starting transfers between devices: none -> 62.7 us  [the longest x27 33 us: mix(): return lax.ppermute(value, ('x', 'y', 'c'), pairs)]
    dot_general x6 -> x0, matrix products: 55.6 us -> none  [the longest x1 9.65 us: on_device(): lax.dot_general(hidden, out_all, first_dims, preferred_element_type=jnp.f...]
    pallas_call x0 -> x10, Pallas kernels: none -> 47.1 us  [the longest x2 20.5 us: weight_grads(): pl.pallas_call(kernel, grid=(width // tile,), in_specs=[pl.BlockSpec(left...]
    unnamed x12 -> x18, local copies, waits for them, and re-layouts: 10.3 us -> 2.93 us
  transfers between devices with their start and end apart: 7 -> 46, of which waited for: 7 -> 25; matrix products, arithmetic and copies ran while one was open for 14% -> 2% of each run, Pallas kernels for 0% -> 17%
where the time goes in v1:
time: 258 us
  waiting for transfers between devices  122 us (47%)
  starting transfers between devices  62.7 us (24%)
  Pallas kernels  47.1 us (18%)
  between operations  14.4 us (6%)
  local copies, waits for them, and re-layouts  6.15 us (2%)
  other arithmetic  5.12 us (2%)
    ppermute x27, waiting for transfers between devices, mix(): return lax.ppermute(value, ('x', 'y', 'c'), pairs)  118 us
    ppermute x27, starting transfers between devices, mix(): return lax.ppermute(value, ('x', 'y', 'c'), pairs)  33 us
    ppermute x15, starting transfers between devices, swap(): return lax.ppermute(value, 'c', [(0, 1), (1, 0)])  24.6 us
    pallas_call x2, Pallas kernels, weight_grads(): pl.pallas_call(kernel, grid=(width // tile,), in_specs=[pl.BlockSpec(left...  20.5 us
    pallas_call x2, Pallas kernels, input_products(): pl.pallas_call(kernel, grid=(steps,), in_specs=([pl.BlockSpec(memory_spac...  17.9 us
    pallas_call x4, Pallas kernels, down_products(): pl.pallas_call(kernel, grid=(2,), in_specs=in_specs, out_specs=[pl.BlockS...  7.24 us
  transfers between devices with their start and end apart: 46, of which 25 were waited for; matrix products, arithmetic and copies ran while one was open for 2% of the time, Pallas kernels for 17%

profile of v1, /device:TPU:1, one launch (start us, length us, event | category | flops | bytes accessed | tf_op | source)
XLA Modules:
  0.0 257.9 jit_solution(7262041819686441848)
XLA Ops:
  14.2 2.9 %collective-permute-start.3 = (bf16[2,1,64,1792]{3,2,1,0:T(8,128)(2,1)S(1)}, bf16[2,1,64,1792]{3,2,1,0:T(8,128)(2,1)S(1)}, u32[]{:S(2)}, u32[]{:S(2)}) collective-permute-start(bf16[2,1,64,1792]{3,2,1,0:T(8,128)(2,1)S(1)} %pad_maximum_fusion.7), channel_id=1, source_target_pairs={{0,64},{1,17},{8,72},{9,25},{16,80},{17,1},{24,88},{25,9},{32,96},... | collective-permute-start | bytes 1376264 | tf_op jit(solution)/shard_map/ppermute | solution.py:26
  17.9 3.3 %collective-permute-done.4 = bf16[2,1,64,1792]{3,2,1,0:T(8,128)(2,1)S(1)} collective-permute-done((bf16[2,1,64,1792]{3,2,1,0:T(8,128)(2,1)S(1)}, bf16[2,1,64,1792]{3,2,1,0:T(8,128)(2,1)S(1)}, u32[]{:S(2)}, u32[]{:S(2)}) %collective-permute-start.4) | collective-permute-done | bytes 458784 | tf_op jit(solution)/shard_map/ppermute | solution.py:26
  21.3 6.1 %collective-permute-done.3 = bf16[2,1,64,1792]{3,2,1,0:T(8,128)(2,1)S(1)} collective-permute-done((bf16[2,1,64,1792]{3,2,1,0:T(8,128)(2,1)S(1)}, bf16[2,1,64,1792]{3,2,1,0:T(8,128)(2,1)S(1)}, u32[]{:S(2)}, u32[]{:S(2)}) %collective-permute-start.3) | collective-permute-done | bytes 458784 | tf_op jit(solution)/shard_map/ppermute | solution.py:26
  34.4 8.5 %collective-permute-done.7.refs_3_ = bf16[1,256,1792]{2,1,0:T(8,128)(2,1)S(1)} collective-permute-done((bf16[1,256,1792]{2,1,0:T(8,128)(2,1)S(1)}, bf16[1,256,1792]{2,1,0:T(8,128)(2,1)S(1)}, u32[]{:S(2)}, u32[]{:S(2)}) %collective-permute-start.7) | collective-permute-done | bytes 917536 | tf_op jit(solution)/shard_map/ppermute | solution.py:26
  53.1 3.6 %collective-permute-done.8 = bf16[1,256,1792]{2,1,0:T(8,128)(2,1)} collective-permute-done((bf16[1,256,1792]{2,1,0:T(8,128)(2,1)}, bf16[1,256,1792]{2,1,0:T(8,128)(2,1)}, u32[]{:S(2)}, u32[]{:S(2)}) %collective-permute-start.8) | collective-permute-done | bytes 917536 | tf_op jit(solution)/shard_map/ppermute | solution.py:26
  63.5 9.6 %collective-permute-done.11.refs_2_ = bf16[256,1792]{1,0:T(8,128)(2,1)S(1)} collective-permute-done((bf16[256,1792]{1,0:T(8,128)(2,1)S(1)}, bf16[256,1792]{1,0:T(8,128)(2,1)S(1)}, u32[]{:S(2)}, u32[]{:S(2)}) %collective-permute-start.11) | collective-permute-done | bytes 917536 | tf_op jit(solution)/shard_map/ppermute | solution.py:26
  75.1 2.7 %collective-permute-start.16 = (bf16[256,1792]{1,0:T(8,128)(2,1)S(1)}, bf16[256,1792]{1,0:T(8,128)(2,1)S(1)}, u32[]{:S(2)}, u32[]{:S(2)}) collective-permute-start(bf16[256,1792]{1,0:T(8,128)(2,1)S(1)} %get-tuple-element.54), channel_id=1, source_target_pairs={{0,24},{1,97},{8,0},{9,105},{16,8},{17,113},{24,16},{25,121},{32,5... | collective-permute-start | bytes 2752520 | tf_op jit(solution)/shard_map/ppermute | solution.py:26
  77.8 4.4 %collective-permute-done.14.refs_3_ = bf16[256,1792]{1,0:T(8,128)(2,1)S(1)} collective-permute-done((bf16[256,1792]{1,0:T(8,128)(2,1)S(1)}, bf16[256,1792]{1,0:T(8,128)(2,1)S(1)}, u32[]{:S(2)}, u32[]{:S(2)}) %collective-permute-start.14) | collective-permute-done | bytes 917536 | tf_op jit(solution)/shard_map/ppermute | solution.py:26
  82.9 9.8 %collective-permute-done.13.refs_2_ = bf16[256,1792]{1,0:T(8,128)(2,1)S(1)} collective-permute-done((bf16[256,1792]{1,0:T(8,128)(2,1)S(1)}, bf16[256,1792]{1,0:T(8,128)(2,1)S(1)}, u32[]{:S(2)}, u32[]{:S(2)}) %collective-permute-start.13) | collective-permute-done | bytes 917536 | tf_op jit(solution)/shard_map/ppermute | solution.py:26
  94.9 2.7 %collective-permute-start.18 = (bf16[1,256,1792]{2,1,0:T(8,128)(2,1)}, bf16[1,256,1792]{2,1,0:T(8,128)(2,1)S(1)}, u32[]{:S(2)}, u32[]{:S(2)}) collective-permute-start(bf16[1,256,1792]{2,1,0:T(8,128)(2,1)} %collective-permute-done.5.refs_1_), channel_id=1, source_target_pairs={{0,24},{1,97},{8,0},{9,105},{16,8},{17,113},{24,16},{25,121},{32,5... | collective-permute-start | bytes 2752520 | tf_op jit(solution)/shard_map/ppermute | solution.py:26
  101.2 9.2 %collective-permute-done.18.refs_2_ = bf16[1,256,1792]{2,1,0:T(8,128)(2,1)S(1)} collective-permute-done((bf16[1,256,1792]{2,1,0:T(8,128)(2,1)}, bf16[1,256,1792]{2,1,0:T(8,128)(2,1)S(1)}, u32[]{:S(2)}, u32[]{:S(2)}) %collective-permute-start.18) | collective-permute-done | bytes 917536 | tf_op jit(solution)/shard_map/ppermute | solution.py:26
  110.4 11.1 %collective-permute-start.23 = (bf16[1,64,1792]{2,1,0:T(8,128)(2,1)S(1)}, bf16[1,64,1792]{2,1,0:T(8,128)(2,1)S(1)}, u32[]{:S(2)}, u32[]{:S(2)}) collective-permute-start(bf16[1,64,1792]{2,1,0:T(8,128)(2,1)S(1)} %dynamic-slice_bitcast_fusion), channel_id=1, source_target_pairs={{0,1},{1,0},{2,3},{3,2},{4,5},{5,4},{6,7},{7,6},{8,9},{9,8},{10,11... | collective-permute-start | bytes 688136 | tf_op jit(solution)/shard_map/ppermute | solution.py:34
  127.9 10.0 %collective-permute-done.25 = bf16[2,2,64,1792]{3,2,1,0:T(8,128)(2,1)S(1)} collective-permute-done((bf16[2,2,64,1792]{3,2,1,0:T(8,128)(2,1)S(1)}, bf16[2,2,64,1792]{3,2,1,0:T(8,128)(2,1)S(1)}, u32[]{:S(2)}, u32[]{:S(2)}) %collective-permute-start.25) | collective-permute-done | bytes 917536 | tf_op jit(solution)/shard_map/ppermute | solution.py:26
  138.7 9.8 %collective-permute-done.24 = bf16[2,2,64,1792]{3,2,1,0:T(8,128)(2,1)S(1)} collective-permute-done((bf16[2,2,64,1792]{3,2,1,0:T(8,128)(2,1)S(1)}, bf16[2,2,64,1792]{3,2,1,0:T(8,128)(2,1)S(1)}, u32[]{:S(2)}, u32[]{:S(2)}) %collective-permute-start.24) | collective-permute-done | bytes 917536 | tf_op jit(solution)/shard_map/ppermute | solution.py:26
  148.5 3.6 %collective-permute-done.26 = bf16[2,2,64,1792]{3,2,1,0:T(8,128)(2,1)S(1)} collective-permute-done((bf16[2,2,64,1792]{3,2,1,0:T(8,128)(2,1)S(1)}, bf16[2,2,64,1792]{3,2,1,0:T(8,128)(2,1)S(1)}, u32[]{:S(2)}, u32[]{:S(2)}) %collective-permute-start.26) | collective-permute-done | bytes 917536 | tf_op jit(solution)/shard_map/ppermute | solution.py:26
  157.1 2.9 %collective-permute-start.33 = (bf16[1,256,1792]{2,1,0:T(8,128)(2,1)S(1)}, bf16[1,256,1792]{2,1,0:T(8,128)(2,1)S(1)}, u32[]{:S(2)}, u32[]{:S(2)}) collective-permute-start(bf16[1,256,1792]{2,1,0:T(8,128)(2,1)S(1)} %collective-permute-done.17), channel_id=1, source_target_pairs={{0,1},{1,0},{2,3},{3,2},{4,5},{5,4},{6,7},{7,6},{8,9},{9,8},{10,11... | collective-permute-start | bytes 2752520 | tf_op jit(solution)/shard_map/ppermute | solution.py:34
  162.5 8.8 %weight_grads.2 = f32[1792,512]{1,0:T(8,128)} custom-call(bf16[4,256,512]{2,1,0:T(8,128)(2,1)S(1)} %get-tuple-element.44.refs_0_.refs_2_.refs_3_.refs_4_.mine_ref, bf16[4,256,512]{2,1,0:T(8,128)(2,1)S(1)} %get-tuple-element.60.theirs_ref, bf16[1,256,1792]{2,1,0:T(8,128)(2,1)S(1)} %bitcast.102, bf16[1,256,1792]{2,1,0:T(8,128)(2,1)} %collective-permute-done.5.refs_1_, ...), custom_call_target="tpu_custom_call" | custom-call | flops 3758096384 | bytes 11010048 | tf_op jit(solution)/shard_map/weight_grads/pallas_call | solution.py:176
  171.2 5.0 %collective-permute-done.29.refs_2_.refs_3_ = bf16[2,256,1792]{2,1,0:T(8,128)(2,1)S(1)} collective-permute-done((bf16[2,256,1792]{2,1,0:T(8,128)(2,1)S(1)}, bf16[2,256,1792]{2,1,0:T(8,128)(2,1)S(1)}, u32[]{:S(2)}, u32[]{:S(2)}) %collective-permute-start.29) | collective-permute-done | bytes 1835040 | tf_op jit(solution)/shard_map/ppermute | solution.py:26
  176.2 18.9 %collective-permute-done.30.refs_4_ = bf16[2,256,1792]{2,1,0:T(8,128)(2,1)S(1)} collective-permute-done((bf16[2,256,1792]{2,1,0:T(8,128)(2,1)S(1)}, bf16[2,256,1792]{2,1,0:T(8,128)(2,1)S(1)}, u32[]{:S(2)}, u32[]{:S(2)}) %collective-permute-start.30) | collective-permute-done | bytes 1835040 | tf_op jit(solution)/shard_map/ppermute | solution.py:26
  201.7 12.9 %input_products.2 = (bf16[256,512]{1,0:T(8,128)(2,1)S(1)}, bf16[256,512]{1,0:T(8,128)(2,1)S(1)}, bf16[256,512]{1,0:T(8,128)(2,1)S(1)}) custom-call(bf16[2,256,1792]{2,1,0:T(8,128)(2,1)S(1)} %bitcast.92, bf16[2,256,1792]{2,1,0:T(8,128)(2,1)S(1)} %collective-permute-done.27.refs_1_, bf16[2,256,1792]{2,1,0:T(8,128)(2,1)S(1)} %collective-permute-done.29.refs_2_.refs_3_, ...), custom_call_target="tpu_custom_call" | custom-call | flops 5637144576 | bytes 18350080 | tf_op jit(solution)/shard_map/input_products/pallas_call | solution.py:256
  214.7 6.1 %collective-permute-done.35.refs_1_.refs_2_ = bf16[2,256,1792]{2,1,0:T(8,128)(2,1)S(1)} collective-permute-done((bf16[2,256,1792]{2,1,0:T(8,128)(2,1)S(1)}, bf16[2,256,1792]{2,1,0:T(8,128)(2,1)S(1)}, u32[]{:S(2)}, u32[]{:S(2)}) %collective-permute-start.35) | collective-permute-done | bytes 1835040 | tf_op jit(solution)/shard_map/ppermute | solution.py:26
  220.8 4.5 %collective-permute-done.36.refs_2_ = bf16[2,256,1792]{2,1,0:T(8,128)(2,1)S(1)} collective-permute-done((bf16[2,256,1792]{2,1,0:T(8,128)(2,1)S(1)}, bf16[2,256,1792]{2,1,0:T(8,128)(2,1)S(1)}, u32[]{:S(2)}, u32[]{:S(2)}) %collective-permute-start.36) | collective-permute-done | bytes 1835040 | tf_op jit(solution)/shard_map/ppermute | solution.py:26
  226.2 5.0 %input_products.3 = (bf16[2,2,64,512]{3,2,1,0:T(8,128)(2,1)S(1)}, bf16[2,2,64,512]{3,2,1,0:T(8,128)(2,1)S(1)}, bf16[2,2,64,512]{3,2,1,0:T(8,128)(2,1)S(1)}, bf16[2,2,64,512]{3,2,1,0:T(8,128)(2,1)S(1)}) custom-call(s32[4]{0:T(128)S(1)} %pad_add_fusion.place_ref.refs_0_, bf16[2,256,1792]{2,1,0:T(8,128)(2,1)S(1)} %collective-permute-done.35.refs_1_.refs_2_, ...), custom_call_target="tpu_custom_call" | custom-call | flops 1879048192 | bytes 11010048 | tf_op jit(solution)/shard_map/input_products/pallas_call | solution.py:256
  236.3 11.7 %weight_grads.3 = (f32[512,1792]{1,0:T(8,128)}, f32[512,1792]{1,0:T(8,128)}) custom-call(bf16[4,256,512]{2,1,0:T(8,128)(2,1)S(1)} %get-tuple-element.62.mine_ref, bf16[4,256,512]{2,1,0:T(8,128)(2,1)S(1)} %get-tuple-element.76.theirs_ref, bf16[2,256,1792]{2,1,0:T(8,128)(2,1)S(1)} %bitcast.93, bf16[2,256,1792]{2,1,0:T(8,128)(2,1)S(1)} %collective-permute-done.27.refs_1_, ...), custom_call_target="tpu_custom_call" | custom-call | flops 7516192768 | bytes 22020096 | tf_op jit(solution)/shard_map/weight_grads/pallas_call | solution.py:176
  (126 shorter events, 70.5 us)
Async XLA Ops:
  7.2 39.4 %all-gather.2.cloned.1.call-start = ((), (), s32[]{:S(2)}) async-start(), calls=%async_computation | async-start | bytes 4718592 | tf_op jit(solution)/shard_map/all_gather | solution.py:281
  13.7 30.4 %collective-permute-start = (bf16[1792,512]{1,0:T(8,128)(2,1)S(1)}, bf16[1792,512]{1,0:T(8,128)(2,1)S(1)}, u32[]{:S(2)}, u32[]{:S(2)}) collective-permute-start(bf16[1792,512]{1,0:T(8,128)(2,1)S(1)} %copy-done), channel_id=1, source_target_pairs={{0,1},{1,0},{2,3},{3,2},{4,5},{5,4},{6,7},{7,6},{8,9},{9,8},{10,11... | collective-permute-start | bytes 5505032 | tf_op jit(solution)/shard_map/ppermute | solution.py:34
  30.2 29.1 %collective-permute-start.9 = (bf16[512,1792]{1,0:T(8,128)(2,1)}, bf16[512,1792]{1,0:T(8,128)(2,1)}, u32[]{:S(2)}, u32[]{:S(2)}) collective-permute-start(bf16[512,1792]{1,0:T(8,128)(2,1)} %refs_3_.3), channel_id=1, source_target_pairs={{0,1},{1,0},{2,3},{3,2},{4,5},{5,4},{6,7},{7,6},{8,9},{9,8},{10,11... | collective-permute-start | bytes 5505032 | tf_op jit(solution)/shard_map/ppermute | solution.py:34
  31.0 28.3 %collective-permute-start.10 = (bf16[512,1792]{1,0:T(8,128)(2,1)}, bf16[512,1792]{1,0:T(8,128)(2,1)}, u32[]{:S(2)}, u32[]{:S(2)}) collective-permute-start(bf16[512,1792]{1,0:T(8,128)(2,1)} %refs_4_.1), channel_id=1, source_target_pairs={{0,1},{1,0},{2,3},{3,2},{4,5},{5,4},{6,7},{7,6},{8,9},{9,8},{10,11... | collective-permute-start | bytes 5505032 | tf_op jit(solution)/shard_map/ppermute | solution.py:34
  31.0 22.1 %collective-permute-start.5 = (bf16[1,256,1792]{2,1,0:T(8,128)(2,1)S(1)}, bf16[1,256,1792]{2,1,0:T(8,128)(2,1)}, u32[]{:S(2)}, u32[]{:S(2)}) collective-permute-start(bf16[1,256,1792]{2,1,0:T(8,128)(2,1)S(1)} %bitcast.101), channel_id=1, source_target_pairs={{0,24},{1,97},{8,0},{9,105},{16,8},{17,113},{24,16},{25,121},{32,5... | collective-permute-start | bytes 2752520 | tf_op jit(solution)/shard_map/ppermute | solution.py:26
  62.0 20.2 %collective-permute-start.14 = (bf16[256,1792]{1,0:T(8,128)(2,1)S(1)}, bf16[256,1792]{1,0:T(8,128)(2,1)S(1)}, u32[]{:S(2)}, u32[]{:S(2)}) collective-permute-start(bf16[256,1792]{1,0:T(8,128)(2,1)S(1)} %get-tuple-element.52), channel_id=1, source_target_pairs={{0,24},{1,97},{8,0},{9,105},{16,8},{17,113},{24,16},{25,121},{32,5... | collective-permute-start | bytes 2752520 | tf_op jit(solution)/shard_map/ppermute | solution.py:26
  62.1 20.9 %collective-permute-start.15 = (bf16[256,1792]{1,0:T(8,128)(2,1)S(1)}, bf16[256,1792]{1,0:T(8,128)(2,1)S(1)}, u32[]{:S(2)}, u32[]{:S(2)}) collective-permute-start(bf16[256,1792]{1,0:T(8,128)(2,1)S(1)} %get-tuple-element.53), channel_id=1, source_target_pairs={{0,8},{1,33},{8,16},{9,41},{16,24},{17,49},{24,0},{25,57},{32,40},... | collective-permute-start | bytes 2752520 | tf_op jit(solution)/shard_map/ppermute | solution.py:26
  97.6 23.8 %collective-permute-start.17 = (bf16[1,256,1792]{2,1,0:T(8,128)(2,1)}, bf16[1,256,1792]{2,1,0:T(8,128)(2,1)S(1)}, u32[]{:S(2)}, u32[]{:S(2)}) collective-permute-start(bf16[1,256,1792]{2,1,0:T(8,128)(2,1)} %collective-permute-done.6), channel_id=1, source_target_pairs={{0,8},{1,33},{8,16},{9,41},{16,24},{17,49},{24,0},{25,57},{32,40},... | collective-permute-start | bytes 2752520 | tf_op jit(solution)/shard_map/ppermute | solution.py:26
  97.8 25.2 %collective-permute-start.19 = (bf16[2,64,1792]{2,1,0:T(8,128)(2,1)S(1)}, bf16[2,64,1792]{2,1,0:T(8,128)(2,1)S(1)}, u32[]{:S(2)}, u32[]{:S(2)}) collective-permute-start(bf16[2,64,1792]{2,1,0:T(8,128)(2,1)S(1)} %get-tuple-element.87), channel_id=1, source_target_pairs={{0,32},{1,9},{8,40},{9,17},{16,48},{17,25},{24,56},{25,1},{32,64},... | collective-permute-start | bytes 1376264 | tf_op jit(solution)/shard_map/ppermute | solution.py:26
  98.7 24.3 %collective-permute-start.20 = (bf16[2,64,1792]{2,1,0:T(8,128)(2,1)S(1)}, bf16[2,64,1792]{2,1,0:T(8,128)(2,1)S(1)}, u32[]{:S(2)}, u32[]{:S(2)}) collective-permute-start(bf16[2,64,1792]{2,1,0:T(8,128)(2,1)S(1)} %get-tuple-element.88), channel_id=1, source_target_pairs={{0,96},{1,25},{8,104},{9,1},{16,112},{17,9},{24,120},{25,17},{32,0... | collective-permute-start | bytes 1376264 | tf_op jit(solution)/shard_map/ppermute | solution.py:26
  100.6 22.4 %collective-permute-start.21 = (bf16[2,64,1792]{2,1,0:T(8,128)(2,1)S(1)}, bf16[2,64,1792]{2,1,0:T(8,128)(2,1)S(1)}, u32[]{:S(2)}, u32[]{:S(2)}) collective-permute-start(bf16[2,64,1792]{2,1,0:T(8,128)(2,1)S(1)} %get-tuple-element.89), channel_id=1, source_target_pairs={{0,64},{1,17},{8,72},{9,25},{16,80},{17,1},{24,88},{25,9},{32,96},... | collective-permute-start | bytes 1376264 | tf_op jit(solution)/shard_map/ppermute | solution.py:26
  126.3 22.2 %collective-permute-start.24 = (bf16[2,2,64,1792]{3,2,1,0:T(8,128)(2,1)S(1)}, bf16[2,2,64,1792]{3,2,1,0:T(8,128)(2,1)S(1)}, u32[]{:S(2)}, u32[]{:S(2)}) collective-permute-start(bf16[2,2,64,1792]{3,2,1,0:T(8,128)(2,1)S(1)} %pad_maximum_fusion.3), channel_id=1, source_target_pairs={{0,96},{1,25},{8,104},{9,1},{16,112},{17,9},{24,120},{25,17},{32,0... | collective-permute-start | bytes 2752520 | tf_op jit(solution)/shard_map/ppermute | solution.py:26
  127.0 28.5 %collective-permute-start.31 = (bf16[1,256,1792]{2,1,0:T(8,128)(2,1)}, bf16[1,256,1792]{2,1,0:T(8,128)(2,1)S(1)}, u32[]{:S(2)}, u32[]{:S(2)}) collective-permute-start(bf16[1,256,1792]{2,1,0:T(8,128)(2,1)} %bitcast.9), channel_id=1, source_target_pairs={{0,1},{1,0},{2,3},{3,2},{4,5},{5,4},{6,7},{7,6},{8,9},{9,8},{10,11... | collective-permute-start | bytes 2752520 | tf_op jit(solution)/shard_map/ppermute | solution.py:34
  127.4 29.4 %collective-permute-start.32 = (bf16[1,256,1792]{2,1,0:T(8,128)(2,1)}, bf16[1,256,1792]{2,1,0:T(8,128)(2,1)S(1)}, u32[]{:S(2)}, u32[]{:S(2)}) collective-permute-start(bf16[1,256,1792]{2,1,0:T(8,128)(2,1)} %collective-permute-done.8), channel_id=1, source_target_pairs={{0,1},{1,0},{2,3},{3,2},{4,5},{5,4},{6,7},{7,6},{8,9},{9,8},{10,11... | collective-permute-start | bytes 2752520 | tf_op jit(solution)/shard_map/ppermute | solution.py:34
  127.5 29.6 %collective-permute-start.34 = (bf16[1,256,1792]{2,1,0:T(8,128)(2,1)}, bf16[1,256,1792]{2,1,0:T(8,128)(2,1)S(1)}, u32[]{:S(2)}, u32[]{:S(2)}) collective-permute-start(bf16[1,256,1792]{2,1,0:T(8,128)(2,1)} %collective-permute-done.6), channel_id=1, source_target_pairs={{0,1},{1,0},{2,3},{3,2},{4,5},{5,4},{6,7},{7,6},{8,9},{9,8},{10,11... | collective-permute-start | bytes 2752520 | tf_op jit(solution)/shard_map/ppermute | solution.py:34
  152.5 23.6 %collective-permute-start.29 = (bf16[2,256,1792]{2,1,0:T(8,128)(2,1)S(1)}, bf16[2,256,1792]{2,1,0:T(8,128)(2,1)S(1)}, u32[]{:S(2)}, u32[]{:S(2)}) collective-permute-start(bf16[2,256,1792]{2,1,0:T(8,128)(2,1)S(1)} %bitcast.90), channel_id=1, source_target_pairs={{0,8},{1,33},{8,16},{9,41},{16,24},{17,49},{24,0},{25,57},{32,40},... | collective-permute-start | bytes 5505032 | tf_op jit(solution)/shard_map/ppermute | solution.py:26
  152.6 23.6 %collective-permute-start.27 = (bf16[2,256,1792]{2,1,0:T(8,128)(2,1)S(1)}, bf16[2,256,1792]{2,1,0:T(8,128)(2,1)S(1)}, u32[]{:S(2)}, u32[]{:S(2)}) collective-permute-start(bf16[2,256,1792]{2,1,0:T(8,128)(2,1)S(1)} %bitcast.91), channel_id=1, source_target_pairs={{0,24},{1,97},{8,0},{9,105},{16,8},{17,113},{24,16},{25,121},{32,5... | collective-permute-start | bytes 5505032 | tf_op jit(solution)/shard_map/ppermute | solution.py:26
  155.5 39.6 %collective-permute-start.30 = (bf16[2,256,1792]{2,1,0:T(8,128)(2,1)S(1)}, bf16[2,256,1792]{2,1,0:T(8,128)(2,1)S(1)}, u32[]{:S(2)}, u32[]{:S(2)}) collective-permute-start(bf16[2,256,1792]{2,1,0:T(8,128)(2,1)S(1)} %bitcast.94), channel_id=1, source_target_pairs={{0,24},{1,97},{8,0},{9,105},{16,8},{17,113},{24,16},{25,121},{32,5... | collective-permute-start | bytes 5505032 | tf_op jit(solution)/shard_map/ppermute | solution.py:26
  156.8 39.1 %collective-permute-start.28 = (bf16[2,256,1792]{2,1,0:T(8,128)(2,1)S(1)}, bf16[2,256,1792]{2,1,0:T(8,128)(2,1)S(1)}, u32[]{:S(2)}, u32[]{:S(2)}) collective-permute-start(bf16[2,256,1792]{2,1,0:T(8,128)(2,1)S(1)} %bitcast.95), channel_id=1, source_target_pairs={{0,8},{1,33},{8,16},{9,41},{16,24},{17,49},{24,0},{25,57},{32,40},... | collective-permute-start | bytes 5505032 | tf_op jit(solution)/shard_map/ppermute | solution.py:26
  162.1 52.6 %collective-permute-start.37 = (bf16[2,256,1792]{2,1,0:T(8,128)(2,1)S(1)}, bf16[2,256,1792]{2,1,0:T(8,128)(2,1)S(1)}, u32[]{:S(2)}, u32[]{:S(2)}) collective-permute-start(bf16[2,256,1792]{2,1,0:T(8,128)(2,1)S(1)} %bitcast.96), channel_id=1, source_target_pairs={{0,1},{1,0},{2,3},{3,2},{4,5},{5,4},{6,7},{7,6},{8,9},{9,8},{10,11... | collective-permute-start | bytes 5505032 | tf_op jit(solution)/shard_map/ppermute | solution.py:34
  195.9 18.8 %collective-permute-start.38 = (bf16[2,256,1792]{2,1,0:T(8,128)(2,1)S(1)}, bf16[2,256,1792]{2,1,0:T(8,128)(2,1)S(1)}, u32[]{:S(2)}, u32[]{:S(2)}) collective-permute-start(bf16[2,256,1792]{2,1,0:T(8,128)(2,1)S(1)} %collective-permute-done.30.refs_4_), channel_id=1, source_target_pairs={{0,1},{1,0},{2,3},{3,2},{4,5},{5,4},{6,7},{7,6},{8,9},{9,8},{10,11... | collective-permute-start | bytes 5505032 | tf_op jit(solution)/shard_map/ppermute | solution.py:34
  198.4 22.4 %collective-permute-start.35 = (bf16[2,256,1792]{2,1,0:T(8,128)(2,1)S(1)}, bf16[2,256,1792]{2,1,0:T(8,128)(2,1)S(1)}, u32[]{:S(2)}, u32[]{:S(2)}) collective-permute-start(bf16[2,256,1792]{2,1,0:T(8,128)(2,1)S(1)} %collective-permute-done.27.refs_1_), channel_id=1, source_target_pairs={{0,24},{1,97},{8,0},{9,105},{16,8},{17,113},{24,16},{25,121},{32,5... | collective-permute-start | bytes 5505032 | tf_op jit(solution)/shard_map/ppermute | solution.py:26
  200.0 20.8 %collective-permute-start.39 = (bf16[2,256,1792]{2,1,0:T(8,128)(2,1)S(1)}, bf16[2,256,1792]{2,1,0:T(8,128)(2,1)S(1)}, u32[]{:S(2)}, u32[]{:S(2)}) collective-permute-start(bf16[2,256,1792]{2,1,0:T(8,128)(2,1)S(1)} %collective-permute-done.28.refs_5_), channel_id=1, source_target_pairs={{0,1},{1,0},{2,3},{3,2},{4,5},{5,4},{6,7},{7,6},{8,9},{9,8},{10,11... | collective-permute-start | bytes 5505032 | tf_op jit(solution)/shard_map/ppermute | solution.py:34
  201.7 23.6 %collective-permute-start.36 = (bf16[2,256,1792]{2,1,0:T(8,128)(2,1)S(1)}, bf16[2,256,1792]{2,1,0:T(8,128)(2,1)S(1)}, u32[]{:S(2)}, u32[]{:S(2)}) collective-permute-start(bf16[2,256,1792]{2,1,0:T(8,128)(2,1)S(1)} %collective-permute-done.28.refs_5_), channel_id=1, source_target_pairs={{0,8},{1,33},{8,16},{9,41},{16,24},{17,49},{24,0},{25,57},{32,40},... | collective-permute-start | bytes 5505032 | tf_op jit(solution)/shard_map/ppermute | solution.py:26
  (31 other events, 286.4 us)
Sparse Core Ops, SparseCore 0:
  9.7 35.9 all-gather.1

commit v2 on v1

v2 whole, which is shorter than its diff:
```python
import jax
import jax.numpy as jnp
from jax import lax
from jax.experimental import pallas as pl
from jax.experimental.pallas import tpu as pltpu
from jax.sharding import Mesh, PartitionSpec as P

F32 = jnp.float32
BF16 = jnp.bfloat16
RING = 4
LAST = (((1,), (1,)), ((), ()))
FIRST = (((0,), (0,)), ((), ()))
MIB = 2**20


def mix(value, phase, step):
    pairs = []
    for x in range(RING):
        for y in range(RING):
            for core in range(2):
                if (core == 0) == (phase == 1):
                    to = ((x + step) % RING, y)
                else:
                    to = (x, (y + step) % RING)
                pairs.append(((x * RING + y) * 2 + core, (to[0] * RING + to[1]) * 2 + core))
    return lax.ppermute(value, ("x", "y", "c"), pairs)


def along_z(value, step):
    return lax.ppermute(value, "z", [(z, (z + step) % RING) for z in range(RING)])


def swap(value):
    return lax.ppermute(value, "c", [(0, 1), (1, 0)])


def pick(value, at, axis=0):
    return lax.dynamic_index_in_dim(value, at, axis, keepdims=False)


def tie(value, *after):
    return lax.optimization_barrier((value, *after))[0]


def params(mebibytes):
    return pltpu.CompilerParams(vmem_limit_bytes=mebibytes * MIB)


def light():
    return pl.CostEstimate(flops=1, bytes_accessed=1, transcendentals=0)


def travel_order(place, value, part, flip=False):
    tokens, model = value.shape[0], value.shape[1] // 2
    half = tokens // 32
    value = value.reshape(RING, RING, 2, half, 2 * model)

    def kernel(place_ref, value_ref, *results):
        x, y, core = place_ref[0], place_ref[1], place_ref[3]
        for i, owner in enumerate((core, 1 - core)):
            for second in range(RING):
                block = []
                for first in range(RING):
                    at_x = lax.rem(x + jnp.where(owner == 0, first, second), RING)
                    at_y = lax.rem(y + jnp.where(owner == 0, second, first), RING)
                    block.append(value_ref[at_x, at_y, owner])
                block = jnp.concatenate(block, 0)
                if flip:
                    at = (i * RING + second) * RING * half
                    results[0][:, at : at + RING * half] = block.T
                else:
                    results[i][second] = block

    shape, count = ((model, tokens), 1) if flip else ((RING, RING * half, model), 2)
    return pl.pallas_call(
        kernel,
        grid=(1,),
        in_specs=[
            pl.BlockSpec(memory_space=pltpu.SMEM),
            pl.BlockSpec((RING, RING, 2, half, model), lambda j: (0, 0, 0, 0, part)),
        ],
        out_specs=[pl.BlockSpec(shape, lambda j: (0,) * len(shape))] * count,
        out_shape=[jax.ShapeDtypeStruct(shape, BF16)] * count,
        compiler_params=params(12),
        cost_estimate=light(),
        name="travel_order",
    )(place, value)


def down_products(tokens, groups):
    _, rows, model = tokens.shape
    parts = [part for group in groups for part in group]
    width = parts[0][1].shape[0]
    tile = width // 2
    operands, in_specs = [], []
    for k, weight, extras in parts:
        operands += [tokens, weight] + [stack for stack, _ in extras]
        in_specs.append(pl.BlockSpec((1, rows, model), lambda j, k=k: (k, 0, 0)))
        in_specs.append(pl.BlockSpec((tile, model), lambda j: (j, 0)))
        for _, at in extras:
            in_specs.append(pl.BlockSpec((1, rows, tile), lambda j, at=at: (at, 0, j)))

    def kernel(*refs):
        at = 0
        for out, group in zip(refs[len(operands) :], groups):
            for n, (_, _, extras) in enumerate(group):
                total = lax.dot_general(
                    refs[at][0], refs[at + 1][...], LAST, preferred_element_type=F32
                )
                for i in range(len(extras)):
                    total = total + refs[at + 2 + i][0].astype(F32)
                at += 2 + len(extras)
                out[n] = total.astype(BF16)

    return pl.pallas_call(
        kernel,
        grid=(2,),
        in_specs=in_specs,
        out_specs=[pl.BlockSpec((len(group), rows, tile), lambda j: (0, 0, j)) for group in groups],
        out_shape=[jax.ShapeDtypeStruct((len(group), rows, width), BF16) for group in groups],
        compiler_params=params(14),
        cost_estimate=light(),
        name="down_products",
    )(*operands)


def scatter_sum(tokens, weight, weight_other, before, between, beside):
    (fwd,) = down_products(tokens, [[(2, weight, ()), (1, weight_other, ())]])
    (back,) = down_products(tokens, [[(2, weight_other, ()), (3, weight, ())]])
    fwd, back, *_ = lax.optimization_barrier((fwd, back, *before))
    fwd, back = mix(fwd, 2, 1), mix(back, 2, -1)
    moved = between()
    own, other = down_products(
        tokens, [[(1, weight, ((fwd, 0),))], [(3, weight_other, ((back, 0),))]]
    )
    own, other = mix(own, 2, 1), mix(other, 2, -1)
    (sums,) = down_products(
        tie(tokens, *moved),
        [
            [
                (0, weight, ((own, 0), (back, 1))),
                (0, weight_other, ((fwd, 1), (other, 0))),
            ]
        ],
    )
    sums = sums.reshape(2, RING, -1, sums.shape[-1])
    done = beside(sums, *moved)
    total = tie(sums[:, 0], *done).astype(F32)
    for distance, step in ((2, 2), (1, 1), (3, -1)):
        total = total + mix(sums[:, distance], 1, step).astype(F32)
    return total, moved, done


def first_gather(block):
    _, n, half, width = block.shape
    across, after, before = mix(block, 1, 2), mix(block, 1, -1), mix(block, 1, 1)
    return tuple(
        jnp.stack([piece[i] for piece in (block, after, across, before)], 1).reshape(
            n, RING * half, width
        )
        for i in range(2)
    )


def weight_grads(left, mine, theirs, flip=False):
    n, rows, width = mine[0].shape
    ready = len(left) == 1
    model = left[0].shape[0] if ready else left[0].shape[2]
    places = [0] * RING + ([0] * RING if isinstance(theirs, list) else list(range(RING)))
    pieces = [*mine, *(theirs if isinstance(theirs, list) else [theirs] * RING)]
    tile = 256

    def kernel(*refs):
        left_refs, refs = refs[: len(left)], refs[len(left) :]
        held = left_refs[0]
        if not ready:
            held = refs[-1]

            @pl.when(pl.program_id(0) == 0)
            def _():
                for i, ref in enumerate(left_refs):
                    for k in range(RING):
                        at = (i * RING + k) * rows
                        held[:, at : at + rows] = ref[k].T

        for i in range(n):
            right = jnp.concatenate([ref[i] for ref in refs[: len(pieces)]], 0)
            result = jnp.dot(held[...], right, preferred_element_type=F32)
            refs[len(pieces) + i][...] = result.T if flip else result

    if flip:
        shape, out_spec = (width, model), pl.BlockSpec((tile, model), lambda j: (j, 0))
    else:
        shape, out_spec = (model, width), pl.BlockSpec((model, tile), lambda j: (0, j))
    scratch = [] if ready else [pltpu.VMEM((model, rows * len(pieces)), BF16)]
    return pl.pallas_call(
        kernel,
        grid=(width // tile,),
        in_specs=[pl.BlockSpec(a.shape, lambda j, r=a.ndim: (0,) * r) for a in left]
        + [pl.BlockSpec((n, rows, tile), lambda j, at=at: (at, 0, j)) for at in places],
        out_specs=[out_spec] * n,
        out_shape=[jax.ShapeDtypeStruct(shape, F32)] * n,
        scratch_shapes=scratch,
        compiler_params=params(18 if n > 1 else 14),
        cost_estimate=light(),
        name="weight_grads",
    )(*left, *pieces)


def input_products(groups, ready=(), place=None, whole=True):
    last = place is not None
    terms = [term for group in groups for term in group]
    _, rows, width = terms[0][0].shape
    model = terms[0][1][0][0].shape[-2]
    tile = 256 if len(terms) > 1 else width // 2
    steps = width // tile
    half = rows // RING
    pairs = {id(weights): weights for _, weights in terms}
    order = list(pairs)
    weights = [weight for key in order for weight in pairs[key]]
    inputs = ([place] if last else []) + [piece for piece, _ in terms]
    inputs += [weight for weight, _ in weights] + list(ready)
    count = RING if last else len(groups)

    def kernel(*refs):
        ins, refs = refs[: len(inputs)], refs[len(inputs) :]
        outs, scratch = refs[:count], refs[count:]
        place_ref, ins = (ins[0], ins[1:]) if last else (None, ins)
        weight_refs, ready_refs = ins[len(terms) :][: len(weights)], ins[len(terms) + len(weights) :]
        total = scratch[0]
        step = pl.program_id(0)
        at = 0
        for p, group in enumerate(groups):
            value = None
            for _, own_weights in group:
                pair = 2 * order.index(id(own_weights))
                for i in range(2):
                    term = lax.dot_general(
                        ins[at][i], weight_refs[pair + i][...], LAST, preferred_element_type=F32
                    )
                    value = term if value is None else value + term
                at += 1

            @pl.when(step == 0)
            def _():
                total[p] = value

            @pl.when((step > 0) & (step < steps - 1))
            def _():
                total[p] += value

            @pl.when(step == steps - 1)
            def _():
                result = total[p] + value
                if not last:
                    outs[p][...] = result.astype(outs[p].dtype)
                    return
                held = scratch[1]
                x, y, z, core = (place_ref[i] for i in range(4))
                held[2] = (result + ready_refs[0][...]).astype(BF16).reshape(RING, half, model)
                for k, ref in zip((0, 1, 3), ready_refs[1:]):
                    held[k] = ref[...].reshape(RING, half, model)
                for distance in range(RING):
                    at_x = lax.rem(z + distance - x + RING, RING)
                    for j in range(2):
                        for low in range(2):
                            at_y = lax.rem(2 * lax.rem(core + j, 2) + low - y + RING, RING)
                            second = jnp.where(core == 0, at_y, at_x)
                            first = jnp.where(core == 0, at_x, at_y)
                            outs[distance][j, low] = held[second, first]

    scratch = [pltpu.VMEM((len(groups), rows, model), F32)]
    block = pl.BlockSpec((rows, model), lambda j: (0, 0))
    if last:
        scratch.append(pltpu.VMEM((RING, RING, half, model), BF16))
        out_specs = [pl.BlockSpec((2, 2, half, model), lambda j: (0, 0, 0, 0))] * RING
        out_shape = [jax.ShapeDtypeStruct((2, 2, half, model), BF16)] * RING
    else:
        out_specs = [block] * count
        out_shape = [jax.ShapeDtypeStruct((rows, model), BF16 if whole else F32)] * count
    return pl.pallas_call(
        kernel,
        grid=(steps,),
        in_specs=([pl.BlockSpec(memory_space=pltpu.SMEM)] if last else [])
        + [pl.BlockSpec((2, rows, tile), lambda j: (0, 0, j))] * len(terms)
        + [
            pl.BlockSpec((model, tile), lambda j: (0, j))
            if at is None
            else pl.BlockSpec((None, model, tile), lambda j, at=at: (at, 0, j))
            for _, at in weights
        ]
        + [block] * len(ready),
        out_specs=out_specs,
        out_shape=out_shape,
        scratch_shapes=scratch,
        compiler_params=params(16),
        cost_estimate=light(),
        name="input_products",
    )(*inputs)


def on_device(layer_input, gate_pre, up_pre, grad_out, w_gate, w_up, w_down):
    x, y, z, core = (lax.axis_index(name) for name in ("x", "y", "z", "c"))
    place = jnp.stack([x, y, z, core]).astype(jnp.int32)
    rows, width = gate_pre.shape
    half, model = rows // 2, w_down.shape[1]

    def half_of_tokens(value, shape):
        halves = value.reshape(shape)
        return jnp.stack([pick(halves, core, 1), swap(pick(halves, 1 - core, 1))])

    gate_val, up_val = gate_pre.astype(F32), up_pre.astype(F32)
    hidden = (gate_val * jax.nn.sigmoid(gate_val) * up_val).astype(BF16)
    both = jnp.concatenate([tie(grad_out, hidden), layer_input], 1)
    both = lax.all_gather(both, ("z", "c"), axis=0, tiled=True)
    hid_own, hid_other = first_gather(half_of_tokens(hidden, (1, 2, half, width)))
    w_down_other = swap(w_down)
    hid_own, hid_other, w_down_other = lax.optimization_barrier((hid_own, hid_other, w_down_other))
    hid_own_after, hid_other_before = mix(hid_own, 2, -1), mix(hid_other, 2, 1)
    hid_own_before, hid_other_after = mix(hid_own, 2, 1), mix(hid_other, 2, -1)

    tokens, tokens_theirs = travel_order(place, both, 0)
    pre = half_of_tokens(jnp.stack([gate_pre, up_pre]), (2, 2, half, width))

    def hidden_across():
        return mix(hid_other_before, 2, 1), mix(hid_own_after, 2, -1)

    def hidden_swap(sums, other_across, own_across):
        pieces = [hid_other, hid_other_after, other_across, hid_other_before]
        return (swap(tie(jnp.concatenate(pieces), sums)),)

    grad_hidden, (_, hid_own_across), (hid_theirs,) = scatter_sum(
        tokens,
        w_down,
        w_down_other,
        (hid_own_after, hid_other_before, hid_own_before, hid_other_after, pre),
        hidden_across,
        hidden_swap,
    )

    gate_val, up_val = pre[:, 0].astype(F32), pre[:, 1].astype(F32)
    sigmoid_val = jax.nn.sigmoid(gate_val)
    gate_grad = grad_hidden * up_val * sigmoid_val * (1.0 + gate_val * (1.0 - sigmoid_val))
    up_grad = grad_hidden * (gate_val * sigmoid_val)
    own, other = first_gather(jnp.stack([gate_grad, up_grad], 1).astype(BF16))

    w_other = swap(tie(jnp.stack([w_gate, w_up]), grad_hidden))
    own, other, w_other = lax.optimization_barrier((own, other, w_other))
    own_after, other_before = mix(own, 2, -1), mix(other, 2, 1)

    (grad_down,) = weight_grads(
        (tokens, tokens_theirs),
        [hid_own, hid_own_after, hid_own_across, hid_own_before],
        hid_theirs,
        flip=True,
    )
    (input_left,) = travel_order(place, tie(both, own), 1, flip=True)
    theirs = [swap(other)]
    own_before, other_after = mix(own, 2, 1), mix(other, 2, -1)
    own_after, other_before, *_ = lax.optimization_barrier(
        (own_after, other_before, input_left, grad_down, theirs[0])
    )
    other_across, own_across = mix(other_before, 2, 1), mix(own_after, 2, -1)

    here, there = ((w_gate, None), (w_up, None)), ((w_other, 0), (w_other, 1))
    ready = input_products(
        [
            [(own, here), (other, there)],
            [(own_after, here), (other_after, there)],
            [(own_before, here), (other_before, there)],
        ]
    )
    other_across, *ready, theirs_before = lax.optimization_barrier(
        (other_across, *ready, swap(other_before))
    )
    theirs += [swap(other_after), swap(other_across), theirs_before]
    (first,) = input_products([[(other_across, there)]], whole=False)
    parts = input_products([[(own_across, here)]], [first, *ready], place)
    grad_gate, grad_up = weight_grads(
        (input_left,),
        [own, own_after, own_across, own_before],
        theirs,
    )
    received = [along_z(parts[k], step) for k, step in ((2, 2), (1, 1), (3, -1))]
    total = tie(parts[0], grad_gate, grad_up).astype(F32)
    for part in received:
        total = total + part.astype(F32)
    total = total.astype(BF16)
    keep, got = total[0], swap(total[1])
    grad_input = jnp.where(
        core == 0, jnp.stack([keep, got], 1), jnp.stack([got, keep], 1)
    ).reshape(4 * half, model)

    return grad_input, grad_gate, grad_up, grad_down


def solution(mesh):
    chips = Mesh(mesh.devices.reshape(RING, RING, RING, 2), ("x", "y", "z", "c"))
    row, col = ("x", "y"), ("z", "c")
    in_specs = (
        P(col, row),
        P(row, col),
        P(row, col),
        P(col, row),
        P(row, col),
        P(row, col),
        P(col, row),
    )
    out_specs = (P(col, row), P(row, col), P(row, col), P(col, row))
    return jax.shard_map(
        on_device, mesh=chips, in_specs=in_specs, out_specs=out_specs, check_vma=False
    )
```

time: 258 us -> 245 us (0.950)
  starting transfers between devices: 62.7 us -> 47.7 us
  other arithmetic: 5.12 us -> 8.74 us
    ppermute x15 -> x10, starting transfers between devices: 24.6 us -> 8.9 us  [swap(): return lax.ppermute(value, 'c', [(0, 1), (1, 0)])]
    all_gather x1, waiting for transfers between devices: 0.01 us -> 10.2 us  [on_device(): both = lax.all_gather(both, ('z', 'c'), axis=0, tiled=True)]
    ppermute x27 -> x25, waiting for transfers between devices: 118 us -> 108 us  [mix(): return lax.ppermute(value, ('x', 'y', 'c'), pairs)]
    pallas_call x2 -> x3, Pallas kernels: 17.9 us -> 16.9 us  [input_products(): pl.pallas_call(kernel, grid=(steps,), in_specs=([pl.BlockSpec(memory_spac...]
    ppermute x27 -> x25, starting transfers between devices: 33 us -> 32.1 us  [mix(): return lax.ppermute(value, ('x', 'y', 'c'), pairs)]
  transfers between devices with their start and end apart: 46 -> 39, of which waited for: 25 -> 20; matrix products, arithmetic and copies ran while one was open for 2% -> 2% of each run, Pallas kernels for 17% -> 18%
where the time goes in v2:
time: 245 us
  waiting for transfers between devices  122 us (50%)
  starting transfers between devices  47.7 us (19%)
  Pallas kernels  46.3 us (19%)
  between operations  14.4 us (6%)
  other arithmetic  8.74 us (4%)
  local copies, waits for them, and re-layouts  5.51 us (2%)
    ppermute x25, waiting for transfers between devices, mix(): return lax.ppermute(value, ('x', 'y', 'c'), pairs)  108 us
    ppermute x25, starting transfers between devices, mix(): return lax.ppermute(value, ('x', 'y', 'c'), pairs)  32.1 us
    pallas_call x2, Pallas kernels, weight_grads(): pl.pallas_call(kernel, grid=(width // tile,), in_specs=[pl.BlockSpec(a.sh...  20.2 us
    pallas_call x3, Pallas kernels, input_products(): pl.pallas_call(kernel, grid=(steps,), in_specs=([pl.BlockSpec(memory_spac...  16.9 us
    all_gather x1, waiting for transfers between devices, on_device(): both = lax.all_gather(both, ('z', 'c'), axis=0, tiled=True)  10.2 us
    ppermute x10, starting transfers between devices, swap(): return lax.ppermute(value, 'c', [(0, 1), (1, 0)])  8.9 us
    pallas_call x4, Pallas kernels, down_products(): pl.pallas_call(kernel, grid=(2,), in_specs=in_specs, out_specs=[pl.BlockS...  7.35 us
    ppermute x3, starting transfers between devices, along_z(): lax.ppermute(value, 'z', [(z, (z + step) % RING) for z in range(RING)])  6.58 us
  transfers between devices with their start and end apart: 39, of which 20 were waited for; matrix products, arithmetic and copies ran while one was open for 2% of the time, Pallas kernels for 18%

profile of v2, /device:TPU:1, one launch (start us, length us, event | category | flops | bytes accessed | tf_op | source)
XLA Modules:
  0.0 244.9 jit_solution(2124401290427561366)
XLA Ops:
  15.4 2.9 %collective-permute-start.2 = (bf16[2,1,64,1792]{3,2,1,0:T(8,128)(2,1)S(1)}, bf16[2,1,64,1792]{3,2,1,0:T(8,128)(2,1)S(1)}, u32[]{:S(2)}, u32[]{:S(2)}) collective-permute-start(bf16[2,1,64,1792]{3,2,1,0:T(8,128)(2,1)S(1)} %pad_maximum_fusion.9), channel_id=1, source_target_pairs={{0,64},{1,17},{8,72},{9,25},{16,80},{17,1},{24,88},{25,9},{32,96},... | collective-permute-start | bytes 1376264 | tf_op jit(solution)/shard_map/ppermute | solution.py:26
  19.1 3.3 %collective-permute-done.3 = bf16[2,1,64,1792]{3,2,1,0:T(8,128)(2,1)S(1)} collective-permute-done((bf16[2,1,64,1792]{3,2,1,0:T(8,128)(2,1)S(1)}, bf16[2,1,64,1792]{3,2,1,0:T(8,128)(2,1)S(1)}, u32[]{:S(2)}, u32[]{:S(2)}) %collective-permute-start.3) | collective-permute-done | bytes 458784 | tf_op jit(solution)/shard_map/ppermute | solution.py:26
  22.5 6.1 %collective-permute-done.2 = bf16[2,1,64,1792]{3,2,1,0:T(8,128)(2,1)S(1)} collective-permute-done((bf16[2,1,64,1792]{3,2,1,0:T(8,128)(2,1)S(1)}, bf16[2,1,64,1792]{3,2,1,0:T(8,128)(2,1)S(1)}, u32[]{:S(2)}, u32[]{:S(2)}) %collective-permute-start.2) | collective-permute-done | bytes 458784 | tf_op jit(solution)/shard_map/ppermute | solution.py:26
  36.6 10.2 %all-gather.2.cloned.1.call-done = bf16[2048,1024]{1,0:T(8,128)(2,1)} async-done(((bf16[256,1024]{1,0:T(8,128)(2,1)}), bf16[2048,1024]{1,0:T(8,128)(2,1)}) %all-gather.2.cloned.1.call-update) | async-done | bytes 4194320 | tf_op jit(solution)/shard_map/all_gather | solution.py:315
  53.9 3.9 %collective-permute-done.9.refs_5_ = bf16[1,256,1792]{2,1,0:T(8,128)(2,1)} collective-permute-done((bf16[1,256,1792]{2,1,0:T(8,128)(2,1)S(1)}, bf16[1,256,1792]{2,1,0:T(8,128)(2,1)}, u32[]{:S(2)}, u32[]{:S(2)}) %collective-permute-start.9) | collective-permute-done | bytes 917536 | tf_op jit(solution)/shard_map/ppermute | solution.py:26
  57.8 2.7 %collective-permute-start.13 = (bf16[2,256,1792]{2,1,0:T(8,128)(2,1)S(1)}, bf16[2,256,1792]{2,1,0:T(8,128)(2,1)S(1)}, u32[]{:S(2)}, u32[]{:S(2)}) collective-permute-start(bf16[2,256,1792]{2,1,0:T(8,128)(2,1)S(1)} %down_products.5), channel_id=1, source_target_pairs={{0,24},{1,97},{8,0},{9,105},{16,8},{17,113},{24,16},{25,121},{32,5... | collective-permute-start | bytes 5505032 | tf_op jit(solution)/shard_map/ppermute | solution.py:26
  60.4 2.7 %collective-permute-start.8 = (bf16[1,256,1792]{2,1,0:T(8,128)(2,1)}, bf16[1,256,1792]{2,1,0:T(8,128)(2,1)S(1)}, u32[]{:S(2)}, u32[]{:S(2)}) collective-permute-start(bf16[1,256,1792]{2,1,0:T(8,128)(2,1)} %collective-permute-done.7.refs_3_), channel_id=1, source_target_pairs={{0,24},{1,97},{8,0},{9,105},{16,8},{17,113},{24,16},{25,121},{32,5... | collective-permute-start | bytes 2752520 | tf_op jit(solution)/shard_map/ppermute | solution.py:26
  63.1 18.2 %collective-permute-done.12.refs_2_.refs_6_ = bf16[2,256,1792]{2,1,0:T(8,128)(2,1)S(1)} collective-permute-done((bf16[2,256,1792]{2,1,0:T(8,128)(2,1)S(1)}, bf16[2,256,1792]{2,1,0:T(8,128)(2,1)S(1)}, u32[]{:S(2)}, u32[]{:S(2)}) %collective-permute-start.12) | collective-permute-done | bytes 1835040 | tf_op jit(solution)/shard_map/ppermute | solution.py:26
  83.3 2.7 %collective-permute-start.15 = (bf16[1,256,1792]{2,1,0:T(8,128)(2,1)S(1)}, bf16[1,256,1792]{2,1,0:T(8,128)(2,1)S(1)}, u32[]{:S(2)}, u32[]{:S(2)}) collective-permute-start(bf16[1,256,1792]{2,1,0:T(8,128)(2,1)S(1)} %get-tuple-element.48), channel_id=1, source_target_pairs={{0,24},{1,97},{8,0},{9,105},{16,8},{17,113},{24,16},{25,121},{32,5... | collective-permute-start | bytes 2752520 | tf_op jit(solution)/shard_map/ppermute | solution.py:26
  86.1 5.1 %collective-permute-done.6 = bf16[1,256,1792]{2,1,0:T(8,128)(2,1)S(1)} collective-permute-done((bf16[1,256,1792]{2,1,0:T(8,128)(2,1)}, bf16[1,256,1792]{2,1,0:T(8,128)(2,1)S(1)}, u32[]{:S(2)}, u32[]{:S(2)}) %collective-permute-start.6) | collective-permute-done | bytes 917536 | tf_op jit(solution)/shard_map/ppermute | solution.py:26
  93.2 7.8 %collective-permute-done.14.refs_2_ = bf16[1,256,1792]{2,1,0:T(8,128)(2,1)S(1)} collective-permute-done((bf16[1,256,1792]{2,1,0:T(8,128)(2,1)S(1)}, bf16[1,256,1792]{2,1,0:T(8,128)(2,1)S(1)}, u32[]{:S(2)}, u32[]{:S(2)}) %collective-permute-start.14) | collective-permute-done | bytes 917536 | tf_op jit(solution)/shard_map/ppermute | solution.py:26
  103.1 2.9 %collective-permute-start.16 = (bf16[4,256,1792]{2,1,0:T(8,128)(2,1)S(1)}, bf16[4,256,1792]{2,1,0:T(8,128)(2,1)S(1)}, u32[]{:S(2)}, u32[]{:S(2)}) collective-permute-start(bf16[4,256,1792]{2,1,0:T(8,128)(2,1)S(1)} %pad_maximum_fusion), channel_id=1, source_target_pairs={{0,1},{1,0},{2,3},{3,2},{4,5},{5,4},{6,7},{7,6},{8,9},{9,8},{10,11... | collective-permute-start | bytes 11010056 | tf_op jit(solution)/shard_map/ppermute | solution.py:34
  106.5 4.1 %collective-permute-start.17 = (bf16[2,64,1792]{2,1,0:T(8,128)(2,1)S(1)}, bf16[2,64,1792]{2,1,0:T(8,128)(2,1)S(1)}, u32[]{:S(2)}, u32[]{:S(2)}) collective-permute-start(bf16[2,64,1792]{2,1,0:T(8,128)(2,1)S(1)} %get-tuple-element.78), channel_id=1, source_target_pairs={{0,64},{1,17},{8,72},{9,25},{16,80},{17,1},{24,88},{25,9},{32,96},... | collective-permute-start | bytes 1376264 | tf_op jit(solution)/shard_map/ppermute | solution.py:26
  112.8 2.9 %collective-permute-done.18 = bf16[2,64,1792]{2,1,0:T(8,128)(2,1)S(1)} collective-permute-done((bf16[2,64,1792]{2,1,0:T(8,128)(2,1)S(1)}, bf16[2,64,1792]{2,1,0:T(8,128)(2,1)S(1)}, u32[]{:S(2)}, u32[]{:S(2)}) %collective-permute-start.18) | collective-permute-done | bytes 458784 | tf_op jit(solution)/shard_map/ppermute | solution.py:26
  115.7 6.1 %collective-permute-done.17 = bf16[2,64,1792]{2,1,0:T(8,128)(2,1)S(1)} collective-permute-done((bf16[2,64,1792]{2,1,0:T(8,128)(2,1)S(1)}, bf16[2,64,1792]{2,1,0:T(8,128)(2,1)S(1)}, u32[]{:S(2)}, u32[]{:S(2)}) %collective-permute-start.17) | collective-permute-done | bytes 458784 | tf_op jit(solution)/shard_map/ppermute | solution.py:26
  127.2 10.5 %collective-permute-done.21 = bf16[2,2,64,1792]{3,2,1,0:T(8,128)(2,1)S(1)} collective-permute-done((bf16[2,2,64,1792]{3,2,1,0:T(8,128)(2,1)S(1)}, bf16[2,2,64,1792]{3,2,1,0:T(8,128)(2,1)S(1)}, u32[]{:S(2)}, u32[]{:S(2)}) %collective-permute-start.21) | collective-permute-done | bytes 917536 | tf_op jit(solution)/shard_map/ppermute | solution.py:26
  137.8 10.2 %collective-permute-done.20 = bf16[2,2,64,1792]{3,2,1,0:T(8,128)(2,1)S(1)} collective-permute-done((bf16[2,2,64,1792]{3,2,1,0:T(8,128)(2,1)S(1)}, bf16[2,2,64,1792]{3,2,1,0:T(8,128)(2,1)S(1)}, u32[]{:S(2)}, u32[]{:S(2)}) %collective-permute-start.20) | collective-permute-done | bytes 917536 | tf_op jit(solution)/shard_map/ppermute | solution.py:26
  151.9 9.3 %weight_grads.2 = f32[1792,512]{1,0:T(8,128)} custom-call(bf16[4,256,512]{2,1,0:T(8,128)(2,1)S(1)} %get-tuple-element.43.refs_0_.refs_2_.refs_3_.refs_4_, bf16[4,256,512]{2,1,0:T(8,128)(2,1)S(1)} %get-tuple-element.55.refs_1_, bf16[1,256,1792]{2,1,0:T(8,128)(2,1)S(1)} %bitcast.103, bf16[1,256,1792]{2,1,0:T(8,128)(2,1)} %collective-permute-done.7.refs_3_, ...), custom_call_target="tpu_custom_call" | custom-call | flops 1 | bytes 1 | tf_op jit(solution)/shard_map/weight_grads/pallas_call | solution.py:196
  163.8 9.0 %collective-permute-done.25.refs_5_ = bf16[2,256,1792]{2,1,0:T(8,128)(2,1)S(1)} collective-permute-done((bf16[2,256,1792]{2,1,0:T(8,128)(2,1)S(1)}, bf16[2,256,1792]{2,1,0:T(8,128)(2,1)S(1)}, u32[]{:S(2)}, u32[]{:S(2)}) %collective-permute-start.25) | collective-permute-done | bytes 1835040 | tf_op jit(solution)/shard_map/ppermute | solution.py:26
  176.4 16.5 %collective-permute-done.29.refs_3_ = bf16[2,256,1792]{2,1,0:T(8,128)(2,1)S(1)} collective-permute-done((bf16[2,256,1792]{2,1,0:T(8,128)(2,1)S(1)}, bf16[2,256,1792]{2,1,0:T(8,128)(2,1)S(1)}, u32[]{:S(2)}, u32[]{:S(2)}) %collective-permute-start.29) | collective-permute-done | bytes 1835040 | tf_op jit(solution)/shard_map/ppermute | solution.py:26
  193.0 12.2 %input_products.3 = (bf16[256,512]{1,0:T(8,128)(2,1)S(1)}, bf16[256,512]{1,0:T(8,128)(2,1)S(1)}, bf16[256,512]{1,0:T(8,128)(2,1)S(1)}) custom-call(bf16[2,256,1792]{2,1,0:T(8,128)(2,1)S(1)} %bitcast.94, bf16[2,256,1792]{2,1,0:T(8,128)(2,1)S(1)} %bitcast.100, bf16[2,256,1792]{2,1,0:T(8,128)(2,1)S(1)} %collective-permute-done.24.refs_2_, ...), custom_call_target="tpu_custom_call" | custom-call | flops 1 | bytes 1 | tf_op jit(solution)/shard_map/input_products/pallas_call | solution.py:281
  205.3 6.8 %collective-permute-done.28.refs_0_ = bf16[2,256,1792]{2,1,0:T(8,128)(2,1)S(1)} collective-permute-done((bf16[2,256,1792]{2,1,0:T(8,128)(2,1)S(1)}, bf16[2,256,1792]{2,1,0:T(8,128)(2,1)S(1)}, u32[]{:S(2)}, u32[]{:S(2)}) %collective-permute-start.28) | collective-permute-done | bytes 1835040 | tf_op jit(solution)/shard_map/ppermute | solution.py:26
  217.7 3.9 %collective-permute-start.34 = (bf16[2,2,64,512]{3,2,1,0:T(8,128)(2,1)S(1)}, bf16[2,2,64,512]{3,2,1,0:T(8,128)(2,1)S(1)}, u32[]{:S(2)}, u32[]{:S(2)}) collective-permute-start(bf16[2,2,64,512]{3,2,1,0:T(8,128)(2,1)S(1)} %get-tuple-element.71), channel_id=1, source_target_pairs={{0,4},{2,6},{4,0},{6,2},{1,5},{3,7},{5,1},{7,3},{8,12},{10,14},{12... | collective-permute-start | bytes 786440 | tf_op jit(solution)/shard_map/ppermute | solution.py:30
  224.3 10.9 %weight_grads.3 = (f32[512,1792]{1,0:T(8,128)}, f32[512,1792]{1,0:T(8,128)}) custom-call(bf16[512,2048]{1,0:T(8,128)(2,1)S(1)} %travel_order.3.refs_0_, bf16[2,256,1792]{2,1,0:T(8,128)(2,1)S(1)} %bitcast.95, bf16[2,256,1792]{2,1,0:T(8,128)(2,1)S(1)} %collective-permute-done.24.refs_2_, bf16[2,256,1792]{2,1,0:T(8,128)(2,1)S(1)} %collective-permute-done.27.refs_1_.refs_3_, ...), custom_call_target="tpu_custom_call" | custom-call | flops 1 | bytes 1 | tf_op jit(solution)/shard_map/weight_grads/pallas_call | solution.py:196
  (111 shorter events, 59.6 us)
Async XLA Ops:
  7.2 39.6 %all-gather.2.cloned.1.call-start = ((), (), s32[]{:S(2)}) async-start(), calls=%async_computation | async-start | bytes 4718592 | tf_op jit(solution)/shard_map/all_gather | solution.py:315
  14.9 16.3 %collective-permute-start.4 = (bf16[1792,512]{1,0:T(8,128)(2,1)S(1)}, bf16[1792,512]{1,0:T(8,128)(2,1)S(1)}, u32[]{:S(2)}, u32[]{:S(2)}) collective-permute-start(bf16[1792,512]{1,0:T(8,128)(2,1)S(1)} %copy-done), channel_id=1, source_target_pairs={{0,1},{1,0},{2,3},{3,2},{4,5},{5,4},{6,7},{7,6},{8,9},{9,8},{10,11... | collective-permute-start | bytes 5505032 | tf_op jit(solution)/shard_map/ppermute | solution.py:34
  32.4 21.5 %collective-permute-start.10 = (bf16[1,256,1792]{2,1,0:T(8,128)(2,1)}, bf16[1,256,1792]{2,1,0:T(8,128)(2,1)}, u32[]{:S(2)}, u32[]{:S(2)}) collective-permute-start(bf16[1,256,1792]{2,1,0:T(8,128)(2,1)} %bitcast.9), channel_id=1, source_target_pairs={{0,24},{1,97},{8,0},{9,105},{16,8},{17,113},{24,16},{25,121},{32,5... | collective-permute-start | bytes 2752520 | tf_op jit(solution)/shard_map/ppermute | solution.py:26
  33.9 20.0 %collective-permute-start.5 = (bf16[1,256,1792]{2,1,0:T(8,128)(2,1)}, bf16[1,256,1792]{2,1,0:T(8,128)(2,1)}, u32[]{:S(2)}, u32[]{:S(2)}) collective-permute-start(bf16[1,256,1792]{2,1,0:T(8,128)(2,1)} %bitcast.9), channel_id=1, source_target_pairs={{0,8},{1,33},{8,16},{9,41},{16,24},{17,49},{24,0},{25,57},{32,40},... | collective-permute-start | bytes 2752520 | tf_op jit(solution)/shard_map/ppermute | solution.py:26
  33.9 23.9 %collective-permute-start.9 = (bf16[1,256,1792]{2,1,0:T(8,128)(2,1)S(1)}, bf16[1,256,1792]{2,1,0:T(8,128)(2,1)}, u32[]{:S(2)}, u32[]{:S(2)}) collective-permute-start(bf16[1,256,1792]{2,1,0:T(8,128)(2,1)S(1)} %bitcast.101), channel_id=1, source_target_pairs={{0,8},{1,33},{8,16},{9,41},{16,24},{17,49},{24,0},{25,57},{32,40},... | collective-permute-start | bytes 2752520 | tf_op jit(solution)/shard_map/ppermute | solution.py:26
  35.1 22.7 %collective-permute-start.7 = (bf16[1,256,1792]{2,1,0:T(8,128)(2,1)S(1)}, bf16[1,256,1792]{2,1,0:T(8,128)(2,1)}, u32[]{:S(2)}, u32[]{:S(2)}) collective-permute-start(bf16[1,256,1792]{2,1,0:T(8,128)(2,1)S(1)} %bitcast.102), channel_id=1, source_target_pairs={{0,24},{1,97},{8,0},{9,105},{16,8},{17,113},{24,16},{25,121},{32,5... | collective-permute-start | bytes 2752520 | tf_op jit(solution)/shard_map/ppermute | solution.py:26
  57.8 23.6 %collective-permute-start.12 = (bf16[2,256,1792]{2,1,0:T(8,128)(2,1)S(1)}, bf16[2,256,1792]{2,1,0:T(8,128)(2,1)S(1)}, u32[]{:S(2)}, u32[]{:S(2)}) collective-permute-start(bf16[2,256,1792]{2,1,0:T(8,128)(2,1)S(1)} %down_products.4), channel_id=1, source_target_pairs={{0,8},{1,33},{8,16},{9,41},{16,24},{17,49},{24,0},{25,57},{32,40},... | collective-permute-start | bytes 5505032 | tf_op jit(solution)/shard_map/ppermute | solution.py:26
  57.8 23.6 %collective-permute-start.13 = (bf16[2,256,1792]{2,1,0:T(8,128)(2,1)S(1)}, bf16[2,256,1792]{2,1,0:T(8,128)(2,1)S(1)}, u32[]{:S(2)}, u32[]{:S(2)}) collective-permute-start(bf16[2,256,1792]{2,1,0:T(8,128)(2,1)S(1)} %down_products.5), channel_id=1, source_target_pairs={{0,24},{1,97},{8,0},{9,105},{16,8},{17,113},{24,16},{25,121},{32,5... | collective-permute-start | bytes 5505032 | tf_op jit(solution)/shard_map/ppermute | solution.py:26
  60.4 30.7 %collective-permute-start.6 = (bf16[1,256,1792]{2,1,0:T(8,128)(2,1)}, bf16[1,256,1792]{2,1,0:T(8,128)(2,1)S(1)}, u32[]{:S(2)}, u32[]{:S(2)}) collective-permute-start(bf16[1,256,1792]{2,1,0:T(8,128)(2,1)} %collective-permute-done.5), channel_id=1, source_target_pairs={{0,8},{1,33},{8,16},{9,41},{16,24},{17,49},{24,0},{25,57},{32,40},... | collective-permute-start | bytes 2752520 | tf_op jit(solution)/shard_map/ppermute | solution.py:26
  60.4 32.7 %collective-permute-start.8 = (bf16[1,256,1792]{2,1,0:T(8,128)(2,1)}, bf16[1,256,1792]{2,1,0:T(8,128)(2,1)S(1)}, u32[]{:S(2)}, u32[]{:S(2)}) collective-permute-start(bf16[1,256,1792]{2,1,0:T(8,128)(2,1)} %collective-permute-done.7.refs_3_), channel_id=1, source_target_pairs={{0,24},{1,97},{8,0},{9,105},{16,8},{17,113},{24,16},{25,121},{32,5... | collective-permute-start | bytes 2752520 | tf_op jit(solution)/shard_map/ppermute | solution.py:26
  83.2 17.8 %collective-permute-start.14 = (bf16[1,256,1792]{2,1,0:T(8,128)(2,1)S(1)}, bf16[1,256,1792]{2,1,0:T(8,128)(2,1)S(1)}, u32[]{:S(2)}, u32[]{:S(2)}) collective-permute-start(bf16[1,256,1792]{2,1,0:T(8,128)(2,1)S(1)} %get-tuple-element.47), channel_id=1, source_target_pairs={{0,8},{1,33},{8,16},{9,41},{16,24},{17,49},{24,0},{25,57},{32,40},... | collective-permute-start | bytes 2752520 | tf_op jit(solution)/shard_map/ppermute | solution.py:26
  83.3 17.7 %collective-permute-start.15 = (bf16[1,256,1792]{2,1,0:T(8,128)(2,1)S(1)}, bf16[1,256,1792]{2,1,0:T(8,128)(2,1)S(1)}, u32[]{:S(2)}, u32[]{:S(2)}) collective-permute-start(bf16[1,256,1792]{2,1,0:T(8,128)(2,1)S(1)} %get-tuple-element.48), channel_id=1, source_target_pairs={{0,24},{1,97},{8,0},{9,105},{16,8},{17,113},{24,16},{25,121},{32,5... | collective-permute-start | bytes 2752520 | tf_op jit(solution)/shard_map/ppermute | solution.py:26
  122.3 26.4 %collective-permute-start.23 = (bf16[2,512,1792]{2,1,0:T(8,128)(2,1)S(1)}, bf16[2,512,1792]{2,1,0:T(8,128)(2,1)S(1)}, u32[]{:S(2)}, u32[]{:S(2)}) collective-permute-start(bf16[2,512,1792]{2,1,0:T(8,128)(2,1)S(1)} %pad_maximum_fusion.1), channel_id=1, source_target_pairs={{0,1},{1,0},{2,3},{3,2},{4,5},{5,4},{6,7},{7,6},{8,9},{9,8},{10,11... | collective-permute-start | bytes 11010056 | tf_op jit(solution)/shard_map/ppermute | solution.py:34
  124.8 23.2 %collective-permute-start.20 = (bf16[2,2,64,1792]{3,2,1,0:T(8,128)(2,1)S(1)}, bf16[2,2,64,1792]{3,2,1,0:T(8,128)(2,1)S(1)}, u32[]{:S(2)}, u32[]{:S(2)}) collective-permute-start(bf16[2,2,64,1792]{3,2,1,0:T(8,128)(2,1)S(1)} %pad_maximum_fusion.5), channel_id=1, source_target_pairs={{0,96},{1,25},{8,104},{9,1},{16,112},{17,9},{24,120},{25,17},{32,0... | collective-permute-start | bytes 2752520 | tf_op jit(solution)/shard_map/ppermute | solution.py:26
  126.7 21.4 %collective-permute-start.22 = (bf16[2,2,64,1792]{3,2,1,0:T(8,128)(2,1)S(1)}, bf16[2,2,64,1792]{3,2,1,0:T(8,128)(2,1)S(1)}, u32[]{:S(2)}, u32[]{:S(2)}) collective-permute-start(bf16[2,2,64,1792]{3,2,1,0:T(8,128)(2,1)S(1)} %pad_maximum_fusion.5), channel_id=1, source_target_pairs={{0,32},{1,9},{8,40},{9,17},{16,48},{17,25},{24,56},{25,1},{32,64},... | collective-permute-start | bytes 2752520 | tf_op jit(solution)/shard_map/ppermute | solution.py:26
  149.2 23.6 %collective-permute-start.25 = (bf16[2,256,1792]{2,1,0:T(8,128)(2,1)S(1)}, bf16[2,256,1792]{2,1,0:T(8,128)(2,1)S(1)}, u32[]{:S(2)}, u32[]{:S(2)}) collective-permute-start(bf16[2,256,1792]{2,1,0:T(8,128)(2,1)S(1)} %bitcast.98), channel_id=1, source_target_pairs={{0,8},{1,33},{8,16},{9,41},{16,24},{17,49},{24,0},{25,57},{32,40},... | collective-permute-start | bytes 5505032 | tf_op jit(solution)/shard_map/ppermute | solution.py:26
  150.9 22.4 %collective-permute-start.24 = (bf16[2,256,1792]{2,1,0:T(8,128)(2,1)S(1)}, bf16[2,256,1792]{2,1,0:T(8,128)(2,1)S(1)}, u32[]{:S(2)}, u32[]{:S(2)}) collective-permute-start(bf16[2,256,1792]{2,1,0:T(8,128)(2,1)S(1)} %bitcast.92), channel_id=1, source_target_pairs={{0,24},{1,97},{8,0},{9,105},{16,8},{17,113},{24,16},{25,121},{32,5... | collective-permute-start | bytes 5505032 | tf_op jit(solution)/shard_map/ppermute | solution.py:26
  161.1 31.8 %collective-permute-start.29 = (bf16[2,256,1792]{2,1,0:T(8,128)(2,1)S(1)}, bf16[2,256,1792]{2,1,0:T(8,128)(2,1)S(1)}, u32[]{:S(2)}, u32[]{:S(2)}) collective-permute-start(bf16[2,256,1792]{2,1,0:T(8,128)(2,1)S(1)} %bitcast.99), channel_id=1, source_target_pairs={{0,24},{1,97},{8,0},{9,105},{16,8},{17,113},{24,16},{25,121},{32,5... | collective-permute-start | bytes 5505032 | tf_op jit(solution)/shard_map/ppermute | solution.py:26
  162.3 30.7 %collective-permute-start.30 = (bf16[2,256,1792]{2,1,0:T(8,128)(2,1)S(1)}, bf16[2,256,1792]{2,1,0:T(8,128)(2,1)S(1)}, u32[]{:S(2)}, u32[]{:S(2)}) collective-permute-start(bf16[2,256,1792]{2,1,0:T(8,128)(2,1)S(1)} %bitcast.93), channel_id=1, source_target_pairs={{0,8},{1,33},{8,16},{9,41},{16,24},{17,49},{24,0},{25,57},{32,40},... | collective-permute-start | bytes 5505032 | tf_op jit(solution)/shard_map/ppermute | solution.py:26
  173.3 32.0 %collective-permute-start.31 = (bf16[2,256,1792]{2,1,0:T(8,128)(2,1)S(1)}, bf16[2,256,1792]{2,1,0:T(8,128)(2,1)S(1)}, u32[]{:S(2)}, u32[]{:S(2)}) collective-permute-start(bf16[2,256,1792]{2,1,0:T(8,128)(2,1)S(1)} %collective-permute-done.25.refs_5_), channel_id=1, source_target_pairs={{0,1},{1,0},{2,3},{3,2},{4,5},{5,4},{6,7},{7,6},{8,9},{9,8},{10,11... | collective-permute-start | bytes 5505032 | tf_op jit(solution)/shard_map/ppermute | solution.py:34
  173.7 38.3 %collective-permute-start.28 = (bf16[2,256,1792]{2,1,0:T(8,128)(2,1)S(1)}, bf16[2,256,1792]{2,1,0:T(8,128)(2,1)S(1)}, u32[]{:S(2)}, u32[]{:S(2)}) collective-permute-start(bf16[2,256,1792]{2,1,0:T(8,128)(2,1)S(1)} %collective-permute-done.25.refs_5_), channel_id=1, source_target_pairs={{0,8},{1,33},{8,16},{9,41},{16,24},{17,49},{24,0},{25,57},{32,40},... | collective-permute-start | bytes 5505032 | tf_op jit(solution)/shard_map/ppermute | solution.py:26
  175.4 39.7 %collective-permute-start.27 = (bf16[2,256,1792]{2,1,0:T(8,128)(2,1)S(1)}, bf16[2,256,1792]{2,1,0:T(8,128)(2,1)S(1)}, u32[]{:S(2)}, u32[]{:S(2)}) collective-permute-start(bf16[2,256,1792]{2,1,0:T(8,128)(2,1)S(1)} %collective-permute-done.24.refs_2_), channel_id=1, source_target_pairs={{0,24},{1,97},{8,0},{9,105},{16,8},{17,113},{24,16},{25,121},{32,5... | collective-permute-start | bytes 5505032 | tf_op jit(solution)/shard_map/ppermute | solution.py:26
  192.9 31.4 %collective-permute-start.32 = (bf16[2,256,1792]{2,1,0:T(8,128)(2,1)S(1)}, bf16[2,256,1792]{2,1,0:T(8,128)(2,1)S(1)}, u32[]{:S(2)}, u32[]{:S(2)}) collective-permute-start(bf16[2,256,1792]{2,1,0:T(8,128)(2,1)S(1)} %collective-permute-done.29.refs_3_), channel_id=1, source_target_pairs={{0,1},{1,0},{2,3},{3,2},{4,5},{5,4},{6,7},{7,6},{8,9},{9,8},{10,11... | collective-permute-start | bytes 5505032 | tf_op jit(solution)/shard_map/ppermute | solution.py:34
  217.7 17.5 %collective-permute-start.34 = (bf16[2,2,64,512]{3,2,1,0:T(8,128)(2,1)S(1)}, bf16[2,2,64,512]{3,2,1,0:T(8,128)(2,1)S(1)}, u32[]{:S(2)}, u32[]{:S(2)}) collective-permute-start(bf16[2,2,64,512]{3,2,1,0:T(8,128)(2,1)S(1)} %get-tuple-element.71), channel_id=1, source_target_pairs={{0,4},{2,6},{4,0},{6,2},{1,5},{3,7},{5,1},{7,3},{8,12},{10,14},{12... | collective-permute-start | bytes 786440 | tf_op jit(solution)/shard_map/ppermute | solution.py:30
  (24 other events, 214.2 us)
Sparse Core Ops, SparseCore 0:
  10.8 35.9 all-gather.1

commit v3 on v2

--- a/solution.py
+++ b/solution.py
@@ -50,52 +50,53 @@
     return pl.CostEstimate(flops=1, bytes_accessed=1, transcendentals=0)
 
 
-def travel_order(place, value, part, flip=False):
-    tokens, model = value.shape[0], value.shape[1] // 2
-    half = tokens // 32
-    value = value.reshape(RING, RING, 2, half, 2 * model)
-
-    def kernel(place_ref, value_ref, *results):
-        x, y, core = place_ref[0], place_ref[1], place_ref[3]
-        for i, owner in enumerate((core, 1 - core)):
-            for second in range(RING):
-                block = []
-                for first in range(RING):
-                    at_x = lax.rem(x + jnp.where(owner == 0, first, second), RING)
-                    at_y = lax.rem(y + jnp.where(owner == 0, second, first), RING)
-                    block.append(value_ref[at_x, at_y, owner])
-                block = jnp.concatenate(block, 0)
-                if flip:
-                    at = (i * RING + second) * RING * half
-                    results[0][:, at : at + RING * half] = block.T
-                else:
-                    results[i][second] = block
-
-    shape, count = ((model, tokens), 1) if flip else ((RING, RING * half, model), 2)
-    return pl.pallas_call(
+def travel_order(place, own, other, flip=False):
+    _, rows, model = own.shape
+    half = rows // 4
+    own, other = (value.reshape(RING, 2, 2, half, model) for value in (own, other))
+
+    def kernel(place_ref, own_ref, other_ref, result, *held):
+        x, y, z, core = (place_ref[i] for i in range(4))
+        target = held[0] if flip else result
+        for side, ref in enumerate((own_ref, other_ref)):
+            for step in range(RING):
+                at_x = lax.rem(z + step - x + RING, RING)
+                for low in range(2):
+                    at_y = lax.rem(2 * lax.rem(core + side, 2) + low - y + RING, RING)
+                    for owner in range(2):
+                        second, first = (at_y, at_x) if owner == 0 else (at_x, at_y)
+                        target[lax.rem(core + owner, 2), second, first] = ref[step, low, owner]
+        if flip:
+            for i in range(2 * RING):
+                block = target[i // RING, i % RING].reshape(RING * half, model)
+                result[:, i * RING * half : (i + 1) * RING * half] = block.T
+
+    order = (2, RING, RING, half, model)
+    shape = (model, 2 * RING * RING * half) if flip else order
+    block = pl.BlockSpec((RING, 2, 2, half, model), lambda j: (0,) * 5)
+    result = pl.pallas_call(
         kernel,
         grid=(1,),
-        in_specs=[
-            pl.BlockSpec(memory_space=pltpu.SMEM),
-            pl.BlockSpec((RING, RING, 2, half, model), lambda j: (0, 0, 0, 0, part)),
-        ],
-        out_specs=[pl.BlockSpec(shape, lambda j: (0,) * len(shape))] * count,
-        out_shape=[jax.ShapeDtypeStruct(shape, BF16)] * count,
-        compiler_params=params(12),
+        in_specs=[pl.BlockSpec(memory_space=pltpu.SMEM), block, block],
+        out_specs=pl.BlockSpec(shape, lambda j: (0,) * len(shape)),
+        out_shape=jax.ShapeDtypeStruct(shape, BF16),
+        scratch_shapes=[pltpu.VMEM(order, BF16)] if flip else [],
+        compiler_params=params(16),
         cost_estimate=light(),
         name="travel_order",
-    )(place, value)
+    )(place, own, other)
+    return result if flip else result.reshape(2, RING, RING * half, model)
 
 
 def down_products(tokens, groups):
-    _, rows, model = tokens.shape
+    _, _, rows, model = tokens.shape
     parts = [part for group in groups for part in group]
     width = parts[0][1].shape[0]
     tile = width // 2
     operands, in_specs = [], []
     for k, weight, extras in parts:
         operands += [tokens, weight] + [stack for stack, _ in extras]
-        in_specs.append(pl.BlockSpec((1, rows, model), lambda j, k=k: (k, 0, 0)))
+        in_specs.append(pl.BlockSpec((None, 1, rows, model), lambda j, k=k: (0, k, 0, 0)))
         in_specs.append(pl.BlockSpec((tile, model), lambda j: (j, 0)))
         for _, at in extras:
             in_specs.append(pl.BlockSpec((1, rows, tile), lambda j, at=at: (at, 0, j)))
@@ -163,25 +164,26 @@
 
 
 def weight_grads(left, mine, theirs, flip=False):
-    n, rows, width = mine[0].shape
-    ready = len(left) == 1
-    model = left[0].shape[0] if ready else left[0].shape[2]
-    places = [0] * RING + ([0] * RING if isinstance(theirs, list) else list(range(RING)))
-    pieces = [*mine, *(theirs if isinstance(theirs, list) else [theirs] * RING)]
+    stacked = not isinstance(theirs, list)
+    n, (_, rows, width) = (1, theirs.shape) if stacked else (mine[0].shape[0], mine[0].shape)
+    ready = left.ndim == 2
+    model = left.shape[0] if ready else left.shape[-1]
+    if stacked:
+        places = [at for _, at in mine] + list(range(RING))
+        pieces = [stack for stack, _ in mine] + [theirs] * RING
+    else:
+        places, pieces = [0] * (2 * RING), [*mine, *theirs]
     tile = 256
 
-    def kernel(*refs):
-        left_refs, refs = refs[: len(left)], refs[len(left) :]
-        held = left_refs[0]
+    def kernel(left_ref, *refs):
+        held = left_ref
         if not ready:
             held = refs[-1]
 
             @pl.when(pl.program_id(0) == 0)
             def _():
-                for i, ref in enumerate(left_refs):
-                    for k in range(RING):
-                        at = (i * RING + k) * rows
-                        held[:, at : at + rows] = ref[k].T
+                for i in range(2 * RING):
+                    held[:, i * rows : (i + 1) * rows] = left_ref[i // RING, i % RING].T
 
         for i in range(n):
             right = jnp.concatenate([ref[i] for ref in refs[: len(pieces)]], 0)
@@ -196,7 +198,7 @@
     return pl.pallas_call(
         kernel,
         grid=(width // tile,),
-        in_specs=[pl.BlockSpec(a.shape, lambda j, r=a.ndim: (0,) * r) for a in left]
+        in_specs=[pl.BlockSpec(left.shape, lambda j: (0,) * left.ndim)]
         + [pl.BlockSpec((n, rows, tile), lambda j, at=at: (at, 0, j)) for at in places],
         out_specs=[out_spec] * n,
         out_shape=[jax.ShapeDtypeStruct(shape, F32)] * n,
@@ -204,7 +206,7 @@
         compiler_params=params(18 if n > 1 else 14),
         cost_estimate=light(),
         name="weight_grads",
-    )(*left, *pieces)
+    )(left, *pieces)
 
 
 def input_products(groups, ready=(), place=None, whole=True):
@@ -311,29 +313,31 @@
 
     gate_val, up_val = gate_pre.astype(F32), up_pre.astype(F32)
     hidden = (gate_val * jax.nn.sigmoid(gate_val) * up_val).astype(BF16)
-    both = jnp.concatenate([tie(grad_out, hidden), layer_input], 1)
-    both = lax.all_gather(both, ("z", "c"), axis=0, tiled=True)
-    hid_own, hid_other = first_gather(half_of_tokens(hidden, (1, 2, half, width)))
-    w_down_other = swap(w_down)
-    hid_own, hid_other, w_down_other = lax.optimization_barrier((hid_own, hid_other, w_down_other))
-    hid_own_after, hid_other_before = mix(hid_own, 2, -1), mix(hid_other, 2, 1)
-    hid_own_before, hid_other_after = mix(hid_own, 2, 1), mix(hid_other, 2, -1)
-
-    tokens, tokens_theirs = travel_order(place, both, 0)
+    def from_z(value):
+        return jnp.stack([value, along_z(value, -1), along_z(value, 2), along_z(value, 1)])
+
+    hidden = half_of_tokens(hidden, (1, 2, half, width))
+    hid = jnp.concatenate(first_gather(hidden))
+    w_down_other = swap(tie(w_down, hidden))
+    hid, w_down_other = lax.optimization_barrier((hid, w_down_other))
+    hid_after, hid_before = mix(hid, 2, -1), mix(hid, 2, 1)
+
+    out_blocks = from_z(tie(grad_out, hidden))
+    tokens = travel_order(place, out_blocks, swap(out_blocks))
     pre = half_of_tokens(jnp.stack([gate_pre, up_pre]), (2, 2, half, width))
 
     def hidden_across():
-        return mix(hid_other_before, 2, 1), mix(hid_own_after, 2, -1)
+        return mix(hid_before[1], 2, 1), mix(hid_after[0], 2, -1)
 
     def hidden_swap(sums, other_across, own_across):
-        pieces = [hid_other, hid_other_after, other_across, hid_other_before]
-        return (swap(tie(jnp.concatenate(pieces), sums)),)
+        pieces = jnp.stack([hid[1], hid_after[1], other_across, hid_before[1]])
+        return (swap(tie(pieces, sums)),)
 
     grad_hidden, (_, hid_own_across), (hid_theirs,) = scatter_sum(
         tokens,
         w_down,
         w_down_other,
-        (hid_own_after, hid_other_before, hid_own_before, hid_other_after, pre),
+        (hid_after, hid_before, pre),
         hidden_across,
         hidden_swap,
     )
@@ -349,17 +353,17 @@
     own_after, other_before = mix(own, 2, -1), mix(other, 2, 1)
 
     (grad_down,) = weight_grads(
-        (tokens, tokens_theirs),
-        [hid_own, hid_own_after, hid_own_across, hid_own_before],
+        tokens,
+        [(hid, 0), (hid_after, 0), (hid_own_across[None], 0), (hid_before, 0)],
         hid_theirs,
         flip=True,
     )
-    (input_left,) = travel_order(place, tie(both, own), 1, flip=True)
-    theirs = [swap(other)]
-    own_before, other_after = mix(own, 2, 1), mix(other, 2, -1)
-    own_after, other_before, *_ = lax.optimization_barrier(
-        (own_after, other_before, input_left, grad_down, theirs[0])
-    )
+    input_blocks = from_z(tie(layer_input, own))
+    own_later, other_later, input_blocks, grad_down = lax.optimization_barrier(
+        (own, other, input_blocks, grad_down)
+    )
+    own_before, other_after = mix(own_later, 2, 1), mix(other_later, 2, -1)
+    input_left = travel_order(place, input_blocks, swap(input_blocks), flip=True)
     other_across, own_across = mix(other_before, 2, 1), mix(own_after, 2, -1)
 
     here, there = ((w_gate, None), (w_up, None)), ((w_other, 0), (w_other, 1))
@@ -370,14 +374,14 @@
             [(own_before, here), (other_before, there)],
         ]
     )
-    other_across, *ready, theirs_before = lax.optimization_barrier(
-        (other_across, *ready, swap(other_before))
-    )
-    theirs += [swap(other_after), swap(other_across), theirs_before]
+    other_across, input_left, *ready, theirs_here, theirs_before = lax.optimization_barrier(
+        (other_across, input_left, *ready, swap(other_later), swap(other_before))
+    )
+    theirs = [theirs_here, swap(other_after), swap(other_across), theirs_before]
     (first,) = input_products([[(other_across, there)]], whole=False)
     parts = input_products([[(own_across, here)]], [first, *ready], place)
     grad_gate, grad_up = weight_grads(
-        (input_left,),
+        input_left,
         [own, own_after, own_across, own_before],
         theirs,
     )

time: 245 us -> 232 us (0.947)
  waiting for transfers between devices: 122 us -> 104 us
  starting transfers between devices: 47.7 us -> 63.4 us
  between operations: 14.4 us -> 1.04 us
  local copies, waits for them, and re-layouts: 5.51 us -> 8.04 us
    ppermute x25 -> x23, waiting for transfers between devices: 108 us -> 89 us  [mix(): return lax.ppermute(value, ('x', 'y', 'c'), pairs)]
    ppermute x3 -> x9, waiting for transfers between devices: 0.01 us -> 10.4 us  [along_z(): lax.ppermute(value, 'z', [(z, (z + step) % RING) for z in range(RING)])]
    all_gather x1 -> x0, waiting for transfers between devices: 10.2 us -> none  [on_device(): both = lax.all_gather(both, ('z', 'c'), axis=0, tiled=True)]
    ppermute x10 -> x12, starting transfers between devices: 8.9 us -> 18.3 us  [swap(): return lax.ppermute(value, 'c', [(0, 1), (1, 0)])]
    ppermute x3 -> x9, starting transfers between devices: 6.58 us -> 15.1 us  [along_z(): lax.ppermute(value, 'z', [(z, (z + step) % RING) for z in range(RING)])]
    slice x0 -> x3, local copies, waits for them, and re-layouts: none -> 4.11 us  [the longest x2 2.81 us: hidden_swap(): pieces = jnp.stack([hid[1], hid_after[1], other_across, hid_before[1]])]
    another operation x0 -> x4, other arithmetic: none -> 2.88 us  [the longest x3 2.4 us: from_z(): jnp.stack([value, along_z(value, -1), along_z(value, 2), along_z(value, 1)])]
    concatenate x2 -> x1, other arithmetic: 3.97 us -> 1.39 us  [on_device(): hid = jnp.concatenate(first_gather(hidden))]
  transfers between devices with their start and end apart: 39 -> 44, of which waited for: 20 -> 22; matrix products, arithmetic and copies ran while one was open for 2% -> 5% of each run, Pallas kernels for 18% -> 19%
where the time goes in v3:
time: 232 us; the launch traced here: 231 us
  waiting for transfers between devices  104 us (45%)
  starting transfers between devices  63.4 us (27%)
  Pallas kernels  46.3 us (20%)
  other arithmetic  8.24 us (4%)
  local copies, waits for them, and re-layouts  8.04 us (3%)
    ppermute x23, waiting for transfers between devices, mix(): return lax.ppermute(value, ('x', 'y', 'c'), pairs)  89 us
    ppermute x23, starting transfers between devices, mix(): return lax.ppermute(value, ('x', 'y', 'c'), pairs)  29.9 us
    pallas_call x2, Pallas kernels, weight_grads(): pl.pallas_call(kernel, grid=(width // tile,), in_specs=[pl.BlockSpec(left...  20.3 us
    ppermute x12, starting transfers between devices, swap(): return lax.ppermute(value, 'c', [(0, 1), (1, 0)])  18.3 us
    pallas_call x3, Pallas kernels, input_products(): pl.pallas_call(kernel, grid=(steps,), in_specs=([pl.BlockSpec(memory_spac...  16.9 us
    ppermute x9, starting transfers between devices, along_z(): lax.ppermute(value, 'z', [(z, (z + step) % RING) for z in range(RING)])  15.1 us
    ppermute x9, waiting for transfers between devices, along_z(): lax.ppermute(value, 'z', [(z, (z + step) % RING) for z in range(RING)])  10.4 us
    pallas_call x4, Pallas kernels, down_products(): pl.pallas_call(kernel, grid=(2,), in_specs=in_specs, out_specs=[pl.BlockS...  7.15 us
  transfers between devices with their start and end apart: 44, of which 22 were waited for; matrix products, arithmetic and copies ran while one was open for 5% of the time, Pallas kernels for 19%

profile of v3, /device:TPU:1, one launch (start us, length us, event | category | flops | bytes accessed | tf_op | source)
XLA Modules:
  0.0 231.4 jit_solution(6647584577084301390)
XLA Ops:
  6.4 2.6 %collective-permute-start.6 = (bf16[2,1,64,1792]{3,2,1,0:T(8,128)(2,1)S(1)}, bf16[2,1,64,1792]{3,2,1,0:T(8,128)(2,1)S(1)}, u32[]{:S(2)}, u32[]{:S(2)}) collective-permute-start(bf16[2,1,64,1792]{3,2,1,0:T(8,128)(2,1)S(1)} %pad_maximum_fusion.12), channel_id=1, source_target_pairs={{0,64},{1,17},{8,72},{9,25},{16,80},{17,1},{24,88},{25,9},{32,96},... | collective-permute-start | bytes 1376264 | tf_op jit(solution)/shard_map/ppermute | solution.py:26
  11.1 2.9 %collective-permute-done.7 = bf16[2,1,64,1792]{3,2,1,0:T(8,128)(2,1)S(1)} collective-permute-done((bf16[2,1,64,1792]{3,2,1,0:T(8,128)(2,1)S(1)}, bf16[2,1,64,1792]{3,2,1,0:T(8,128)(2,1)S(1)}, u32[]{:S(2)}, u32[]{:S(2)}) %collective-permute-start.7) | collective-permute-done | bytes 458784 | tf_op jit(solution)/shard_map/ppermute | solution.py:26
  14.0 6.1 %collective-permute-done.6 = bf16[2,1,64,1792]{3,2,1,0:T(8,128)(2,1)S(1)} collective-permute-done((bf16[2,1,64,1792]{3,2,1,0:T(8,128)(2,1)S(1)}, bf16[2,1,64,1792]{3,2,1,0:T(8,128)(2,1)S(1)}, u32[]{:S(2)}, u32[]{:S(2)}) %collective-permute-start.6) | collective-permute-done | bytes 458784 | tf_op jit(solution)/shard_map/ppermute | solution.py:26
  26.9 3.3 %collective-permute-start.2 = (bf16[256,512]{1,0:T(8,128)(2,1)S(1)}, bf16[256,512]{1,0:T(8,128)(2,1)S(1)}, u32[]{:S(2)}, u32[]{:S(2)}) collective-permute-start(bf16[256,512]{1,0:T(8,128)(2,1)S(1)} %copy-done.7), channel_id=1, source_target_pairs={{0,4},{2,6},{4,0},{6,2},{1,5},{3,7},{5,1},{7,3},{8,12},{10,14},{12... | collective-permute-start | bytes 786440 | tf_op jit(solution)/shard_map/ppermute | solution.py:30
  30.9 3.0 %collective-permute-done.3 = bf16[256,512]{1,0:T(8,128)(2,1)S(1)} collective-permute-done((bf16[256,512]{1,0:T(8,128)(2,1)S(1)}, bf16[256,512]{1,0:T(8,128)(2,1)S(1)}, u32[]{:S(2)}, u32[]{:S(2)}) %collective-permute-start.3) | collective-permute-done | bytes 262176 | tf_op jit(solution)/shard_map/ppermute | solution.py:30
  33.9 6.4 %collective-permute-done.2 = bf16[256,512]{1,0:T(8,128)(2,1)S(1)} collective-permute-done((bf16[256,512]{1,0:T(8,128)(2,1)S(1)}, bf16[256,512]{1,0:T(8,128)(2,1)S(1)}, u32[]{:S(2)}, u32[]{:S(2)}) %collective-permute-start.2) | collective-permute-done | bytes 262176 | tf_op jit(solution)/shard_map/ppermute | solution.py:30
  42.1 2.7 %collective-permute-start.4 = (bf16[4,256,512]{2,1,0:T(8,128)(2,1)}, bf16[4,256,512]{2,1,0:T(8,128)(2,1)S(1)}, u32[]{:S(2)}, u32[]{:S(2)}) collective-permute-start(bf16[4,256,512]{2,1,0:T(8,128)(2,1)} %pad_maximum_fusion.8), channel_id=1, source_target_pairs={{0,1},{1,0},{2,3},{3,2},{4,5},{5,4},{6,7},{7,6},{8,9},{9,8},{10,11... | collective-permute-start | bytes 3145736 | tf_op jit(solution)/shard_map/ppermute | solution.py:34
  52.4 2.6 %collective-permute-start.15 = (bf16[2,256,1792]{2,1,0:T(8,128)(2,1)S(1)}, bf16[2,256,1792]{2,1,0:T(8,128)(2,1)S(1)}, u32[]{:S(2)}, u32[]{:S(2)}) collective-permute-start(bf16[2,256,1792]{2,1,0:T(8,128)(2,1)S(1)} %down_products.5), channel_id=1, source_target_pairs={{0,24},{1,97},{8,0},{9,105},{16,8},{17,113},{24,16},{25,121},{32,5... | collective-permute-start | bytes 5505032 | tf_op jit(solution)/shard_map/ppermute | solution.py:26
  59.5 16.3 %collective-permute-done.14.refs_2_.refs_6_ = bf16[2,256,1792]{2,1,0:T(8,128)(2,1)S(1)} collective-permute-done((bf16[2,256,1792]{2,1,0:T(8,128)(2,1)S(1)}, bf16[2,256,1792]{2,1,0:T(8,128)(2,1)S(1)}, u32[]{:S(2)}, u32[]{:S(2)}) %collective-permute-start.14) | collective-permute-done | bytes 1835040 | tf_op jit(solution)/shard_map/ppermute | solution.py:26
  81.8 3.2 %collective-permute-done.12 = bf16[256,1792]{1,0:T(8,128)(2,1)S(1)} collective-permute-done((bf16[256,1792]{1,0:T(8,128)(2,1)S(1)}, bf16[256,1792]{1,0:T(8,128)(2,1)S(1)}, u32[]{:S(2)}, u32[]{:S(2)}) %collective-permute-start.12) | collective-permute-done | bytes 917536 | tf_op jit(solution)/shard_map/ppermute | solution.py:26
  86.2 9.3 %collective-permute-done.16.refs_2_ = bf16[1,256,1792]{2,1,0:T(8,128)(2,1)S(1)} collective-permute-done((bf16[1,256,1792]{2,1,0:T(8,128)(2,1)S(1)}, bf16[1,256,1792]{2,1,0:T(8,128)(2,1)S(1)}, u32[]{:S(2)}, u32[]{:S(2)}) %collective-permute-start.16) | collective-permute-done | bytes 917536 | tf_op jit(solution)/shard_map/ppermute | solution.py:26
  100.8 2.8 %collective-permute-start.19 = (bf16[2,64,1792]{2,1,0:T(8,128)(2,1)S(1)}, bf16[2,64,1792]{2,1,0:T(8,128)(2,1)S(1)}, u32[]{:S(2)}, u32[]{:S(2)}) collective-permute-start(bf16[2,64,1792]{2,1,0:T(8,128)(2,1)S(1)} %get-tuple-element.86), channel_id=1, source_target_pairs={{0,64},{1,17},{8,72},{9,25},{16,80},{17,1},{24,88},{25,9},{32,96},... | collective-permute-start | bytes 1376264 | tf_op jit(solution)/shard_map/ppermute | solution.py:26
  105.8 2.8 %collective-permute-done.20 = bf16[2,64,1792]{2,1,0:T(8,128)(2,1)S(1)} collective-permute-done((bf16[2,64,1792]{2,1,0:T(8,128)(2,1)S(1)}, bf16[2,64,1792]{2,1,0:T(8,128)(2,1)S(1)}, u32[]{:S(2)}, u32[]{:S(2)}) %collective-permute-start.20) | collective-permute-done | bytes 458784 | tf_op jit(solution)/shard_map/ppermute | solution.py:26
  108.6 6.1 %collective-permute-done.19 = bf16[2,64,1792]{2,1,0:T(8,128)(2,1)S(1)} collective-permute-done((bf16[2,64,1792]{2,1,0:T(8,128)(2,1)S(1)}, bf16[2,64,1792]{2,1,0:T(8,128)(2,1)S(1)}, u32[]{:S(2)}, u32[]{:S(2)}) %collective-permute-start.19) | collective-permute-done | bytes 458784 | tf_op jit(solution)/shard_map/ppermute | solution.py:26
  120.8 10.4 %collective-permute-done.23 = bf16[2,2,64,1792]{3,2,1,0:T(8,128)(2,1)S(1)} collective-permute-done((bf16[2,2,64,1792]{3,2,1,0:T(8,128)(2,1)S(1)}, bf16[2,2,64,1792]{3,2,1,0:T(8,128)(2,1)S(1)}, u32[]{:S(2)}, u32[]{:S(2)}) %collective-permute-start.23) | collective-permute-done | bytes 917536 | tf_op jit(solution)/shard_map/ppermute | solution.py:26
  131.2 10.1 %collective-permute-done.22 = bf16[2,2,64,1792]{3,2,1,0:T(8,128)(2,1)S(1)} collective-permute-done((bf16[2,2,64,1792]{3,2,1,0:T(8,128)(2,1)S(1)}, bf16[2,2,64,1792]{3,2,1,0:T(8,128)(2,1)S(1)}, u32[]{:S(2)}, u32[]{:S(2)}) %collective-permute-start.22) | collective-permute-done | bytes 917536 | tf_op jit(solution)/shard_map/ppermute | solution.py:26
  145.2 3.3 %collective-permute-start.31 = (bf16[256,512]{1,0:T(8,128)(2,1)S(1)}, bf16[256,512]{1,0:T(8,128)(2,1)S(1)}, u32[]{:S(2)}, u32[]{:S(2)}) collective-permute-start(bf16[256,512]{1,0:T(8,128)(2,1)S(1)} %copy-done.10), channel_id=1, source_target_pairs={{0,4},{2,6},{4,0},{6,2},{1,5},{3,7},{5,1},{7,3},{8,12},{10,14},{12... | collective-permute-start | bytes 786440 | tf_op jit(solution)/shard_map/ppermute | solution.py:30
  149.3 9.4 %weight_grads.2 = f32[1792,512]{1,0:T(8,128)} custom-call(bf16[2,4,256,512]{3,2,1,0:T(8,128)(2,1)S(1)} %bitcast.116, bf16[2,256,1792]{2,1,0:T(8,128)(2,1)} %pad_maximum_fusion.2.refs_0_, bf16[2,256,1792]{2,1,0:T(8,128)(2,1)} %collective-permute-done.11.refs_1_, bf16[1,256,1792]{2,1,0:T(8,128)(2,1)S(1)} %bitcast.131, ...), custom_call_target="tpu_custom_call" | custom-call | flops 1 | bytes 1 | tf_op jit(solution)/shard_map/weight_grads/pallas_call | solution.py:198
  167.9 17.5 %collective-permute-done.35.refs_4_.refs_3_ = bf16[2,256,1792]{2,1,0:T(8,128)(2,1)S(1)} collective-permute-done((bf16[2,256,1792]{2,1,0:T(8,128)(2,1)S(1)}, bf16[2,256,1792]{2,1,0:T(8,128)(2,1)S(1)}, u32[]{:S(2)}, u32[]{:S(2)}) %collective-permute-start.35) | collective-permute-done | bytes 1835040 | tf_op jit(solution)/shard_map/ppermute | solution.py:26
  189.9 12.2 %input_products.3 = (bf16[256,512]{1,0:T(8,128)(2,1)S(1)}, bf16[256,512]{1,0:T(8,128)(2,1)S(1)}, bf16[256,512]{1,0:T(8,128)(2,1)S(1)}) custom-call(bf16[2,256,1792]{2,1,0:T(8,128)(2,1)S(1)} %bitcast.121, bf16[2,256,1792]{2,1,0:T(8,128)(2,1)S(1)} %bitcast.126, bf16[2,256,1792]{2,1,0:T(8,128)(2,1)S(1)} %collective-permute-done.26.refs_2_.refs_1_, ...), custom_call_target="tpu_custom_call" | custom-call | flops 1 | bytes 1 | tf_op jit(solution)/shard_map/input_products/pallas_call | solution.py:283
  202.2 2.9 %collective-permute-done.29.refs_0_ = bf16[2,256,1792]{2,1,0:T(8,128)(2,1)S(1)} collective-permute-done((bf16[2,256,1792]{2,1,0:T(8,128)(2,1)S(1)}, bf16[2,256,1792]{2,1,0:T(8,128)(2,1)S(1)}, u32[]{:S(2)}, u32[]{:S(2)}) %collective-permute-start.29) | collective-permute-done | bytes 1835040 | tf_op jit(solution)/shard_map/ppermute | solution.py:26
  208.4 2.6 %input_products.5 = (bf16[2,2,64,512]{3,2,1,0:T(8,128)(2,1)S(1)}, bf16[2,2,64,512]{3,2,1,0:T(8,128)(2,1)S(1)}, bf16[2,2,64,512]{3,2,1,0:T(8,128)(2,1)S(1)}, bf16[2,2,64,512]{3,2,1,0:T(8,128)(2,1)S(1)}) custom-call(s32[4]{0:T(128)S(1)} %pad_add_fusion.place_ref.refs_0_, bf16[2,256,1792]{2,1,0:T(8,128)(2,1)S(1)} %collective-permute-done.27.refs_1_.refs_2_, ...), custom_call_target="tpu_custom_call" | custom-call | flops 1 | bytes 1 | tf_op jit(solution)/shard_map/input_products/pallas_call | solution.py:283
  216.1 10.9 %weight_grads.3 = (f32[512,1792]{1,0:T(8,128)}, f32[512,1792]{1,0:T(8,128)}) custom-call(bf16[512,2048]{1,0:T(8,128)(2,1)S(1)} %travel_order.3.left_ref, bf16[2,256,1792]{2,1,0:T(8,128)(2,1)S(1)} %bitcast.122, bf16[2,256,1792]{2,1,0:T(8,128)(2,1)S(1)} %collective-permute-done.26.refs_2_.refs_1_, ...), custom_call_target="tpu_custom_call" | custom-call | flops 1 | bytes 1 | tf_op jit(solution)/shard_map/weight_grads/pallas_call | solution.py:198
  227.2 2.4 %collective-permute-start.43 = (bf16[2,64,512]{2,1,0:T(8,128)(2,1)S(1)}, bf16[2,64,512]{2,1,0:T(8,128)(2,1)S(1)}, u32[]{:S(2)}, u32[]{:S(2)}) collective-permute-start(bf16[2,64,512]{2,1,0:T(8,128)(2,1)S(1)} %get-tuple-element.107), channel_id=1, source_target_pairs={{0,1},{1,0},{2,3},{3,2},{4,5},{5,4},{6,7},{7,6},{8,9},{9,8},{10,11... | collective-permute-start | bytes 393224 | tf_op jit(solution)/shard_map/ppermute | solution.py:34
  (130 shorter events, 78.5 us)
Async XLA Ops:
  23.0 29.1 %collective-permute-start.11 = (bf16[2,256,1792]{2,1,0:T(8,128)(2,1)}, bf16[2,256,1792]{2,1,0:T(8,128)(2,1)}, u32[]{:S(2)}, u32[]{:S(2)}) collective-permute-start(bf16[2,256,1792]{2,1,0:T(8,128)(2,1)} %pad_maximum_fusion.2.refs_0_), channel_id=1, source_target_pairs={{0,24},{1,97},{8,0},{9,105},{16,8},{17,113},{24,16},{25,121},{32,5... | collective-permute-start | bytes 5505032 | tf_op jit(solution)/shard_map/ppermute | solution.py:26
  25.2 27.0 %collective-permute-start.9 = (bf16[2,256,1792]{2,1,0:T(8,128)(2,1)}, bf16[2,256,1792]{2,1,0:T(8,128)(2,1)}, u32[]{:S(2)}, u32[]{:S(2)}) collective-permute-start(bf16[2,256,1792]{2,1,0:T(8,128)(2,1)} %pad_maximum_fusion.2.refs_0_), channel_id=1, source_target_pairs={{0,8},{1,33},{8,16},{9,41},{16,24},{17,49},{24,0},{25,57},{32,40},... | collective-permute-start | bytes 5505032 | tf_op jit(solution)/shard_map/ppermute | solution.py:26
  52.2 23.7 %collective-permute-start.14 = (bf16[2,256,1792]{2,1,0:T(8,128)(2,1)S(1)}, bf16[2,256,1792]{2,1,0:T(8,128)(2,1)S(1)}, u32[]{:S(2)}, u32[]{:S(2)}) collective-permute-start(bf16[2,256,1792]{2,1,0:T(8,128)(2,1)S(1)} %down_products.4), channel_id=1, source_target_pairs={{0,8},{1,33},{8,16},{9,41},{16,24},{17,49},{24,0},{25,57},{32,40},... | collective-permute-start | bytes 5505032 | tf_op jit(solution)/shard_map/ppermute | solution.py:26
  52.4 23.4 %collective-permute-start.15 = (bf16[2,256,1792]{2,1,0:T(8,128)(2,1)S(1)}, bf16[2,256,1792]{2,1,0:T(8,128)(2,1)S(1)}, u32[]{:S(2)}, u32[]{:S(2)}) collective-permute-start(bf16[2,256,1792]{2,1,0:T(8,128)(2,1)S(1)} %down_products.5), channel_id=1, source_target_pairs={{0,24},{1,97},{8,0},{9,105},{16,8},{17,113},{24,16},{25,121},{32,5... | collective-permute-start | bytes 5505032 | tf_op jit(solution)/shard_map/ppermute | solution.py:26
  56.6 28.4 %collective-permute-start.12 = (bf16[256,1792]{1,0:T(8,128)(2,1)S(1)}, bf16[256,1792]{1,0:T(8,128)(2,1)S(1)}, u32[]{:S(2)}, u32[]{:S(2)}) collective-permute-start(bf16[256,1792]{1,0:T(8,128)(2,1)S(1)} %get-tuple-element.81), channel_id=1, source_target_pairs={{0,24},{1,97},{8,0},{9,105},{16,8},{17,113},{24,16},{25,121},{32,5... | collective-permute-start | bytes 2752520 | tf_op jit(solution)/shard_map/ppermute | solution.py:26
  59.3 26.3 %collective-permute-start.10 = (bf16[256,1792]{1,0:T(8,128)(2,1)S(1)}, bf16[256,1792]{1,0:T(8,128)(2,1)S(1)}, u32[]{:S(2)}, u32[]{:S(2)}) collective-permute-start(bf16[256,1792]{1,0:T(8,128)(2,1)S(1)} %get-tuple-element.83), channel_id=1, source_target_pairs={{0,8},{1,33},{8,16},{9,41},{16,24},{17,49},{24,0},{25,57},{32,40},... | collective-permute-start | bytes 2752520 | tf_op jit(solution)/shard_map/ppermute | solution.py:26
  77.7 17.8 %collective-permute-start.16 = (bf16[1,256,1792]{2,1,0:T(8,128)(2,1)S(1)}, bf16[1,256,1792]{2,1,0:T(8,128)(2,1)S(1)}, u32[]{:S(2)}, u32[]{:S(2)}) collective-permute-start(bf16[1,256,1792]{2,1,0:T(8,128)(2,1)S(1)} %get-tuple-element.48), channel_id=1, source_target_pairs={{0,8},{1,33},{8,16},{9,41},{16,24},{17,49},{24,0},{25,57},{32,40},... | collective-permute-start | bytes 2752520 | tf_op jit(solution)/shard_map/ppermute | solution.py:26
  78.6 16.9 %collective-permute-start.17 = (bf16[1,256,1792]{2,1,0:T(8,128)(2,1)S(1)}, bf16[1,256,1792]{2,1,0:T(8,128)(2,1)S(1)}, u32[]{:S(2)}, u32[]{:S(2)}) collective-permute-start(bf16[1,256,1792]{2,1,0:T(8,128)(2,1)S(1)} %get-tuple-element.49), channel_id=1, source_target_pairs={{0,24},{1,97},{8,0},{9,105},{16,8},{17,113},{24,16},{25,121},{32,5... | collective-permute-start | bytes 2752520 | tf_op jit(solution)/shard_map/ppermute | solution.py:26
  100.8 13.9 %collective-permute-start.19 = (bf16[2,64,1792]{2,1,0:T(8,128)(2,1)S(1)}, bf16[2,64,1792]{2,1,0:T(8,128)(2,1)S(1)}, u32[]{:S(2)}, u32[]{:S(2)}) collective-permute-start(bf16[2,64,1792]{2,1,0:T(8,128)(2,1)S(1)} %get-tuple-element.86), channel_id=1, source_target_pairs={{0,64},{1,17},{8,72},{9,25},{16,80},{17,1},{24,88},{25,9},{32,96},... | collective-permute-start | bytes 1376264 | tf_op jit(solution)/shard_map/ppermute | solution.py:26
  115.3 26.8 %collective-permute-start.25 = (bf16[2,512,1792]{2,1,0:T(8,128)(2,1)S(1)}, bf16[2,512,1792]{2,1,0:T(8,128)(2,1)S(1)}, u32[]{:S(2)}, u32[]{:S(2)}) collective-permute-start(bf16[2,512,1792]{2,1,0:T(8,128)(2,1)S(1)} %pad_maximum_fusion.1), channel_id=1, source_target_pairs={{0,1},{1,0},{2,3},{3,2},{4,5},{5,4},{6,7},{7,6},{8,9},{9,8},{10,11... | collective-permute-start | bytes 11010056 | tf_op jit(solution)/shard_map/ppermute | solution.py:34
  117.0 14.2 %collective-permute-start.23 = (bf16[2,2,64,1792]{3,2,1,0:T(8,128)(2,1)S(1)}, bf16[2,2,64,1792]{3,2,1,0:T(8,128)(2,1)S(1)}, u32[]{:S(2)}, u32[]{:S(2)}) collective-permute-start(bf16[2,2,64,1792]{3,2,1,0:T(8,128)(2,1)S(1)} %pad_maximum_fusion.6), channel_id=1, source_target_pairs={{0,64},{1,17},{8,72},{9,25},{16,80},{17,1},{24,88},{25,9},{32,96},... | collective-permute-start | bytes 2752520 | tf_op jit(solution)/shard_map/ppermute | solution.py:26
  119.2 22.1 %collective-permute-start.22 = (bf16[2,2,64,1792]{3,2,1,0:T(8,128)(2,1)S(1)}, bf16[2,2,64,1792]{3,2,1,0:T(8,128)(2,1)S(1)}, u32[]{:S(2)}, u32[]{:S(2)}) collective-permute-start(bf16[2,2,64,1792]{3,2,1,0:T(8,128)(2,1)S(1)} %pad_maximum_fusion.6), channel_id=1, source_target_pairs={{0,96},{1,25},{8,104},{9,1},{16,112},{17,9},{24,120},{25,17},{32,0... | collective-permute-start | bytes 2752520 | tf_op jit(solution)/shard_map/ppermute | solution.py:26
  120.5 20.9 %collective-permute-start.24 = (bf16[2,2,64,1792]{3,2,1,0:T(8,128)(2,1)S(1)}, bf16[2,2,64,1792]{3,2,1,0:T(8,128)(2,1)S(1)}, u32[]{:S(2)}, u32[]{:S(2)}) collective-permute-start(bf16[2,2,64,1792]{3,2,1,0:T(8,128)(2,1)S(1)} %pad_maximum_fusion.6), channel_id=1, source_target_pairs={{0,32},{1,9},{8,40},{9,17},{16,48},{17,25},{24,56},{25,1},{32,64},... | collective-permute-start | bytes 2752520 | tf_op jit(solution)/shard_map/ppermute | solution.py:26
  142.1 23.6 %collective-permute-start.28 = (bf16[2,256,1792]{2,1,0:T(8,128)(2,1)S(1)}, bf16[2,256,1792]{2,1,0:T(8,128)(2,1)S(1)}, u32[]{:S(2)}, u32[]{:S(2)}) collective-permute-start(bf16[2,256,1792]{2,1,0:T(8,128)(2,1)S(1)} %bitcast.123), channel_id=1, source_target_pairs={{0,8},{1,33},{8,16},{9,41},{16,24},{17,49},{24,0},{25,57},{32,40},... | collective-permute-start | bytes 5505032 | tf_op jit(solution)/shard_map/ppermute | solution.py:26
  143.0 24.1 %collective-permute-start.26 = (bf16[2,256,1792]{2,1,0:T(8,128)(2,1)S(1)}, bf16[2,256,1792]{2,1,0:T(8,128)(2,1)S(1)}, u32[]{:S(2)}, u32[]{:S(2)}) collective-permute-start(bf16[2,256,1792]{2,1,0:T(8,128)(2,1)S(1)} %bitcast.119), channel_id=1, source_target_pairs={{0,24},{1,97},{8,0},{9,105},{16,8},{17,113},{24,16},{25,121},{32,5... | collective-permute-start | bytes 5505032 | tf_op jit(solution)/shard_map/ppermute | solution.py:26
  145.2 14.2 %collective-permute-start.31 = (bf16[256,512]{1,0:T(8,128)(2,1)S(1)}, bf16[256,512]{1,0:T(8,128)(2,1)S(1)}, u32[]{:S(2)}, u32[]{:S(2)}) collective-permute-start(bf16[256,512]{1,0:T(8,128)(2,1)S(1)} %copy-done.10), channel_id=1, source_target_pairs={{0,4},{2,6},{4,0},{6,2},{1,5},{3,7},{5,1},{7,3},{8,12},{10,14},{12... | collective-permute-start | bytes 786440 | tf_op jit(solution)/shard_map/ppermute | solution.py:30
  161.6 23.8 %collective-permute-start.35 = (bf16[2,256,1792]{2,1,0:T(8,128)(2,1)S(1)}, bf16[2,256,1792]{2,1,0:T(8,128)(2,1)S(1)}, u32[]{:S(2)}, u32[]{:S(2)}) collective-permute-start(bf16[2,256,1792]{2,1,0:T(8,128)(2,1)S(1)} %bitcast.120), channel_id=1, source_target_pairs={{0,8},{1,33},{8,16},{9,41},{16,24},{17,49},{24,0},{25,57},{32,40},... | collective-permute-start | bytes 5505032 | tf_op jit(solution)/shard_map/ppermute | solution.py:26
  162.4 25.2 %collective-permute-start.34 = (bf16[2,256,1792]{2,1,0:T(8,128)(2,1)S(1)}, bf16[2,256,1792]{2,1,0:T(8,128)(2,1)S(1)}, u32[]{:S(2)}, u32[]{:S(2)}) collective-permute-start(bf16[2,256,1792]{2,1,0:T(8,128)(2,1)S(1)} %bitcast.124), channel_id=1, source_target_pairs={{0,24},{1,97},{8,0},{9,105},{16,8},{17,113},{24,16},{25,121},{32,5... | collective-permute-start | bytes 5505032 | tf_op jit(solution)/shard_map/ppermute | solution.py:26
  164.3 37.8 %collective-permute-start.36 = (bf16[2,256,1792]{2,1,0:T(8,128)(2,1)S(1)}, bf16[2,256,1792]{2,1,0:T(8,128)(2,1)S(1)}, u32[]{:S(2)}, u32[]{:S(2)}) collective-permute-start(bf16[2,256,1792]{2,1,0:T(8,128)(2,1)S(1)} %bitcast.125), channel_id=1, source_target_pairs={{0,1},{1,0},{2,3},{3,2},{4,5},{5,4},{6,7},{7,6},{8,9},{9,8},{10,11... | collective-permute-start | bytes 5505032 | tf_op jit(solution)/shard_map/ppermute | solution.py:34
  165.7 36.4 %collective-permute-start.37 = (bf16[2,256,1792]{2,1,0:T(8,128)(2,1)S(1)}, bf16[2,256,1792]{2,1,0:T(8,128)(2,1)S(1)}, u32[]{:S(2)}, u32[]{:S(2)}) collective-permute-start(bf16[2,256,1792]{2,1,0:T(8,128)(2,1)S(1)} %collective-permute-done.28.refs_5_), channel_id=1, source_target_pairs={{0,1},{1,0},{2,3},{3,2},{4,5},{5,4},{6,7},{7,6},{8,9},{9,8},{10,11... | collective-permute-start | bytes 5505032 | tf_op jit(solution)/shard_map/ppermute | solution.py:34
  167.1 38.0 %collective-permute-start.29 = (bf16[2,256,1792]{2,1,0:T(8,128)(2,1)S(1)}, bf16[2,256,1792]{2,1,0:T(8,128)(2,1)S(1)}, u32[]{:S(2)}, u32[]{:S(2)}) collective-permute-start(bf16[2,256,1792]{2,1,0:T(8,128)(2,1)S(1)} %collective-permute-done.28.refs_5_), channel_id=1, source_target_pairs={{0,8},{1,33},{8,16},{9,41},{16,24},{17,49},{24,0},{25,57},{32,40},... | collective-permute-start | bytes 5505032 | tf_op jit(solution)/shard_map/ppermute | solution.py:26
  185.4 23.0 %collective-permute-start.27 = (bf16[2,256,1792]{2,1,0:T(8,128)(2,1)S(1)}, bf16[2,256,1792]{2,1,0:T(8,128)(2,1)S(1)}, u32[]{:S(2)}, u32[]{:S(2)}) collective-permute-start(bf16[2,256,1792]{2,1,0:T(8,128)(2,1)S(1)} %collective-permute-done.26.refs_2_.refs_1_), channel_id=1, source_target_pairs={{0,24},{1,97},{8,0},{9,105},{16,8},{17,113},{24,16},{25,121},{32,5... | collective-permute-start | bytes 5505032 | tf_op jit(solution)/shard_map/ppermute | solution.py:26
  187.6 28.5 %collective-permute-start.38 = (bf16[2,256,1792]{2,1,0:T(8,128)(2,1)S(1)}, bf16[2,256,1792]{2,1,0:T(8,128)(2,1)S(1)}, u32[]{:S(2)}, u32[]{:S(2)}) collective-permute-start(bf16[2,256,1792]{2,1,0:T(8,128)(2,1)S(1)} %collective-permute-done.34.refs_3_), channel_id=1, source_target_pairs={{0,1},{1,0},{2,3},{3,2},{4,5},{5,4},{6,7},{7,6},{8,9},{9,8},{10,11... | collective-permute-start | bytes 5505032 | tf_op jit(solution)/shard_map/ppermute | solution.py:34
  211.0 16.0 %collective-permute-start.40 = (bf16[2,2,64,512]{3,2,1,0:T(8,128)(2,1)S(1)}, bf16[2,2,64,512]{3,2,1,0:T(8,128)(2,1)S(1)}, u32[]{:S(2)}, u32[]{:S(2)}) collective-permute-start(bf16[2,2,64,512]{3,2,1,0:T(8,128)(2,1)S(1)} %get-tuple-element.74), channel_id=1, source_target_pairs={{0,4},{2,6},{4,0},{6,2},{1,5},{3,7},{5,1},{7,3},{8,12},{10,14},{12... | collective-permute-start | bytes 786440 | tf_op jit(solution)/shard_map/ppermute | solution.py:30
  (31 other events, 248.3 us)

commit v4 on v3

--- a/solution.py
+++ b/solution.py
@@ -125,18 +125,18 @@
     )(*operands)
 
 
-def scatter_sum(tokens, weight, weight_other, before, between, beside):
+def scatter_sum(tokens, weight, weight_other, before, between):
     (fwd,) = down_products(tokens, [[(2, weight, ()), (1, weight_other, ())]])
     (back,) = down_products(tokens, [[(2, weight_other, ()), (3, weight, ())]])
     fwd, back, *_ = lax.optimization_barrier((fwd, back, *before))
     fwd, back = mix(fwd, 2, 1), mix(back, 2, -1)
-    moved = between()
     own, other = down_products(
         tokens, [[(1, weight, ((fwd, 0),))], [(3, weight_other, ((back, 0),))]]
     )
+    moved = between(own, other)
     own, other = mix(own, 2, 1), mix(other, 2, -1)
     (sums,) = down_products(
-        tie(tokens, *moved),
+        tokens,
         [
             [
                 (0, weight, ((own, 0), (back, 1))),
@@ -145,11 +145,10 @@
         ],
     )
     sums = sums.reshape(2, RING, -1, sums.shape[-1])
-    done = beside(sums, *moved)
-    total = tie(sums[:, 0], *done).astype(F32)
+    total = tie(sums[:, 0], *moved).astype(F32)
     for distance, step in ((2, 2), (1, 1), (3, -1)):
         total = total + mix(sums[:, distance], 1, step).astype(F32)
-    return total, moved, done
+    return total, moved
 
 
 def first_gather(block):
@@ -311,12 +310,13 @@
         halves = value.reshape(shape)
         return jnp.stack([pick(halves, core, 1), swap(pick(halves, 1 - core, 1))])
 
-    gate_val, up_val = gate_pre.astype(F32), up_pre.astype(F32)
-    hidden = (gate_val * jax.nn.sigmoid(gate_val) * up_val).astype(BF16)
+    pre = half_of_tokens(jnp.stack([gate_pre, up_pre]), (2, 2, half, width))
+    gate_val, up_val = pre[:, 0].astype(F32), pre[:, 1].astype(F32)
+    sigmoid_val = jax.nn.sigmoid(gate_val)
+    hidden = (gate_val * sigmoid_val * up_val).astype(BF16)[:, None]
     def from_z(value):
         return jnp.stack([value, along_z(value, -1), along_z(value, 2), along_z(value, 1)])
 
-    hidden = half_of_tokens(hidden, (1, 2, half, width))
     hid = jnp.concatenate(first_gather(hidden))
     w_down_other = swap(tie(w_down, hidden))
     hid, w_down_other = lax.optimization_barrier((hid, w_down_other))
@@ -324,23 +324,15 @@
 
     out_blocks = from_z(tie(grad_out, hidden))
     tokens = travel_order(place, out_blocks, swap(out_blocks))
-    pre = half_of_tokens(jnp.stack([gate_pre, up_pre]), (2, 2, half, width))
-
-    def hidden_across():
-        return mix(hid_before[1], 2, 1), mix(hid_after[0], 2, -1)
-
-    def hidden_swap(sums, other_across, own_across):
-        pieces = jnp.stack([hid[1], hid_after[1], other_across, hid_before[1]])
-        return (swap(tie(pieces, sums)),)
-
-    grad_hidden, (_, hid_own_across), (hid_theirs,) = scatter_sum(
-        tokens,
-        w_down,
-        w_down_other,
-        (hid_after, hid_before, pre),
-        hidden_across,
-        hidden_swap,
-    )
+
+    def hidden_across(*after):
+        return mix(tie(hid_before[1], *after), 2, 1), mix(tie(hid_after[0], *after), 2, -1)
+
+    grad_hidden, (hid_other_across, hid_own_across) = scatter_sum(
+        tokens, w_down, w_down_other, (hid_after, hid_before), hidden_across
+    )
+    hid_theirs = jnp.stack([hid[1], hid_after[1], hid_other_across, hid_before[1]])
+    hid_theirs = swap(tie(hid_theirs, grad_hidden))
 
     gate_val, up_val = pre[:, 0].astype(F32), pre[:, 1].astype(F32)
     sigmoid_val = jax.nn.sigmoid(gate_val)
@@ -349,7 +341,9 @@
     own, other = first_gather(jnp.stack([gate_grad, up_grad], 1).astype(BF16))
 
     w_other = swap(tie(jnp.stack([w_gate, w_up]), grad_hidden))
-    own, other, w_other = lax.optimization_barrier((own, other, w_other))
+    own, other, w_other, hid_theirs = lax.optimization_barrier(
+        (own, other, w_other, hid_theirs)
+    )
     own_after, other_before = mix(own, 2, -1), mix(other, 2, 1)
 
     (grad_down,) = weight_grads(

time: 232 us -> 231 us (level)
  starting transfers between devices: 63.4 us -> 60.1 us
  waiting for transfers between devices: 104 us -> 107 us
    ppermute x23, waiting for transfers between devices: 89 us -> 92.1 us  [mix(): return lax.ppermute(value, ('x', 'y', 'c'), pairs)]
    ppermute x12 -> x11, starting transfers between devices: 18.3 us -> 16.9 us  [swap(): return lax.ppermute(value, 'c', [(0, 1), (1, 0)])]
    ppermute x12 -> x11, waiting for transfers between devices: 4.91 us -> 3.55 us  [swap(): return lax.ppermute(value, 'c', [(0, 1), (1, 0)])]
  transfers between devices with their start and end apart: 44 -> 43, of which waited for: 22 -> 21; matrix products, arithmetic and copies ran while one was open for 5% -> 5% of each run, Pallas kernels for 19% -> 19%
where the time goes in v4:
time: 231 us
  waiting for transfers between devices  107 us (46%)
  starting transfers between devices  60.1 us (26%)
  Pallas kernels  46.3 us (20%)
  other arithmetic  8.65 us (4%)
  local copies, waits for them, and re-layouts  7.68 us (3%)
    ppermute x23, waiting for transfers between devices, mix(): return lax.ppermute(value, ('x', 'y', 'c'), pairs)  92.1 us
    ppermute x23, starting transfers between devices, mix(): return lax.ppermute(value, ('x', 'y', 'c'), pairs)  28.8 us
    pallas_call x2, Pallas kernels, weight_grads(): pl.pallas_call(kernel, grid=(width // tile,), in_specs=[pl.BlockSpec(left...  20.3 us
    ppermute x11, starting transfers between devices, swap(): return lax.ppermute(value, 'c', [(0, 1), (1, 0)])  16.9 us
    pallas_call x3, Pallas kernels, input_products(): pl.pallas_call(kernel, grid=(steps,), in_specs=([pl.BlockSpec(memory_spac...  16.9 us
    ppermute x9, starting transfers between devices, along_z(): lax.ppermute(value, 'z', [(z, (z + step) % RING) for z in range(RING)])  14.3 us
    ppermute x9, waiting for transfers between devices, along_z(): lax.ppermute(value, 'z', [(z, (z + step) % RING) for z in range(RING)])  11.1 us
    pallas_call x4, Pallas kernels, down_products(): pl.pallas_call(kernel, grid=(2,), in_specs=in_specs, out_specs=[pl.BlockS...  7.14 us
  transfers between devices with their start and end apart: 43, of which 21 were waited for; matrix products, arithmetic and copies ran while one was open for 5% of the time, Pallas kernels for 19%

profile of v4, /device:TPU:1, one launch (start us, length us, event | category | flops | bytes accessed | tf_op | source)
XLA Modules:
  0.0 230.6 jit_solution(4688594548012302237)
XLA Ops:
  7.1 2.6 %collective-permute-start.6 = (bf16[2,1,64,1792]{3,2,1,0:T(8,128)(2,1)S(1)}, bf16[2,1,64,1792]{3,2,1,0:T(8,128)(2,1)S(1)}, u32[]{:S(2)}, u32[]{:S(2)}) collective-permute-start(bf16[2,1,64,1792]{3,2,1,0:T(8,128)(2,1)S(1)} %fusion.9), channel_id=1, source_target_pairs={{0,64},{1,17},{8,72},{9,25},{16,80},{17,1},{24,88},{25,9},{32,96},... | collective-permute-start | bytes 1376264 | tf_op jit(solution)/shard_map/ppermute | solution.py:26
  11.9 2.8 %collective-permute-done.7 = bf16[2,1,64,1792]{3,2,1,0:T(8,128)(2,1)S(1)} collective-permute-done((bf16[2,1,64,1792]{3,2,1,0:T(8,128)(2,1)S(1)}, bf16[2,1,64,1792]{3,2,1,0:T(8,128)(2,1)S(1)}, u32[]{:S(2)}, u32[]{:S(2)}) %collective-permute-start.7) | collective-permute-done | bytes 458784 | tf_op jit(solution)/shard_map/ppermute | solution.py:26
  14.7 6.1 %collective-permute-done.6 = bf16[2,1,64,1792]{3,2,1,0:T(8,128)(2,1)S(1)} collective-permute-done((bf16[2,1,64,1792]{3,2,1,0:T(8,128)(2,1)S(1)}, bf16[2,1,64,1792]{3,2,1,0:T(8,128)(2,1)S(1)}, u32[]{:S(2)}, u32[]{:S(2)}) %collective-permute-start.6) | collective-permute-done | bytes 458784 | tf_op jit(solution)/shard_map/ppermute | solution.py:26
  28.1 3.3 %collective-permute-start.2 = (bf16[256,512]{1,0:T(8,128)(2,1)S(1)}, bf16[256,512]{1,0:T(8,128)(2,1)S(1)}, u32[]{:S(2)}, u32[]{:S(2)}) collective-permute-start(bf16[256,512]{1,0:T(8,128)(2,1)S(1)} %copy-done.9), channel_id=1, source_target_pairs={{0,4},{2,6},{4,0},{6,2},{1,5},{3,7},{5,1},{7,3},{8,12},{10,14},{12... | collective-permute-start | bytes 786440 | tf_op jit(solution)/shard_map/ppermute | solution.py:30
  32.1 3.3 %collective-permute-done.3 = bf16[256,512]{1,0:T(8,128)(2,1)S(1)} collective-permute-done((bf16[256,512]{1,0:T(8,128)(2,1)S(1)}, bf16[256,512]{1,0:T(8,128)(2,1)S(1)}, u32[]{:S(2)}, u32[]{:S(2)}) %collective-permute-start.3) | collective-permute-done | bytes 262176 | tf_op jit(solution)/shard_map/ppermute | solution.py:30
  35.4 6.4 %collective-permute-done.2 = bf16[256,512]{1,0:T(8,128)(2,1)S(1)} collective-permute-done((bf16[256,512]{1,0:T(8,128)(2,1)S(1)}, bf16[256,512]{1,0:T(8,128)(2,1)S(1)}, u32[]{:S(2)}, u32[]{:S(2)}) %collective-permute-start.2) | collective-permute-done | bytes 262176 | tf_op jit(solution)/shard_map/ppermute | solution.py:30
  52.9 2.7 %collective-permute-start.12 = (bf16[2,256,1792]{2,1,0:T(8,128)(2,1)S(1)}, bf16[2,256,1792]{2,1,0:T(8,128)(2,1)S(1)}, u32[]{:S(2)}, u32[]{:S(2)}) collective-permute-start(bf16[2,256,1792]{2,1,0:T(8,128)(2,1)S(1)} %down_products.5), channel_id=1, source_target_pairs={{0,24},{1,97},{8,0},{9,105},{16,8},{17,113},{24,16},{25,121},{32,5... | collective-permute-start | bytes 5505032 | tf_op jit(solution)/shard_map/ppermute | solution.py:26
  55.5 20.9 %collective-permute-done.11.refs_2_.refs_6_ = bf16[2,256,1792]{2,1,0:T(8,128)(2,1)S(1)} collective-permute-done((bf16[2,256,1792]{2,1,0:T(8,128)(2,1)S(1)}, bf16[2,256,1792]{2,1,0:T(8,128)(2,1)S(1)}, u32[]{:S(2)}, u32[]{:S(2)}) %collective-permute-start.11) | collective-permute-done | bytes 1835040 | tf_op jit(solution)/shard_map/ppermute | solution.py:26
  78.4 2.7 %collective-permute-start.14 = (bf16[1,256,1792]{2,1,0:T(8,128)(2,1)S(1)}, bf16[1,256,1792]{2,1,0:T(8,128)(2,1)S(1)}, u32[]{:S(2)}, u32[]{:S(2)}) collective-permute-start(bf16[1,256,1792]{2,1,0:T(8,128)(2,1)S(1)} %get-tuple-element.50), channel_id=1, source_target_pairs={{0,24},{1,97},{8,0},{9,105},{16,8},{17,113},{24,16},{25,121},{32,5... | collective-permute-start | bytes 2752520 | tf_op jit(solution)/shard_map/ppermute | solution.py:26
  84.0 2.7 %collective-permute-start.16 = (bf16[256,1792]{1,0:T(8,128)(2,1)S(1)}, bf16[256,1792]{1,0:T(8,128)(2,1)S(1)}, u32[]{:S(2)}, u32[]{:S(2)}) collective-permute-start(bf16[256,1792]{1,0:T(8,128)(2,1)S(1)} %get-tuple-element.52), channel_id=1, source_target_pairs={{0,24},{1,97},{8,0},{9,105},{16,8},{17,113},{24,16},{25,121},{32,5... | collective-permute-start | bytes 2752520 | tf_op jit(solution)/shard_map/ppermute | solution.py:26
  86.7 5.4 %collective-permute-done.13.refs_2_ = bf16[1,256,1792]{2,1,0:T(8,128)(2,1)S(1)} collective-permute-done((bf16[1,256,1792]{2,1,0:T(8,128)(2,1)S(1)}, bf16[1,256,1792]{2,1,0:T(8,128)(2,1)S(1)}, u32[]{:S(2)}, u32[]{:S(2)}) %collective-permute-start.13) | collective-permute-done | bytes 917536 | tf_op jit(solution)/shard_map/ppermute | solution.py:26
  94.6 2.7 %collective-permute-start.17 = (bf16[2,64,1792]{2,1,0:T(8,128)(2,1)S(1)}, bf16[2,64,1792]{2,1,0:T(8,128)(2,1)S(1)}, u32[]{:S(2)}, u32[]{:S(2)}) collective-permute-start(bf16[2,64,1792]{2,1,0:T(8,128)(2,1)S(1)} %get-tuple-element.92), channel_id=1, source_target_pairs={{0,64},{1,17},{8,72},{9,25},{16,80},{17,1},{24,88},{25,9},{32,96},... | collective-permute-start | bytes 1376264 | tf_op jit(solution)/shard_map/ppermute | solution.py:26
  99.7 3.2 %collective-permute-done.15 = bf16[256,1792]{1,0:T(8,128)(2,1)S(1)} collective-permute-done((bf16[256,1792]{1,0:T(8,128)(2,1)S(1)}, bf16[256,1792]{1,0:T(8,128)(2,1)S(1)}, u32[]{:S(2)}, u32[]{:S(2)}) %collective-permute-start.15) | collective-permute-done | bytes 917536 | tf_op jit(solution)/shard_map/ppermute | solution.py:26
  102.9 3.4 %collective-permute-done.16 = bf16[256,1792]{1,0:T(8,128)(2,1)S(1)} collective-permute-done((bf16[256,1792]{1,0:T(8,128)(2,1)S(1)}, bf16[256,1792]{1,0:T(8,128)(2,1)S(1)}, u32[]{:S(2)}, u32[]{:S(2)}) %collective-permute-start.16) | collective-permute-done | bytes 917536 | tf_op jit(solution)/shard_map/ppermute | solution.py:26
  108.2 6.4 %collective-permute-done.17 = bf16[2,64,1792]{2,1,0:T(8,128)(2,1)S(1)} collective-permute-done((bf16[2,64,1792]{2,1,0:T(8,128)(2,1)S(1)}, bf16[2,64,1792]{2,1,0:T(8,128)(2,1)S(1)}, u32[]{:S(2)}, u32[]{:S(2)}) %collective-permute-start.17) | collective-permute-done | bytes 458784 | tf_op jit(solution)/shard_map/ppermute | solution.py:26
  119.9 10.4 %collective-permute-done.21 = bf16[2,2,64,1792]{3,2,1,0:T(8,128)(2,1)S(1)} collective-permute-done((bf16[2,2,64,1792]{3,2,1,0:T(8,128)(2,1)S(1)}, bf16[2,2,64,1792]{3,2,1,0:T(8,128)(2,1)S(1)}, u32[]{:S(2)}, u32[]{:S(2)}) %collective-permute-start.21) | collective-permute-done | bytes 917536 | tf_op jit(solution)/shard_map/ppermute | solution.py:26
  130.4 10.3 %collective-permute-done.20 = bf16[2,2,64,1792]{3,2,1,0:T(8,128)(2,1)S(1)} collective-permute-done((bf16[2,2,64,1792]{3,2,1,0:T(8,128)(2,1)S(1)}, bf16[2,2,64,1792]{3,2,1,0:T(8,128)(2,1)S(1)}, u32[]{:S(2)}, u32[]{:S(2)}) %collective-permute-start.20) | collective-permute-done | bytes 917536 | tf_op jit(solution)/shard_map/ppermute | solution.py:26
  141.6 2.7 %collective-permute-start.25 = (bf16[2,256,1792]{2,1,0:T(8,128)(2,1)S(1)}, bf16[2,256,1792]{2,1,0:T(8,128)(2,1)S(1)}, u32[]{:S(2)}, u32[]{:S(2)}) collective-permute-start(bf16[2,256,1792]{2,1,0:T(8,128)(2,1)S(1)} %bitcast.161), channel_id=1, source_target_pairs={{0,24},{1,97},{8,0},{9,105},{16,8},{17,113},{24,16},{25,121},{32,5... | collective-permute-start | bytes 5505032 | tf_op jit(solution)/shard_map/ppermute | solution.py:26
  148.2 9.4 %weight_grads.2 = f32[1792,512]{1,0:T(8,128)} custom-call(bf16[2,4,256,512]{3,2,1,0:T(8,128)(2,1)S(1)} %bitcast.158, bf16[2,256,1792]{2,1,0:T(8,128)(2,1)} %pad_maximum_fusion.2.refs_0_, bf16[2,256,1792]{2,1,0:T(8,128)(2,1)} %collective-permute-done.9.refs_1_, bf16[1,256,1792]{2,1,0:T(8,128)(2,1)S(1)} %bitcast.173, ...), custom_call_target="tpu_custom_call" | custom-call | flops 1 | bytes 1 | tf_op jit(solution)/shard_map/weight_grads/pallas_call | solution.py:197
  160.6 2.7 %collective-permute-start.33 = (bf16[2,256,1792]{2,1,0:T(8,128)(2,1)S(1)}, bf16[2,256,1792]{2,1,0:T(8,128)(2,1)S(1)}, u32[]{:S(2)}, u32[]{:S(2)}) collective-permute-start(bf16[2,256,1792]{2,1,0:T(8,128)(2,1)S(1)} %bitcast.166), channel_id=1, source_target_pairs={{0,24},{1,97},{8,0},{9,105},{16,8},{17,113},{24,16},{25,121},{32,5... | collective-permute-start | bytes 5505032 | tf_op jit(solution)/shard_map/ppermute | solution.py:26
  166.7 18.1 %collective-permute-done.34.refs_4_.refs_3_ = bf16[2,256,1792]{2,1,0:T(8,128)(2,1)S(1)} collective-permute-done((bf16[2,256,1792]{2,1,0:T(8,128)(2,1)S(1)}, bf16[2,256,1792]{2,1,0:T(8,128)(2,1)S(1)}, u32[]{:S(2)}, u32[]{:S(2)}) %collective-permute-start.34) | collective-permute-done | bytes 1835040 | tf_op jit(solution)/shard_map/ppermute | solution.py:26
  186.2 3.6 %collective-permute-start.37 = (bf16[2,256,1792]{2,1,0:T(8,128)(2,1)S(1)}, bf16[2,256,1792]{2,1,0:T(8,128)(2,1)S(1)}, u32[]{:S(2)}, u32[]{:S(2)}) collective-permute-start(bf16[2,256,1792]{2,1,0:T(8,128)(2,1)S(1)} %collective-permute-done.33.refs_3_), channel_id=1, source_target_pairs={{0,1},{1,0},{2,3},{3,2},{4,5},{5,4},{6,7},{7,6},{8,9},{9,8},{10,11... | collective-permute-start | bytes 5505032 | tf_op jit(solution)/shard_map/ppermute | solution.py:34
  189.8 12.2 %input_products.3 = (bf16[256,512]{1,0:T(8,128)(2,1)S(1)}, bf16[256,512]{1,0:T(8,128)(2,1)S(1)}, bf16[256,512]{1,0:T(8,128)(2,1)S(1)}) custom-call(bf16[2,256,1792]{2,1,0:T(8,128)(2,1)S(1)} %bitcast.163, bf16[2,256,1792]{2,1,0:T(8,128)(2,1)S(1)} %bitcast.168, bf16[2,256,1792]{2,1,0:T(8,128)(2,1)S(1)} %collective-permute-done.25.refs_2_.refs_1_, ...), custom_call_target="tpu_custom_call" | custom-call | flops 1 | bytes 1 | tf_op jit(solution)/shard_map/input_products/pallas_call | solution.py:282
  215.3 11.0 %weight_grads.3 = (f32[512,1792]{1,0:T(8,128)}, f32[512,1792]{1,0:T(8,128)}) custom-call(bf16[512,2048]{1,0:T(8,128)(2,1)S(1)} %travel_order.3.left_ref, bf16[2,256,1792]{2,1,0:T(8,128)(2,1)S(1)} %bitcast.164, bf16[2,256,1792]{2,1,0:T(8,128)(2,1)S(1)} %collective-permute-done.25.refs_2_.refs_1_, ...), custom_call_target="tpu_custom_call" | custom-call | flops 1 | bytes 1 | tf_op jit(solution)/shard_map/weight_grads/pallas_call | solution.py:197
  (134 shorter events, 74.6 us)
Async XLA Ops:
  23.8 29.0 %collective-permute-start.10 = (bf16[2,256,1792]{2,1,0:T(8,128)(2,1)}, bf16[2,256,1792]{2,1,0:T(8,128)(2,1)}, u32[]{:S(2)}, u32[]{:S(2)}) collective-permute-start(bf16[2,256,1792]{2,1,0:T(8,128)(2,1)} %pad_maximum_fusion.2.refs_0_), channel_id=1, source_target_pairs={{0,8},{1,33},{8,16},{9,41},{16,24},{17,49},{24,0},{25,57},{32,40},... | collective-permute-start | bytes 5505032 | tf_op jit(solution)/shard_map/ppermute | solution.py:26
  24.7 28.1 %collective-permute-start.9 = (bf16[2,256,1792]{2,1,0:T(8,128)(2,1)}, bf16[2,256,1792]{2,1,0:T(8,128)(2,1)}, u32[]{:S(2)}, u32[]{:S(2)}) collective-permute-start(bf16[2,256,1792]{2,1,0:T(8,128)(2,1)} %pad_maximum_fusion.2.refs_0_), channel_id=1, source_target_pairs={{0,24},{1,97},{8,0},{9,105},{16,8},{17,113},{24,16},{25,121},{32,5... | collective-permute-start | bytes 5505032 | tf_op jit(solution)/shard_map/ppermute | solution.py:26
  52.8 23.6 %collective-permute-start.11 = (bf16[2,256,1792]{2,1,0:T(8,128)(2,1)S(1)}, bf16[2,256,1792]{2,1,0:T(8,128)(2,1)S(1)}, u32[]{:S(2)}, u32[]{:S(2)}) collective-permute-start(bf16[2,256,1792]{2,1,0:T(8,128)(2,1)S(1)} %down_products.4), channel_id=1, source_target_pairs={{0,8},{1,33},{8,16},{9,41},{16,24},{17,49},{24,0},{25,57},{32,40},... | collective-permute-start | bytes 5505032 | tf_op jit(solution)/shard_map/ppermute | solution.py:26
  52.9 23.6 %collective-permute-start.12 = (bf16[2,256,1792]{2,1,0:T(8,128)(2,1)S(1)}, bf16[2,256,1792]{2,1,0:T(8,128)(2,1)S(1)}, u32[]{:S(2)}, u32[]{:S(2)}) collective-permute-start(bf16[2,256,1792]{2,1,0:T(8,128)(2,1)S(1)} %down_products.5), channel_id=1, source_target_pairs={{0,24},{1,97},{8,0},{9,105},{16,8},{17,113},{24,16},{25,121},{32,5... | collective-permute-start | bytes 5505032 | tf_op jit(solution)/shard_map/ppermute | solution.py:26
  83.9 19.0 %collective-permute-start.15 = (bf16[256,1792]{1,0:T(8,128)(2,1)S(1)}, bf16[256,1792]{1,0:T(8,128)(2,1)S(1)}, u32[]{:S(2)}, u32[]{:S(2)}) collective-permute-start(bf16[256,1792]{1,0:T(8,128)(2,1)S(1)} %get-tuple-element.51), channel_id=1, source_target_pairs={{0,8},{1,33},{8,16},{9,41},{16,24},{17,49},{24,0},{25,57},{32,40},... | collective-permute-start | bytes 2752520 | tf_op jit(solution)/shard_map/ppermute | solution.py:26
  84.0 22.3 %collective-permute-start.16 = (bf16[256,1792]{1,0:T(8,128)(2,1)S(1)}, bf16[256,1792]{1,0:T(8,128)(2,1)S(1)}, u32[]{:S(2)}, u32[]{:S(2)}) collective-permute-start(bf16[256,1792]{1,0:T(8,128)(2,1)S(1)} %get-tuple-element.52), channel_id=1, source_target_pairs={{0,24},{1,97},{8,0},{9,105},{16,8},{17,113},{24,16},{25,121},{32,5... | collective-permute-start | bytes 2752520 | tf_op jit(solution)/shard_map/ppermute | solution.py:26
  94.3 13.9 %collective-permute-start.18 = (bf16[2,64,1792]{2,1,0:T(8,128)(2,1)S(1)}, bf16[2,64,1792]{2,1,0:T(8,128)(2,1)S(1)}, u32[]{:S(2)}, u32[]{:S(2)}) collective-permute-start(bf16[2,64,1792]{2,1,0:T(8,128)(2,1)S(1)} %get-tuple-element.91), channel_id=1, source_target_pairs={{0,32},{1,9},{8,40},{9,17},{16,48},{17,25},{24,56},{25,1},{32,64},... | collective-permute-start | bytes 1376264 | tf_op jit(solution)/shard_map/ppermute | solution.py:26
  94.6 20.0 %collective-permute-start.17 = (bf16[2,64,1792]{2,1,0:T(8,128)(2,1)S(1)}, bf16[2,64,1792]{2,1,0:T(8,128)(2,1)S(1)}, u32[]{:S(2)}, u32[]{:S(2)}) collective-permute-start(bf16[2,64,1792]{2,1,0:T(8,128)(2,1)S(1)} %get-tuple-element.92), channel_id=1, source_target_pairs={{0,64},{1,17},{8,72},{9,25},{16,80},{17,1},{24,88},{25,9},{32,96},... | collective-permute-start | bytes 1376264 | tf_op jit(solution)/shard_map/ppermute | solution.py:26
  97.3 17.3 %collective-permute-start.19 = (bf16[2,64,1792]{2,1,0:T(8,128)(2,1)S(1)}, bf16[2,64,1792]{2,1,0:T(8,128)(2,1)S(1)}, u32[]{:S(2)}, u32[]{:S(2)}) collective-permute-start(bf16[2,64,1792]{2,1,0:T(8,128)(2,1)S(1)} %get-tuple-element.93), channel_id=1, source_target_pairs={{0,96},{1,25},{8,104},{9,1},{16,112},{17,9},{24,120},{25,17},{32,0... | collective-permute-start | bytes 1376264 | tf_op jit(solution)/shard_map/ppermute | solution.py:26
  115.2 26.2 %collective-permute-start.23 = (bf16[2,512,1792]{2,1,0:T(8,128)(2,1)S(1)}, bf16[2,512,1792]{2,1,0:T(8,128)(2,1)S(1)}, u32[]{:S(2)}, u32[]{:S(2)}) collective-permute-start(bf16[2,512,1792]{2,1,0:T(8,128)(2,1)S(1)} %pad_maximum_fusion), channel_id=1, source_target_pairs={{0,1},{1,0},{2,3},{3,2},{4,5},{5,4},{6,7},{7,6},{8,9},{9,8},{10,11... | collective-permute-start | bytes 11010056 | tf_op jit(solution)/shard_map/ppermute | solution.py:34
  115.3 26.2 %collective-permute-start.24 = (bf16[4,256,1792]{2,1,0:T(8,128)(2,1)S(1)}, bf16[4,256,1792]{2,1,0:T(8,128)(2,1)S(1)}, u32[]{:S(2)}, u32[]{:S(2)}) collective-permute-start(bf16[4,256,1792]{2,1,0:T(8,128)(2,1)S(1)} %pad_maximum_fusion.1), channel_id=1, source_target_pairs={{0,1},{1,0},{2,3},{3,2},{4,5},{5,4},{6,7},{7,6},{8,9},{9,8},{10,11... | collective-permute-start | bytes 11010056 | tf_op jit(solution)/shard_map/ppermute | solution.py:34
  116.2 14.2 %collective-permute-start.21 = (bf16[2,2,64,1792]{3,2,1,0:T(8,128)(2,1)S(1)}, bf16[2,2,64,1792]{3,2,1,0:T(8,128)(2,1)S(1)}, u32[]{:S(2)}, u32[]{:S(2)}) collective-permute-start(bf16[2,2,64,1792]{3,2,1,0:T(8,128)(2,1)S(1)} %pad_maximum_fusion.5), channel_id=1, source_target_pairs={{0,64},{1,17},{8,72},{9,25},{16,80},{17,1},{24,88},{25,9},{32,96},... | collective-permute-start | bytes 2752520 | tf_op jit(solution)/shard_map/ppermute | solution.py:26
  118.0 22.7 %collective-permute-start.20 = (bf16[2,2,64,1792]{3,2,1,0:T(8,128)(2,1)S(1)}, bf16[2,2,64,1792]{3,2,1,0:T(8,128)(2,1)S(1)}, u32[]{:S(2)}, u32[]{:S(2)}) collective-permute-start(bf16[2,2,64,1792]{3,2,1,0:T(8,128)(2,1)S(1)} %pad_maximum_fusion.5), channel_id=1, source_target_pairs={{0,96},{1,25},{8,104},{9,1},{16,112},{17,9},{24,120},{25,17},{32,0... | collective-permute-start | bytes 2752520 | tf_op jit(solution)/shard_map/ppermute | solution.py:26
  119.4 21.4 %collective-permute-start.22 = (bf16[2,2,64,1792]{3,2,1,0:T(8,128)(2,1)S(1)}, bf16[2,2,64,1792]{3,2,1,0:T(8,128)(2,1)S(1)}, u32[]{:S(2)}, u32[]{:S(2)}) collective-permute-start(bf16[2,2,64,1792]{3,2,1,0:T(8,128)(2,1)S(1)} %pad_maximum_fusion.5), channel_id=1, source_target_pairs={{0,32},{1,9},{8,40},{9,17},{16,48},{17,25},{24,56},{25,1},{32,64},... | collective-permute-start | bytes 2752520 | tf_op jit(solution)/shard_map/ppermute | solution.py:26
  141.5 23.6 %collective-permute-start.27 = (bf16[2,256,1792]{2,1,0:T(8,128)(2,1)S(1)}, bf16[2,256,1792]{2,1,0:T(8,128)(2,1)S(1)}, u32[]{:S(2)}, u32[]{:S(2)}) collective-permute-start(bf16[2,256,1792]{2,1,0:T(8,128)(2,1)S(1)} %bitcast.165), channel_id=1, source_target_pairs={{0,8},{1,33},{8,16},{9,41},{16,24},{17,49},{24,0},{25,57},{32,40},... | collective-permute-start | bytes 5505032 | tf_op jit(solution)/shard_map/ppermute | solution.py:26
  141.6 25.1 %collective-permute-start.25 = (bf16[2,256,1792]{2,1,0:T(8,128)(2,1)S(1)}, bf16[2,256,1792]{2,1,0:T(8,128)(2,1)S(1)}, u32[]{:S(2)}, u32[]{:S(2)}) collective-permute-start(bf16[2,256,1792]{2,1,0:T(8,128)(2,1)S(1)} %bitcast.161), channel_id=1, source_target_pairs={{0,24},{1,97},{8,0},{9,105},{16,8},{17,113},{24,16},{25,121},{32,5... | collective-permute-start | bytes 5505032 | tf_op jit(solution)/shard_map/ppermute | solution.py:26
  160.6 24.2 %collective-permute-start.34 = (bf16[2,256,1792]{2,1,0:T(8,128)(2,1)S(1)}, bf16[2,256,1792]{2,1,0:T(8,128)(2,1)S(1)}, u32[]{:S(2)}, u32[]{:S(2)}) collective-permute-start(bf16[2,256,1792]{2,1,0:T(8,128)(2,1)S(1)} %bitcast.162), channel_id=1, source_target_pairs={{0,8},{1,33},{8,16},{9,41},{16,24},{17,49},{24,0},{25,57},{32,40},... | collective-permute-start | bytes 5505032 | tf_op jit(solution)/shard_map/ppermute | solution.py:26
  160.6 25.5 %collective-permute-start.33 = (bf16[2,256,1792]{2,1,0:T(8,128)(2,1)S(1)}, bf16[2,256,1792]{2,1,0:T(8,128)(2,1)S(1)}, u32[]{:S(2)}, u32[]{:S(2)}) collective-permute-start(bf16[2,256,1792]{2,1,0:T(8,128)(2,1)S(1)} %bitcast.166), channel_id=1, source_target_pairs={{0,24},{1,97},{8,0},{9,105},{16,8},{17,113},{24,16},{25,121},{32,5... | collective-permute-start | bytes 5505032 | tf_op jit(solution)/shard_map/ppermute | solution.py:26
  163.3 38.7 %collective-permute-start.35 = (bf16[2,256,1792]{2,1,0:T(8,128)(2,1)S(1)}, bf16[2,256,1792]{2,1,0:T(8,128)(2,1)S(1)}, u32[]{:S(2)}, u32[]{:S(2)}) collective-permute-start(bf16[2,256,1792]{2,1,0:T(8,128)(2,1)S(1)} %bitcast.167), channel_id=1, source_target_pairs={{0,1},{1,0},{2,3},{3,2},{4,5},{5,4},{6,7},{7,6},{8,9},{9,8},{10,11... | collective-permute-start | bytes 5505032 | tf_op jit(solution)/shard_map/ppermute | solution.py:34
  165.1 36.9 %collective-permute-start.36 = (bf16[2,256,1792]{2,1,0:T(8,128)(2,1)S(1)}, bf16[2,256,1792]{2,1,0:T(8,128)(2,1)S(1)}, u32[]{:S(2)}, u32[]{:S(2)}) collective-permute-start(bf16[2,256,1792]{2,1,0:T(8,128)(2,1)S(1)} %collective-permute-done.27.refs_5_), channel_id=1, source_target_pairs={{0,1},{1,0},{2,3},{3,2},{4,5},{5,4},{6,7},{7,6},{8,9},{9,8},{10,11... | collective-permute-start | bytes 5505032 | tf_op jit(solution)/shard_map/ppermute | solution.py:34
  166.7 37.8 %collective-permute-start.28 = (bf16[2,256,1792]{2,1,0:T(8,128)(2,1)S(1)}, bf16[2,256,1792]{2,1,0:T(8,128)(2,1)S(1)}, u32[]{:S(2)}, u32[]{:S(2)}) collective-permute-start(bf16[2,256,1792]{2,1,0:T(8,128)(2,1)S(1)} %collective-permute-done.27.refs_5_), channel_id=1, source_target_pairs={{0,8},{1,33},{8,16},{9,41},{16,24},{17,49},{24,0},{25,57},{32,40},... | collective-permute-start | bytes 5505032 | tf_op jit(solution)/shard_map/ppermute | solution.py:26
  184.8 23.2 %collective-permute-start.26 = (bf16[2,256,1792]{2,1,0:T(8,128)(2,1)S(1)}, bf16[2,256,1792]{2,1,0:T(8,128)(2,1)S(1)}, u32[]{:S(2)}, u32[]{:S(2)}) collective-permute-start(bf16[2,256,1792]{2,1,0:T(8,128)(2,1)S(1)} %collective-permute-done.25.refs_2_.refs_1_), channel_id=1, source_target_pairs={{0,24},{1,97},{8,0},{9,105},{16,8},{17,113},{24,16},{25,121},{32,5... | collective-permute-start | bytes 5505032 | tf_op jit(solution)/shard_map/ppermute | solution.py:26
  186.2 29.2 %collective-permute-start.37 = (bf16[2,256,1792]{2,1,0:T(8,128)(2,1)S(1)}, bf16[2,256,1792]{2,1,0:T(8,128)(2,1)S(1)}, u32[]{:S(2)}, u32[]{:S(2)}) collective-permute-start(bf16[2,256,1792]{2,1,0:T(8,128)(2,1)S(1)} %collective-permute-done.33.refs_3_), channel_id=1, source_target_pairs={{0,1},{1,0},{2,3},{3,2},{4,5},{5,4},{6,7},{7,6},{8,9},{9,8},{10,11... | collective-permute-start | bytes 5505032 | tf_op jit(solution)/shard_map/ppermute | solution.py:34
  210.6 15.6 %collective-permute-start.39 = (bf16[2,2,64,512]{3,2,1,0:T(8,128)(2,1)S(1)}, bf16[2,2,64,512]{3,2,1,0:T(8,128)(2,1)S(1)}, u32[]{:S(2)}, u32[]{:S(2)}) collective-permute-start(bf16[2,2,64,512]{3,2,1,0:T(8,128)(2,1)S(1)} %get-tuple-element.78), channel_id=1, source_target_pairs={{0,4},{2,6},{4,0},{6,2},{1,5},{3,7},{5,1},{7,3},{8,12},{10,14},{12... | collective-permute-start | bytes 786440 | tf_op jit(solution)/shard_map/ppermute | solution.py:30
  (33 other events, 253.2 us)

commit v5 on v4

--- a/solution.py
+++ b/solution.py
@@ -92,7 +92,7 @@
     _, _, rows, model = tokens.shape
     parts = [part for group in groups for part in group]
     width = parts[0][1].shape[0]
-    tile = width // 2
+    tile = 256
     operands, in_specs = [], []
     for k, weight, extras in parts:
         operands += [tokens, weight] + [stack for stack, _ in extras]
@@ -115,7 +115,7 @@
 
     return pl.pallas_call(
         kernel,
-        grid=(2,),
+        grid=(width // tile,),
         in_specs=in_specs,
         out_specs=[pl.BlockSpec((len(group), rows, tile), lambda j: (0, 0, j)) for group in groups],
         out_shape=[jax.ShapeDtypeStruct((len(group), rows, width), BF16) for group in groups],

time: 231 us -> 234 us (1.013)
  Pallas kernels: 46.3 us -> 50 us
    pallas_call x4, Pallas kernels: 7.14 us -> 10.8 us  [down_products(): pl.pallas_call(kernel, grid=(width // tile,), in_specs=in_specs, out_spec...]
  transfers between devices with their start and end apart: 43 -> 43, of which waited for: 21 -> 20; matrix products, arithmetic and copies ran while one was open for 5% -> 5% of each run, Pallas kernels for 19% -> 20%
where the time goes in v5:
time: 234 us; the launch traced here: 233 us
  waiting for transfers between devices  105 us (45%)
  starting transfers between devices  60.6 us (26%)
  Pallas kernels  50 us (21%)
  other arithmetic  8.67 us (4%)
  local copies, waits for them, and re-layouts  7.68 us (3%)
    ppermute x23, waiting for transfers between devices, mix(): return lax.ppermute(value, ('x', 'y', 'c'), pairs)  90.8 us
    ppermute x23, starting transfers between devices, mix(): return lax.ppermute(value, ('x', 'y', 'c'), pairs)  28.5 us
    pallas_call x2, Pallas kernels, weight_grads(): pl.pallas_call(kernel, grid=(width // tile,), in_specs=[pl.BlockSpec(left...  20.3 us
    ppermute x11, starting transfers between devices, swap(): return lax.ppermute(value, 'c', [(0, 1), (1, 0)])  17.8 us
    pallas_call x3, Pallas kernels, input_products(): pl.pallas_call(kernel, grid=(steps,), in_specs=([pl.BlockSpec(memory_spac...  16.9 us
    ppermute x9, starting transfers between devices, along_z(): lax.ppermute(value, 'z', [(z, (z + step) % RING) for z in range(RING)])  14.3 us
    ppermute x9, waiting for transfers between devices, along_z(): lax.ppermute(value, 'z', [(z, (z + step) % RING) for z in range(RING)])  10.8 us
    pallas_call x4, Pallas kernels, down_products(): pl.pallas_call(kernel, grid=(width // tile,), in_specs=in_specs, out_spec...  10.8 us
  transfers between devices with their start and end apart: 43, of which 20 were waited for; matrix products, arithmetic and copies ran while one was open for 5% of the time, Pallas kernels for 20%

profile of v5, /device:TPU:1, one launch (start us, length us, event | category | flops | bytes accessed | tf_op | source)
XLA Modules:
  0.0 233.1 jit_solution(5280820026026615418)
XLA Ops:
  11.9 2.8 %collective-permute-done.7 = bf16[2,1,64,1792]{3,2,1,0:T(8,128)(2,1)S(1)} collective-permute-done((bf16[2,1,64,1792]{3,2,1,0:T(8,128)(2,1)S(1)}, bf16[2,1,64,1792]{3,2,1,0:T(8,128)(2,1)S(1)}, u32[]{:S(2)}, u32[]{:S(2)}) %collective-permute-start.7) | collective-permute-done | bytes 458784 | tf_op jit(solution)/shard_map/ppermute | solution.py:26
  14.7 6.1 %collective-permute-done.6 = bf16[2,1,64,1792]{3,2,1,0:T(8,128)(2,1)S(1)} collective-permute-done((bf16[2,1,64,1792]{3,2,1,0:T(8,128)(2,1)S(1)}, bf16[2,1,64,1792]{3,2,1,0:T(8,128)(2,1)S(1)}, u32[]{:S(2)}, u32[]{:S(2)}) %collective-permute-start.6) | collective-permute-done | bytes 458784 | tf_op jit(solution)/shard_map/ppermute | solution.py:26
  28.1 3.3 %collective-permute-start.2 = (bf16[256,512]{1,0:T(8,128)(2,1)S(1)}, bf16[256,512]{1,0:T(8,128)(2,1)S(1)}, u32[]{:S(2)}, u32[]{:S(2)}) collective-permute-start(bf16[256,512]{1,0:T(8,128)(2,1)S(1)} %copy-done.9), channel_id=1, source_target_pairs={{0,4},{2,6},{4,0},{6,2},{1,5},{3,7},{5,1},{7,3},{8,12},{10,14},{12... | collective-permute-start | bytes 786440 | tf_op jit(solution)/shard_map/ppermute | solution.py:30
  32.1 3.3 %collective-permute-done.3 = bf16[256,512]{1,0:T(8,128)(2,1)S(1)} collective-permute-done((bf16[256,512]{1,0:T(8,128)(2,1)S(1)}, bf16[256,512]{1,0:T(8,128)(2,1)S(1)}, u32[]{:S(2)}, u32[]{:S(2)}) %collective-permute-start.3) | collective-permute-done | bytes 262176 | tf_op jit(solution)/shard_map/ppermute | solution.py:30
  35.4 6.4 %collective-permute-done.2 = bf16[256,512]{1,0:T(8,128)(2,1)S(1)} collective-permute-done((bf16[256,512]{1,0:T(8,128)(2,1)S(1)}, bf16[256,512]{1,0:T(8,128)(2,1)S(1)}, u32[]{:S(2)}, u32[]{:S(2)}) %collective-permute-start.2) | collective-permute-done | bytes 262176 | tf_op jit(solution)/shard_map/ppermute | solution.py:30
  54.6 2.7 %collective-permute-start.12 = (bf16[2,256,1792]{2,1,0:T(8,128)(2,1)S(1)}, bf16[2,256,1792]{2,1,0:T(8,128)(2,1)S(1)}, u32[]{:S(2)}, u32[]{:S(2)}) collective-permute-start(bf16[2,256,1792]{2,1,0:T(8,128)(2,1)S(1)} %down_products.5), channel_id=1, source_target_pairs={{0,24},{1,97},{8,0},{9,105},{16,8},{17,113},{24,16},{25,121},{32,5... | collective-permute-start | bytes 5505032 | tf_op jit(solution)/shard_map/ppermute | solution.py:26
  57.3 20.9 %collective-permute-done.11.refs_2_.refs_6_ = bf16[2,256,1792]{2,1,0:T(8,128)(2,1)S(1)} collective-permute-done((bf16[2,256,1792]{2,1,0:T(8,128)(2,1)S(1)}, bf16[2,256,1792]{2,1,0:T(8,128)(2,1)S(1)}, u32[]{:S(2)}, u32[]{:S(2)}) %collective-permute-start.11) | collective-permute-done | bytes 1835040 | tf_op jit(solution)/shard_map/ppermute | solution.py:26
  78.2 2.8 %down_products.6 = (bf16[1,256,1792]{2,1,0:T(8,128)(2,1)S(1)}, bf16[1,256,1792]{2,1,0:T(8,128)(2,1)S(1)}) custom-call(bf16[2,4,256,512]{3,2,1,0:T(8,128)(2,1)S(1)} %bitcast.154, bf16[1792,512]{1,0:T(8,128)(2,1)S(1)} %copy-done, bf16[2,256,1792]{2,1,0:T(8,128)(2,1)S(1)} %collective-permute-done.11.refs_2_.refs_6_, bf16[2,4,256,512]{3,2,1,0:T(8,128)(2,1)S(1)} %bitcast.155, ...), custom_call_target="tpu_custom_call" | custom-call | flops 1 | bytes 1 | tf_op jit(solution)/shard_map/down_products/pallas_call | solution.py:116
  81.1 2.7 %collective-permute-start.14 = (bf16[1,256,1792]{2,1,0:T(8,128)(2,1)S(1)}, bf16[1,256,1792]{2,1,0:T(8,128)(2,1)S(1)}, u32[]{:S(2)}, u32[]{:S(2)}) collective-permute-start(bf16[1,256,1792]{2,1,0:T(8,128)(2,1)S(1)} %get-tuple-element.50), channel_id=1, source_target_pairs={{0,24},{1,97},{8,0},{9,105},{16,8},{17,113},{24,16},{25,121},{32,5... | collective-permute-start | bytes 2752520 | tf_op jit(solution)/shard_map/ppermute | solution.py:26
  89.3 5.4 %collective-permute-done.13.refs_2_ = bf16[1,256,1792]{2,1,0:T(8,128)(2,1)S(1)} collective-permute-done((bf16[1,256,1792]{2,1,0:T(8,128)(2,1)S(1)}, bf16[1,256,1792]{2,1,0:T(8,128)(2,1)S(1)}, u32[]{:S(2)}, u32[]{:S(2)}) %collective-permute-start.13) | collective-permute-done | bytes 917536 | tf_op jit(solution)/shard_map/ppermute | solution.py:26
  94.8 3.0 %down_products.7 = bf16[2,256,1792]{2,1,0:T(8,128)(2,1)S(1)} custom-call(bf16[2,4,256,512]{3,2,1,0:T(8,128)(2,1)S(1)} %bitcast.156, bf16[1792,512]{1,0:T(8,128)(2,1)S(1)} %copy-done, bf16[1,256,1792]{2,1,0:T(8,128)(2,1)S(1)} %collective-permute-done.13.refs_2_, bf16[2,256,1792]{2,1,0:T(8,128)(2,1)S(1)} %collective-permute-done.12.refs_5_.refs_3_, ...), custom_call_target="tpu_custom_call" | custom-call | flops 1 | bytes 1 | tf_op jit(solution)/shard_map/down_products/pallas_call | solution.py:116
  98.2 2.7 %collective-permute-start.17 = (bf16[2,64,1792]{2,1,0:T(8,128)(2,1)S(1)}, bf16[2,64,1792]{2,1,0:T(8,128)(2,1)S(1)}, u32[]{:S(2)}, u32[]{:S(2)}) collective-permute-start(bf16[2,64,1792]{2,1,0:T(8,128)(2,1)S(1)} %get-tuple-element.92), channel_id=1, source_target_pairs={{0,64},{1,17},{8,72},{9,25},{16,80},{17,1},{24,88},{25,9},{32,96},... | collective-permute-start | bytes 1376264 | tf_op jit(solution)/shard_map/ppermute | solution.py:26
  105.2 6.1 %collective-permute-done.18 = bf16[2,64,1792]{2,1,0:T(8,128)(2,1)S(1)} collective-permute-done((bf16[2,64,1792]{2,1,0:T(8,128)(2,1)S(1)}, bf16[2,64,1792]{2,1,0:T(8,128)(2,1)S(1)}, u32[]{:S(2)}, u32[]{:S(2)}) %collective-permute-start.18) | collective-permute-done | bytes 458784 | tf_op jit(solution)/shard_map/ppermute | solution.py:26
  111.2 6.1 %collective-permute-done.17 = bf16[2,64,1792]{2,1,0:T(8,128)(2,1)S(1)} collective-permute-done((bf16[2,64,1792]{2,1,0:T(8,128)(2,1)S(1)}, bf16[2,64,1792]{2,1,0:T(8,128)(2,1)S(1)}, u32[]{:S(2)}, u32[]{:S(2)}) %collective-permute-start.17) | collective-permute-done | bytes 458784 | tf_op jit(solution)/shard_map/ppermute | solution.py:26
  122.2 10.8 %collective-permute-done.21 = bf16[2,2,64,1792]{3,2,1,0:T(8,128)(2,1)S(1)} collective-permute-done((bf16[2,2,64,1792]{3,2,1,0:T(8,128)(2,1)S(1)}, bf16[2,2,64,1792]{3,2,1,0:T(8,128)(2,1)S(1)}, u32[]{:S(2)}, u32[]{:S(2)}) %collective-permute-start.21) | collective-permute-done | bytes 917536 | tf_op jit(solution)/shard_map/ppermute | solution.py:26
  133.1 9.6 %collective-permute-done.20 = bf16[2,2,64,1792]{3,2,1,0:T(8,128)(2,1)S(1)} collective-permute-done((bf16[2,2,64,1792]{3,2,1,0:T(8,128)(2,1)S(1)}, bf16[2,2,64,1792]{3,2,1,0:T(8,128)(2,1)S(1)}, u32[]{:S(2)}, u32[]{:S(2)}) %collective-permute-start.20) | collective-permute-done | bytes 917536 | tf_op jit(solution)/shard_map/ppermute | solution.py:26
  143.6 2.7 %collective-permute-start.25 = (bf16[2,256,1792]{2,1,0:T(8,128)(2,1)S(1)}, bf16[2,256,1792]{2,1,0:T(8,128)(2,1)S(1)}, u32[]{:S(2)}, u32[]{:S(2)}) collective-permute-start(bf16[2,256,1792]{2,1,0:T(8,128)(2,1)S(1)} %bitcast.161), channel_id=1, source_target_pairs={{0,24},{1,97},{8,0},{9,105},{16,8},{17,113},{24,16},{25,121},{32,5... | collective-permute-start | bytes 5505032 | tf_op jit(solution)/shard_map/ppermute | solution.py:26
  150.3 9.4 %weight_grads.2 = f32[1792,512]{1,0:T(8,128)} custom-call(bf16[2,4,256,512]{3,2,1,0:T(8,128)(2,1)S(1)} %bitcast.158, bf16[2,256,1792]{2,1,0:T(8,128)(2,1)} %pad_maximum_fusion.2.refs_0_, bf16[2,256,1792]{2,1,0:T(8,128)(2,1)} %collective-permute-done.9.refs_1_, bf16[1,256,1792]{2,1,0:T(8,128)(2,1)S(1)} %bitcast.173, ...), custom_call_target="tpu_custom_call" | custom-call | flops 1 | bytes 1 | tf_op jit(solution)/shard_map/weight_grads/pallas_call | solution.py:197
  162.7 2.7 %collective-permute-start.33 = (bf16[2,256,1792]{2,1,0:T(8,128)(2,1)S(1)}, bf16[2,256,1792]{2,1,0:T(8,128)(2,1)S(1)}, u32[]{:S(2)}, u32[]{:S(2)}) collective-permute-start(bf16[2,256,1792]{2,1,0:T(8,128)(2,1)S(1)} %bitcast.166), channel_id=1, source_target_pairs={{0,24},{1,97},{8,0},{9,105},{16,8},{17,113},{24,16},{25,121},{32,5... | collective-permute-start | bytes 5505032 | tf_op jit(solution)/shard_map/ppermute | solution.py:26
  169.2 17.7 %collective-permute-done.34.refs_4_.refs_3_ = bf16[2,256,1792]{2,1,0:T(8,128)(2,1)S(1)} collective-permute-done((bf16[2,256,1792]{2,1,0:T(8,128)(2,1)S(1)}, bf16[2,256,1792]{2,1,0:T(8,128)(2,1)S(1)}, u32[]{:S(2)}, u32[]{:S(2)}) %collective-permute-start.34) | collective-permute-done | bytes 1835040 | tf_op jit(solution)/shard_map/ppermute | solution.py:26
  188.2 3.3 %collective-permute-start.37 = (bf16[2,256,1792]{2,1,0:T(8,128)(2,1)S(1)}, bf16[2,256,1792]{2,1,0:T(8,128)(2,1)S(1)}, u32[]{:S(2)}, u32[]{:S(2)}) collective-permute-start(bf16[2,256,1792]{2,1,0:T(8,128)(2,1)S(1)} %collective-permute-done.33.refs_3_), channel_id=1, source_target_pairs={{0,1},{1,0},{2,3},{3,2},{4,5},{5,4},{6,7},{7,6},{8,9},{9,8},{10,11... | collective-permute-start | bytes 5505032 | tf_op jit(solution)/shard_map/ppermute | solution.py:34
  191.5 12.2 %input_products.3 = (bf16[256,512]{1,0:T(8,128)(2,1)S(1)}, bf16[256,512]{1,0:T(8,128)(2,1)S(1)}, bf16[256,512]{1,0:T(8,128)(2,1)S(1)}) custom-call(bf16[2,256,1792]{2,1,0:T(8,128)(2,1)S(1)} %bitcast.163, bf16[2,256,1792]{2,1,0:T(8,128)(2,1)S(1)} %bitcast.168, bf16[2,256,1792]{2,1,0:T(8,128)(2,1)S(1)} %collective-permute-done.25.refs_2_.refs_1_, ...), custom_call_target="tpu_custom_call" | custom-call | flops 1 | bytes 1 | tf_op jit(solution)/shard_map/input_products/pallas_call | solution.py:282
  203.8 2.7 %collective-permute-done.28.refs_0_ = bf16[2,256,1792]{2,1,0:T(8,128)(2,1)S(1)} collective-permute-done((bf16[2,256,1792]{2,1,0:T(8,128)(2,1)S(1)}, bf16[2,256,1792]{2,1,0:T(8,128)(2,1)S(1)}, u32[]{:S(2)}, u32[]{:S(2)}) %collective-permute-start.28) | collective-permute-done | bytes 1835040 | tf_op jit(solution)/shard_map/ppermute | solution.py:26
  217.8 10.9 %weight_grads.3 = (f32[512,1792]{1,0:T(8,128)}, f32[512,1792]{1,0:T(8,128)}) custom-call(bf16[512,2048]{1,0:T(8,128)(2,1)S(1)} %travel_order.3.left_ref, bf16[2,256,1792]{2,1,0:T(8,128)(2,1)S(1)} %bitcast.164, bf16[2,256,1792]{2,1,0:T(8,128)(2,1)S(1)} %collective-permute-done.25.refs_2_.refs_1_, ...), custom_call_target="tpu_custom_call" | custom-call | flops 1 | bytes 1 | tf_op jit(solution)/shard_map/weight_grads/pallas_call | solution.py:197
  (134 shorter events, 75.9 us)
Async XLA Ops:
  23.8 30.8 %collective-permute-start.10 = (bf16[2,256,1792]{2,1,0:T(8,128)(2,1)}, bf16[2,256,1792]{2,1,0:T(8,128)(2,1)}, u32[]{:S(2)}, u32[]{:S(2)}) collective-permute-start(bf16[2,256,1792]{2,1,0:T(8,128)(2,1)} %pad_maximum_fusion.2.refs_0_), channel_id=1, source_target_pairs={{0,8},{1,33},{8,16},{9,41},{16,24},{17,49},{24,0},{25,57},{32,40},... | collective-permute-start | bytes 5505032 | tf_op jit(solution)/shard_map/ppermute | solution.py:26
  24.7 29.9 %collective-permute-start.9 = (bf16[2,256,1792]{2,1,0:T(8,128)(2,1)}, bf16[2,256,1792]{2,1,0:T(8,128)(2,1)}, u32[]{:S(2)}, u32[]{:S(2)}) collective-permute-start(bf16[2,256,1792]{2,1,0:T(8,128)(2,1)} %pad_maximum_fusion.2.refs_0_), channel_id=1, source_target_pairs={{0,24},{1,97},{8,0},{9,105},{16,8},{17,113},{24,16},{25,121},{32,5... | collective-permute-start | bytes 5505032 | tf_op jit(solution)/shard_map/ppermute | solution.py:26
  54.6 23.6 %collective-permute-start.11 = (bf16[2,256,1792]{2,1,0:T(8,128)(2,1)S(1)}, bf16[2,256,1792]{2,1,0:T(8,128)(2,1)S(1)}, u32[]{:S(2)}, u32[]{:S(2)}) collective-permute-start(bf16[2,256,1792]{2,1,0:T(8,128)(2,1)S(1)} %down_products.4), channel_id=1, source_target_pairs={{0,8},{1,33},{8,16},{9,41},{16,24},{17,49},{24,0},{25,57},{32,40},... | collective-permute-start | bytes 5505032 | tf_op jit(solution)/shard_map/ppermute | solution.py:26
  54.6 23.6 %collective-permute-start.12 = (bf16[2,256,1792]{2,1,0:T(8,128)(2,1)S(1)}, bf16[2,256,1792]{2,1,0:T(8,128)(2,1)S(1)}, u32[]{:S(2)}, u32[]{:S(2)}) collective-permute-start(bf16[2,256,1792]{2,1,0:T(8,128)(2,1)S(1)} %down_products.5), channel_id=1, source_target_pairs={{0,24},{1,97},{8,0},{9,105},{16,8},{17,113},{24,16},{25,121},{32,5... | collective-permute-start | bytes 5505032 | tf_op jit(solution)/shard_map/ppermute | solution.py:26
  81.0 13.8 %collective-permute-start.13 = (bf16[1,256,1792]{2,1,0:T(8,128)(2,1)S(1)}, bf16[1,256,1792]{2,1,0:T(8,128)(2,1)S(1)}, u32[]{:S(2)}, u32[]{:S(2)}) collective-permute-start(bf16[1,256,1792]{2,1,0:T(8,128)(2,1)S(1)} %get-tuple-element.49), channel_id=1, source_target_pairs={{0,8},{1,33},{8,16},{9,41},{16,24},{17,49},{24,0},{25,57},{32,40},... | collective-permute-start | bytes 2752520 | tf_op jit(solution)/shard_map/ppermute | solution.py:26
  86.6 18.1 %collective-permute-start.15 = (bf16[256,1792]{1,0:T(8,128)(2,1)S(1)}, bf16[256,1792]{1,0:T(8,128)(2,1)S(1)}, u32[]{:S(2)}, u32[]{:S(2)}) collective-permute-start(bf16[256,1792]{1,0:T(8,128)(2,1)S(1)} %get-tuple-element.51), channel_id=1, source_target_pairs={{0,8},{1,33},{8,16},{9,41},{16,24},{17,49},{24,0},{25,57},{32,40},... | collective-permute-start | bytes 2752520 | tf_op jit(solution)/shard_map/ppermute | solution.py:26
  86.7 18.0 %collective-permute-start.16 = (bf16[256,1792]{1,0:T(8,128)(2,1)S(1)}, bf16[256,1792]{1,0:T(8,128)(2,1)S(1)}, u32[]{:S(2)}, u32[]{:S(2)}) collective-permute-start(bf16[256,1792]{1,0:T(8,128)(2,1)S(1)} %get-tuple-element.52), channel_id=1, source_target_pairs={{0,24},{1,97},{8,0},{9,105},{16,8},{17,113},{24,16},{25,121},{32,5... | collective-permute-start | bytes 2752520 | tf_op jit(solution)/shard_map/ppermute | solution.py:26
  98.2 19.1 %collective-permute-start.17 = (bf16[2,64,1792]{2,1,0:T(8,128)(2,1)S(1)}, bf16[2,64,1792]{2,1,0:T(8,128)(2,1)S(1)}, u32[]{:S(2)}, u32[]{:S(2)}) collective-permute-start(bf16[2,64,1792]{2,1,0:T(8,128)(2,1)S(1)} %get-tuple-element.92), channel_id=1, source_target_pairs={{0,64},{1,17},{8,72},{9,25},{16,80},{17,1},{24,88},{25,9},{32,96},... | collective-permute-start | bytes 1376264 | tf_op jit(solution)/shard_map/ppermute | solution.py:26
  100.9 16.4 %collective-permute-start.19 = (bf16[2,64,1792]{2,1,0:T(8,128)(2,1)S(1)}, bf16[2,64,1792]{2,1,0:T(8,128)(2,1)S(1)}, u32[]{:S(2)}, u32[]{:S(2)}) collective-permute-start(bf16[2,64,1792]{2,1,0:T(8,128)(2,1)S(1)} %get-tuple-element.93), channel_id=1, source_target_pairs={{0,96},{1,25},{8,104},{9,1},{16,112},{17,9},{24,120},{25,17},{32,0... | collective-permute-start | bytes 1376264 | tf_op jit(solution)/shard_map/ppermute | solution.py:26
  117.9 25.6 %collective-permute-start.23 = (bf16[2,512,1792]{2,1,0:T(8,128)(2,1)S(1)}, bf16[2,512,1792]{2,1,0:T(8,128)(2,1)S(1)}, u32[]{:S(2)}, u32[]{:S(2)}) collective-permute-start(bf16[2,512,1792]{2,1,0:T(8,128)(2,1)S(1)} %pad_maximum_fusion), channel_id=1, source_target_pairs={{0,1},{1,0},{2,3},{3,2},{4,5},{5,4},{6,7},{7,6},{8,9},{9,8},{10,11... | collective-permute-start | bytes 11010056 | tf_op jit(solution)/shard_map/ppermute | solution.py:34
  118.0 25.5 %collective-permute-start.24 = (bf16[4,256,1792]{2,1,0:T(8,128)(2,1)S(1)}, bf16[4,256,1792]{2,1,0:T(8,128)(2,1)S(1)}, u32[]{:S(2)}, u32[]{:S(2)}) collective-permute-start(bf16[4,256,1792]{2,1,0:T(8,128)(2,1)S(1)} %pad_maximum_fusion.1), channel_id=1, source_target_pairs={{0,1},{1,0},{2,3},{3,2},{4,5},{5,4},{6,7},{7,6},{8,9},{9,8},{10,11... | collective-permute-start | bytes 11010056 | tf_op jit(solution)/shard_map/ppermute | solution.py:34
  118.9 14.2 %collective-permute-start.21 = (bf16[2,2,64,1792]{3,2,1,0:T(8,128)(2,1)S(1)}, bf16[2,2,64,1792]{3,2,1,0:T(8,128)(2,1)S(1)}, u32[]{:S(2)}, u32[]{:S(2)}) collective-permute-start(bf16[2,2,64,1792]{3,2,1,0:T(8,128)(2,1)S(1)} %pad_maximum_fusion.5), channel_id=1, source_target_pairs={{0,64},{1,17},{8,72},{9,25},{16,80},{17,1},{24,88},{25,9},{32,96},... | collective-permute-start | bytes 2752520 | tf_op jit(solution)/shard_map/ppermute | solution.py:26
  120.7 22.0 %collective-permute-start.20 = (bf16[2,2,64,1792]{3,2,1,0:T(8,128)(2,1)S(1)}, bf16[2,2,64,1792]{3,2,1,0:T(8,128)(2,1)S(1)}, u32[]{:S(2)}, u32[]{:S(2)}) collective-permute-start(bf16[2,2,64,1792]{3,2,1,0:T(8,128)(2,1)S(1)} %pad_maximum_fusion.5), channel_id=1, source_target_pairs={{0,96},{1,25},{8,104},{9,1},{16,112},{17,9},{24,120},{25,17},{32,0... | collective-permute-start | bytes 2752520 | tf_op jit(solution)/shard_map/ppermute | solution.py:26
  121.3 21.5 %collective-permute-start.22 = (bf16[2,2,64,1792]{3,2,1,0:T(8,128)(2,1)S(1)}, bf16[2,2,64,1792]{3,2,1,0:T(8,128)(2,1)S(1)}, u32[]{:S(2)}, u32[]{:S(2)}) collective-permute-start(bf16[2,2,64,1792]{3,2,1,0:T(8,128)(2,1)S(1)} %pad_maximum_fusion.5), channel_id=1, source_target_pairs={{0,32},{1,9},{8,40},{9,17},{16,48},{17,25},{24,56},{25,1},{32,64},... | collective-permute-start | bytes 2752520 | tf_op jit(solution)/shard_map/ppermute | solution.py:26
  143.5 23.6 %collective-permute-start.27 = (bf16[2,256,1792]{2,1,0:T(8,128)(2,1)S(1)}, bf16[2,256,1792]{2,1,0:T(8,128)(2,1)S(1)}, u32[]{:S(2)}, u32[]{:S(2)}) collective-permute-start(bf16[2,256,1792]{2,1,0:T(8,128)(2,1)S(1)} %bitcast.165), channel_id=1, source_target_pairs={{0,8},{1,33},{8,16},{9,41},{16,24},{17,49},{24,0},{25,57},{32,40},... | collective-permute-start | bytes 5505032 | tf_op jit(solution)/shard_map/ppermute | solution.py:26
  143.6 25.6 %collective-permute-start.25 = (bf16[2,256,1792]{2,1,0:T(8,128)(2,1)S(1)}, bf16[2,256,1792]{2,1,0:T(8,128)(2,1)S(1)}, u32[]{:S(2)}, u32[]{:S(2)}) collective-permute-start(bf16[2,256,1792]{2,1,0:T(8,128)(2,1)S(1)} %bitcast.161), channel_id=1, source_target_pairs={{0,24},{1,97},{8,0},{9,105},{16,8},{17,113},{24,16},{25,121},{32,5... | collective-permute-start | bytes 5505032 | tf_op jit(solution)/shard_map/ppermute | solution.py:26
  162.7 24.2 %collective-permute-start.34 = (bf16[2,256,1792]{2,1,0:T(8,128)(2,1)S(1)}, bf16[2,256,1792]{2,1,0:T(8,128)(2,1)S(1)}, u32[]{:S(2)}, u32[]{:S(2)}) collective-permute-start(bf16[2,256,1792]{2,1,0:T(8,128)(2,1)S(1)} %bitcast.162), channel_id=1, source_target_pairs={{0,8},{1,33},{8,16},{9,41},{16,24},{17,49},{24,0},{25,57},{32,40},... | collective-permute-start | bytes 5505032 | tf_op jit(solution)/shard_map/ppermute | solution.py:26
  162.7 25.5 %collective-permute-start.33 = (bf16[2,256,1792]{2,1,0:T(8,128)(2,1)S(1)}, bf16[2,256,1792]{2,1,0:T(8,128)(2,1)S(1)}, u32[]{:S(2)}, u32[]{:S(2)}) collective-permute-start(bf16[2,256,1792]{2,1,0:T(8,128)(2,1)S(1)} %bitcast.166), channel_id=1, source_target_pairs={{0,24},{1,97},{8,0},{9,105},{16,8},{17,113},{24,16},{25,121},{32,5... | collective-permute-start | bytes 5505032 | tf_op jit(solution)/shard_map/ppermute | solution.py:26
  165.4 38.4 %collective-permute-start.35 = (bf16[2,256,1792]{2,1,0:T(8,128)(2,1)S(1)}, bf16[2,256,1792]{2,1,0:T(8,128)(2,1)S(1)}, u32[]{:S(2)}, u32[]{:S(2)}) collective-permute-start(bf16[2,256,1792]{2,1,0:T(8,128)(2,1)S(1)} %bitcast.167), channel_id=1, source_target_pairs={{0,1},{1,0},{2,3},{3,2},{4,5},{5,4},{6,7},{7,6},{8,9},{9,8},{10,11... | collective-permute-start | bytes 5505032 | tf_op jit(solution)/shard_map/ppermute | solution.py:34
  167.2 36.6 %collective-permute-start.36 = (bf16[2,256,1792]{2,1,0:T(8,128)(2,1)S(1)}, bf16[2,256,1792]{2,1,0:T(8,128)(2,1)S(1)}, u32[]{:S(2)}, u32[]{:S(2)}) collective-permute-start(bf16[2,256,1792]{2,1,0:T(8,128)(2,1)S(1)} %collective-permute-done.27.refs_5_), channel_id=1, source_target_pairs={{0,1},{1,0},{2,3},{3,2},{4,5},{5,4},{6,7},{7,6},{8,9},{9,8},{10,11... | collective-permute-start | bytes 5505032 | tf_op jit(solution)/shard_map/ppermute | solution.py:34
  169.2 37.3 %collective-permute-start.28 = (bf16[2,256,1792]{2,1,0:T(8,128)(2,1)S(1)}, bf16[2,256,1792]{2,1,0:T(8,128)(2,1)S(1)}, u32[]{:S(2)}, u32[]{:S(2)}) collective-permute-start(bf16[2,256,1792]{2,1,0:T(8,128)(2,1)S(1)} %collective-permute-done.27.refs_5_), channel_id=1, source_target_pairs={{0,8},{1,33},{8,16},{9,41},{16,24},{17,49},{24,0},{25,57},{32,40},... | collective-permute-start | bytes 5505032 | tf_op jit(solution)/shard_map/ppermute | solution.py:26
  186.9 23.7 %collective-permute-start.26 = (bf16[2,256,1792]{2,1,0:T(8,128)(2,1)S(1)}, bf16[2,256,1792]{2,1,0:T(8,128)(2,1)S(1)}, u32[]{:S(2)}, u32[]{:S(2)}) collective-permute-start(bf16[2,256,1792]{2,1,0:T(8,128)(2,1)S(1)} %collective-permute-done.25.refs_2_.refs_1_), channel_id=1, source_target_pairs={{0,24},{1,97},{8,0},{9,105},{16,8},{17,113},{24,16},{25,121},{32,5... | collective-permute-start | bytes 5505032 | tf_op jit(solution)/shard_map/ppermute | solution.py:26
  188.2 29.6 %collective-permute-start.37 = (bf16[2,256,1792]{2,1,0:T(8,128)(2,1)S(1)}, bf16[2,256,1792]{2,1,0:T(8,128)(2,1)S(1)}, u32[]{:S(2)}, u32[]{:S(2)}) collective-permute-start(bf16[2,256,1792]{2,1,0:T(8,128)(2,1)S(1)} %collective-permute-done.33.refs_3_), channel_id=1, source_target_pairs={{0,1},{1,0},{2,3},{3,2},{4,5},{5,4},{6,7},{7,6},{8,9},{9,8},{10,11... | collective-permute-start | bytes 5505032 | tf_op jit(solution)/shard_map/ppermute | solution.py:34
  213.2 15.6 %collective-permute-start.39 = (bf16[2,2,64,512]{3,2,1,0:T(8,128)(2,1)S(1)}, bf16[2,2,64,512]{3,2,1,0:T(8,128)(2,1)S(1)}, u32[]{:S(2)}, u32[]{:S(2)}) collective-permute-start(bf16[2,2,64,512]{3,2,1,0:T(8,128)(2,1)S(1)} %get-tuple-element.78), channel_id=1, source_target_pairs={{0,4},{2,6},{4,0},{6,2},{1,5},{3,7},{5,1},{7,3},{8,12},{10,14},{12... | collective-permute-start | bytes 786440 | tf_op jit(solution)/shard_map/ppermute | solution.py:30
  (33 other events, 261.5 us)
